TPU v7x, 32 devices: a whole 2x2x4 slice. The times are simulated.
32 devices in a mesh: groups: 2 (over y), expert: 8 (over z, x), dp: 2 (over core).
Axes of the slice: x: 2, y: 2, z: 4, core: 2. Of those that a mesh axis runs over, the one named last changes fastest.
Arguments:
- tokens: bfloat16 [4096, 2048], P(('groups', 'expert', 'dp')), parts along dimension 0, may hold values from -6 to 6
- out_grad: bfloat16 [4096, 2048], P(('groups', 'expert', 'dp')), parts along dimension 0, may hold values from -6 to 6
- choices: int32 [4096, 8], P(('groups', 'expert', 'dp')), parts along dimension 0, may hold values from 0 to 127, as said below
- gates: bfloat16 [4096, 8], P(('groups', 'expert', 'dp')), parts along dimension 0, may hold values from 0.049804688 to 1
- gate_weight: bfloat16 [8, 2048, 192], P('expert'), may hold values from -0.125 to 0.125
- up_weight: bfloat16 [8, 2048, 192], P('expert'), may hold values from -0.125 to 0.125
- down_weight: bfloat16 [8, 192, 2048], P('expert'), may hold values from -0.21875 to 0.21875
Outputs:
- in_grad: bfloat16 [4096, 2048], P(('groups', 'expert', 'dp')), parts along dimension 0
- combine_grad: float32 [4096, 8], P(('groups', 'expert', 'dp')), parts along dimension 0
- gate_weight_grad: bfloat16 [16, 2048, 192], P(('groups', 'expert'), 'dp'), parts along dimension 0
- up_weight_grad: bfloat16 [16, 2048, 192], P(('groups', 'expert'), 'dp'), parts along dimension 0
- down_weight_grad: bfloat16 [16, 192, 2048], P(('groups', 'expert'), None, 'dp'), parts along dimension 0
There are 2 independent parts, one for each index of `groups`. A program takes and returns all parts, laid end to end along the dimension named above; an argument that names none is the same for every part. Nothing has to cross between parts.
Inputs may be any that keep to these rules, and one draw needn't show every extreme that they name: `choices`: each row names 8 different experts. Among the 128 rows of one device every expert is named between 7 and 9 times, and one expert below 2 is named exactly 9 times by the rows of every device.
All inputs are finite; a program needn't handle non-finite values.
Results may differ from a plain program's by a relative error of at most 0.0085.
Values may be sent and summed in bfloat16 or wider, within the bound.
No kernel may reach another device: no remote copies, remote signals or barrier semaphores. Data moves between devices by JAX's collectives and lax.ppermute only.
A program may use at most 128 MiB of HBM per device.

v0:
```python
import jax
import jax.numpy as jnp
from jax import lax
from jax.sharding import PartitionSpec as P

SPLIT = 4
CAP = 9


def from_partner(block, axis, bit):
    count = lax.axis_size(axis)
    route = []
    for low in range(count):
        high = low | 1 << bit
        if high != low and high < count:
            route += [(low, high), (high, low)]
    return lax.ppermute(block, axis, route)


def silu_parts(pre_act):
    sigmoid = 1.0 / (1.0 + jnp.exp(-pre_act))
    return (pre_act * sigmoid, sigmoid * (1.0 + pre_act * (1.0 - sigmoid)))


def split_parts(rows, window, capacity, piece_width):
    members = window * SPLIT
    parted = rows.reshape(window, capacity, SPLIT, piece_width).transpose(0, 2, 1, 3)
    return parted.reshape(members, capacity, piece_width)


def body(tokens, out_grad, choices, gates, gate_weight, up_weight, down_weight):
    members = lax.axis_size("expert")
    position = lax.axis_index("expert")
    tok_rows, features = tokens.shape
    picks_per = choices.shape[1]
    hidden = gate_weight.shape[2]
    window = members // SPLIT
    capacity = CAP
    piece_width = features // SPLIT
    levels = SPLIT.bit_length() - 1
    flat_ids = choices.reshape(-1)
    flat_gates = gates.reshape(-1)
    window_ids = jnp.arange(window, dtype=jnp.int32)
    hit_table = (flat_ids[:, None] == window_ids[None, :]).astype(jnp.int32)
    rank_in = jnp.sum((jnp.cumsum(hit_table, axis=0) - hit_table) * hit_table, axis=1)
    seat_index = jnp.arange(capacity, dtype=jnp.int32)
    matched = (flat_ids[None, None, :] == window_ids[:, None, None]) & (
        rank_in[None, None, :] == seat_index[None, :, None]
    )
    owner_tok = jnp.arange(tok_rows * picks_per, dtype=jnp.int32) // picks_per
    slot_tok = jnp.sum(jnp.where(matched, owner_tok[None, None, :], 0), axis=2)
    slot_live = jnp.any(matched, axis=2)
    slot_gate = jnp.sum(
        jnp.where(matched, flat_gates[None, None, :].astype(jnp.float32), 0.0), axis=2
    ).astype(jnp.bfloat16)
    slot_input = jnp.where(slot_live[:, :, None], tokens[slot_tok], jnp.zeros((), tokens.dtype))
    slot_grad = jnp.where(slot_live[:, :, None], out_grad[slot_tok], jnp.zeros((), out_grad.dtype))
    send_gates = jnp.repeat(slot_gate, SPLIT, axis=0)
    split_input = split_parts(slot_input, window, capacity, piece_width)
    split_grad = split_parts(slot_grad, window, capacity, piece_width)
    arrived_input, arrived_grad, arrived_gates = (
        lax.all_to_all(split_input, "expert", split_axis=0, concat_axis=0, tiled=True),
        lax.all_to_all(split_grad, "expert", split_axis=0, concat_axis=0, tiled=True),
        lax.all_to_all(send_gates, "expert", split_axis=0, concat_axis=0, tiled=True),
    )
    input_rows = arrived_input[None]
    grad_rows = arrived_grad[None]
    for section_bit in range(levels):
        other_input, other_grad = from_partner((input_rows, grad_rows), "expert", section_bit)
        lower_half = position >> section_bit & 1 == 0
        input_rows = jnp.where(
            lower_half,
            jnp.concatenate([input_rows, other_input], axis=0),
            jnp.concatenate([other_input, input_rows], axis=0),
        )
        grad_rows = jnp.where(
            lower_half,
            jnp.concatenate([grad_rows, other_grad], axis=0),
            jnp.concatenate([other_grad, grad_rows], axis=0),
        )
    part_count = input_rows.shape[0]
    part_width = features // part_count
    w_both = jnp.concatenate([gate_weight[0], up_weight[0]], axis=1).reshape(
        part_count, part_width, 2 * hidden
    )
    w_down = down_weight[0].reshape(hidden, part_count, part_width)
    pre_both = jnp.einsum("pncq,pqf->ncf", input_rows, w_both, preferred_element_type=jnp.float32)
    pre_gate = pre_both[:, :, :hidden]
    pre_up = pre_both[:, :, hidden:]
    back_grad = jnp.einsum("pncq,fpq->ncf", grad_rows, w_down, preferred_element_type=jnp.float32)
    silu_val, slope = silu_parts(pre_gate)
    activated = silu_val * pre_up
    combine_part = jnp.sum(back_grad * activated, axis=2).astype(jnp.bfloat16)
    gate_wide = arrived_gates.astype(jnp.float32)[:, :, None]
    gated_back = gate_wide * back_grad
    scaled = (gate_wide * activated).astype(jnp.bfloat16)
    grad_gate_pre = (gated_back * slope * pre_up).astype(jnp.bfloat16)
    grad_up_pre = (gated_back * silu_val).astype(jnp.bfloat16)
    grad_both = jnp.concatenate([grad_gate_pre, grad_up_pre], axis=2)
    partial_value = jnp.einsum(
        "ncf,pqf->pncq", grad_both, w_both, preferred_element_type=jnp.float32
    ).astype(jnp.bfloat16)
    both_sum = jnp.einsum(
        "pncq,ncf->pqf", input_rows, grad_both, preferred_element_type=jnp.float32
    ).reshape(features, 2 * hidden)
    gate_sum = both_sum[:, :hidden]
    up_sum = both_sum[:, hidden:]
    down_sum = jnp.einsum(
        "ncf,pncq->fpq", scaled, grad_rows, preferred_element_type=jnp.float32
    ).reshape(hidden, features)
    full_rows = partial_value.transpose(1, 2, 0, 3).reshape(members, capacity, features)
    back_rows, back_combine = (
        lax.all_to_all(full_rows, "expert", split_axis=0, concat_axis=0, tiled=True),
        lax.all_to_all(combine_part, "expert", split_axis=0, concat_axis=0, tiled=True),
    )
    summed = jnp.sum(
        back_rows.reshape(window, SPLIT, capacity, features).astype(jnp.float32), axis=1
    )
    combine_sum = jnp.sum(back_combine.astype(jnp.float32).reshape(window, SPLIT, capacity), axis=1)
    owners = (
        slot_tok[:, :, None] == jnp.arange(tok_rows, dtype=jnp.int32)[None, None, :]
    ) & slot_live[:, :, None]
    owners = owners.astype(jnp.float32).reshape(window * capacity, tok_rows)
    in_grad = jnp.dot(
        owners.T, summed.reshape(window * capacity, features), precision=lax.Precision.HIGHEST
    )
    matched_wide = matched.astype(jnp.float32).reshape(window * capacity, tok_rows * picks_per)
    combine_grad = jnp.dot(
        combine_sum.reshape(1, window * capacity), matched_wide, precision=lax.Precision.HIGHEST
    )
    combine_grad = combine_grad.reshape(tok_rows, picks_per)
    gate_total, up_total, down_total = (
        lax.psum_scatter(
            gate_sum[None].astype(jnp.bfloat16), "dp", scatter_dimension=1, tiled=True
        ).astype(jnp.float32),
        lax.psum_scatter(
            up_sum[None].astype(jnp.bfloat16), "dp", scatter_dimension=1, tiled=True
        ).astype(jnp.float32),
        lax.psum_scatter(
            down_sum[None].astype(jnp.bfloat16), "dp", scatter_dimension=2, tiled=True
        ).astype(jnp.float32),
    )
    return (
        in_grad.astype(jnp.bfloat16),
        combine_grad,
        gate_total.astype(jnp.bfloat16),
        up_total.astype(jnp.bfloat16),
        down_total.astype(jnp.bfloat16),
    )


def solution(mesh):
    return jax.shard_map(
        body,
        mesh=mesh,
        in_specs=(
            P(("groups", "expert", "dp"), None),
            P(("groups", "expert", "dp"), None),
            P(("groups", "expert", "dp"), None),
            P(("groups", "expert", "dp"), None),
            P("expert", None, None),
            P("expert", None, None),
            P("expert", None, None),
        ),
        out_specs=(
            P(("groups", "expert", "dp"), None),
            P(("groups", "expert", "dp"), None),
            P(("groups", "expert"), "dp", None),
            P(("groups", "expert"), "dp", None),
            P(("groups", "expert"), None, "dp"),
        ),
        check_vma=False,
    )
```

profile of v0, /device:TPU:0, one launch (start us, length us, event | category | flops | bytes accessed | tf_op | source)
XLA Modules:
  0.0 101.4 jit_solution(18027381633413333607)
XLA Ops:
  7.2 0.9 copy.42
  8.3 0.6 reduce-window.6
  8.9 0.2 slice_reduce_fusion
  9.1 0.2 reduce-window.9
  9.4 0.6 broadcast_and_fusion
  10.3 0.6 gather_fusion.1
  10.9 0.6 gather_fusion
  11.8 0.7 reshape.192
  12.5 7.3 %all-to-all-start.2 = ((bf16[8,9,512]{2,1,0:T(8,128)(2,1)}), bf16[8,9,512]{2,1,0:T(8,128)(2,1)S(1)}, u32[]{:S(2)}, u32[]{:S(2)}) async-start(bf16[8,9,512]{2,1,0:T(8,128)(2,1)} %reshape.192), calls=%async_computation.2 | async-start | bytes 262144 | tf_op jit(solution)/shard_map/all_to_all | solution.py:62
  19.8 0.7 reshape.191
  20.5 6.6 %all-to-all-done.2 = bf16[8,9,512]{2,1,0:T(8,128)(2,1)S(1)} async-done(((bf16[8,9,512]{2,1,0:T(8,128)(2,1)}), bf16[8,9,512]{2,1,0:T(8,128)(2,1)S(1)}, u32[]{:S(2)}, u32[]{:S(2)}) %all-to-all-start.2) | async-done | bytes 73760 | tf_op jit(solution)/shard_map/all_to_all | solution.py:62
  27.1 4.0 %all-to-all-start.1 = ((bf16[8,9,512]{2,1,0:T(8,128)(2,1)}), bf16[8,9,512]{2,1,0:T(8,128)(2,1)}, u32[]{:S(2)}, u32[]{:S(2)}) async-start(bf16[8,9,512]{2,1,0:T(8,128)(2,1)} %reshape.191), calls=%async_computation.1 | async-start | bytes 262144 | tf_op jit(solution)/shard_map/all_to_all | solution.py:63
  31.3 1.9 %collective-permute-start.2 = (bf16[1,8,9,512]{3,2,1,0:T(8,128)(2,1)S(1)}, bf16[1,8,9,512]{3,2,1,0:T(8,128)(2,1)}, u32[]{:S(2)}, u32[]{:S(2)}) collective-permute-start(bf16[1,8,9,512]{3,2,1,0:T(8,128)(2,1)S(1)} %bitcast.93), channel_id=1, source_target_pairs={{0,2},{2,0},{4,6},{6,4},{8,10},{10,8},{12,14},{14,12},{1,3},{3,1},... | collective-permute-start | bytes 221192 | tf_op jit(solution)/shard_map/ppermute | solution.py:17
  33.4 0.6 copy.45
  34.0 0.5 copy.48
  34.5 0.5 copy.49
  35.0 3.4 %all-to-all-done.1 = bf16[8,9,512]{2,1,0:T(8,128)(2,1)} async-done(((bf16[8,9,512]{2,1,0:T(8,128)(2,1)}), bf16[8,9,512]{2,1,0:T(8,128)(2,1)}, u32[]{:S(2)}, u32[]{:S(2)}) %all-to-all-start.1) | async-done | bytes 73760 | tf_op jit(solution)/shard_map/all_to_all | solution.py:63
  38.4 3.3 %all-to-all-start = ((bf16[8,1,9]{2,1,0:T(2,128)(2,1)}), bf16[8,1,9]{2,1,0:T(2,128)(2,1)S(1)}, u32[]{:S(2)}, u32[]{:S(2)}) async-start(bf16[8,1,9]{2,1,0:T(2,128)(2,1)} %copy.45), calls=%async_computation | async-start | bytes 8192 | tf_op jit(solution)/shard_map/all_to_all | solution.py:64
  41.8 1.9 %collective-permute-start = (bf16[1,8,9,512]{3,2,1,0:T(8,128)(2,1)}, bf16[1,8,9,512]{3,2,1,0:T(8,128)(2,1)S(1)}, u32[]{:S(2)}, u32[]{:S(2)}) collective-permute-start(bf16[1,8,9,512]{3,2,1,0:T(8,128)(2,1)} %bitcast.5), channel_id=1, source_target_pairs={{0,2},{2,0},{4,6},{6,4},{8,10},{10,8},{12,14},{14,12},{1,3},{3,1},... | collective-permute-start | bytes 221192 | tf_op jit(solution)/shard_map/ppermute | solution.py:17
  43.7 1.1 %maximum_select_fusion.3 = bf16[2,8,9,512]{3,2,1,0:T(8,128)(2,1)S(1)} fusion(bf16[1,8,9,512]{3,2,1,0:T(8,128)(2,1)} %collective-permute-done.2, bf16[1,8,9,512]{3,2,1,0:T(8,128)(2,1)S(1)} %bitcast.94, pred[]{:T(512)S(6)} %eq.98), kind=kLoop, calls=%fused_computation.20 | loop fusion | flops 221184 | bytes 294913 | tf_op jit(solution)/shard_map/jit(_where)/select_n | solution.py:71
  44.7 1.5 %collective-permute-start.3 = (bf16[2,8,9,512]{3,2,1,0:T(8,128)(2,1)S(1)}, bf16[2,8,9,512]{3,2,1,0:T(8,128)(2,1)}, u32[]{:S(2)}, u32[]{:S(2)}) collective-permute-start(bf16[2,8,9,512]{3,2,1,0:T(8,128)(2,1)S(1)} %maximum_select_fusion.3), channel_id=1, source_target_pairs={{0,4},{4,0},{2,6},{6,2},{8,12},{12,8},{10,14},{14,10},{1,5},{5,1},... | collective-permute-start | bytes 442376 | tf_op jit(solution)/shard_map/ppermute | solution.py:17
  46.3 0.8 collective-permute-done
  47.1 1.0 %maximum_select_fusion.2 = bf16[2,8,9,512]{3,2,1,0:T(8,128)(2,1)S(1)} fusion(bf16[1,8,9,512]{3,2,1,0:T(8,128)(2,1)S(1)} %collective-permute-done, bf16[1,8,9,512]{3,2,1,0:T(8,128)(2,1)} %bitcast.5, pred[]{:T(512)S(6)} %eq.98), kind=kLoop, calls=%fused_computation.19 | loop fusion | flops 221184 | bytes 294913 | tf_op jit(solution)/shard_map/jit(_where)/select_n | solution.py:76
  48.1 1.9 %collective-permute-start.1 = (bf16[2,8,9,512]{3,2,1,0:T(8,128)(2,1)S(1)}, bf16[2,8,9,512]{3,2,1,0:T(8,128)(2,1)}, u32[]{:S(2)}, u32[]{:S(2)}) collective-permute-start(bf16[2,8,9,512]{3,2,1,0:T(8,128)(2,1)S(1)} %maximum_select_fusion.2), channel_id=1, source_target_pairs={{0,4},{4,0},{2,6},{6,2},{8,12},{12,8},{10,14},{14,10},{1,5},{5,1},... | collective-permute-start | bytes 442376 | tf_op jit(solution)/shard_map/ppermute | solution.py:17
  50.0 2.8 %collective-permute-done.3 = bf16[2,8,9,512]{3,2,1,0:T(8,128)(2,1)} collective-permute-done((bf16[2,8,9,512]{3,2,1,0:T(8,128)(2,1)S(1)}, bf16[2,8,9,512]{3,2,1,0:T(8,128)(2,1)}, u32[]{:S(2)}, u32[]{:S(2)}) %collective-permute-start.3) | collective-permute-done | bytes 147488 | tf_op jit(solution)/shard_map/ppermute | solution.py:17
  52.8 1.8 %fusion.8 = f32[8,9,384]{2,1,0:T(8,128)S(1)} fusion(bf16[4,512,192]{2,1,0:T(8,128)(2,1)S(1)} %bitcast.90, bf16[4,512,192]{2,1,0:T(8,128)(2,1)S(1)} %bitcast.88, bf16[2,8,9,512]{3,2,1,0:T(8,128)(2,1)} %collective-permute-done.3, bf16[2,8,9,512]{3,2,1,0:T(8,128)(2,1)S(1)} %maximum_select_fusion.3, pred[]{:T(512)S(6)} %eq.97), kind=kOutput, calls=%fused_computation.12 | convolution fusion | flops 116834304 | bytes 1978369 | tf_op jit(solution)/shard_map/pncq,pqf->ncf/dot_general | solution.py:87
  54.6 1.0 collective-permute-done.1
  55.6 1.5 %bitcast_convert_fusion.1 = bf16[192,4,512]{2,0,1:T(8,128)(2,1)S(1)} fusion(bf16[2,8,9,512]{3,2,1,0:T(8,128)(2,1)} %collective-permute-done.1, bf16[2,8,9,512]{3,2,1,0:T(8,128)(2,1)S(1)} %maximum_select_fusion.2, pred[]{:T(512)S(6)} %eq.97, f32[8,9]{1,0:T(8,128)S(1)} %bitcast_convert_fusion.2, f32[8,9,384]{2,1,0:T(8,128)S(1)} %fusion.8), kind=kOutput, calls=%fused_computation.8 | convolution fusion | flops 58440192 | bytes 1462273 | tf_op jit(solution)/shard_map/ncf,pncq->fpq/dot_general | solution.py:108
  57.1 0.6 copy.59
  57.7 1.5 %convert_element_type.128 = bf16[1,192,2048]{2,1,0:T(8,128)(2,1)} reshape(bf16[192,4,512]{2,1,0:T(4,128)(2,1)S(1)} %copy.59) | data formatting | bytes 1572864 | tf_op jit(solution)/shard_map/convert_element_type | solution.py:140
  59.3 0.6 reshape_squeeze.3
  59.9 1.6 %multiply_convert_fusion.2 = (bf16[8,9,192]{2,1,0:T(8,128)(2,1)S(1)}, bf16[8,9,192]{2,1,0:T(8,128)(2,1)S(1)}, bf16[8,9]{1,0:T(8,128)(2,1)S(1)}) fusion(f32[8,9,384]{2,1,0:T(8,128)S(1)} %fusion.8, f32[8,9]{1,0:T(8,128)S(1)} %bitcast_convert_fusion.2, bf16[192,4,512,1]{2,1,0,3:T(4,128)(2,1)S(1)} %bitcast.92, ...), kind=kOutput, calls=%fused_computation.24 | convolution fusion | flops 57300408 | bytes 1247665 | tf_op jit(solution)/shard_map/pncq,fpq->ncf/dot_general | solution.py:90
  61.5 1.7 %bitcast_convert_fusion = bf16[4,512,384]{2,1,0:T(8,128)(2,1)S(1)} fusion(bf16[2,8,9,512]{3,2,1,0:T(8,128)(2,1)} %collective-permute-done.3, bf16[2,8,9,512]{3,2,1,0:T(8,128)(2,1)S(1)} %maximum_select_fusion.3, pred[]{:T(512)S(6)} %eq.97, bf16[8,9,192]{2,1,0:T(8,128)(2,1)S(1)} %get-tuple-element.8, bf16[8,9,192]{2,1,0:T(8,128)(2,1)S(1)} %get-tuple-element.7), kind=kOutput, calls=%fused_computation.2 | convolution fusion | flops 114585600 | bytes 1923073 | tf_op jit(solution)/shard_map/pncq,ncf->pqf/dot_general | solution.py:103
  63.2 0.5 fusion.35
  63.7 1.3 %copy.77 = bf16[2048,192]{0,1:T(8,128)(2,1)} copy(bf16[2048,192]{1,0:T(8,128)(2,1)S(1)} %get-tuple-element.5) | data formatting | bytes 1572864
  65.0 1.3 %copy.76 = bf16[2048,192]{0,1:T(8,128)(2,1)} copy(bf16[2048,192]{1,0:T(8,128)(2,1)S(1)} %get-tuple-element.6) | data formatting | bytes 1572864
  66.3 0.6 copy.54
  66.9 5.8 %all-to-all-start.4 = ((bf16[8,1,9]{2,1,0:T(2,128)(2,1)}), bf16[8,1,9]{2,1,0:T(2,128)(2,1)S(1)}, u32[]{:S(2)}, u32[]{:S(2)}) async-start(bf16[8,1,9]{2,1,0:T(2,128)(2,1)} %copy.54), calls=%async_computation.4 | async-start | bytes 8192 | tf_op jit(solution)/shard_map/all_to_all | solution.py:114
  72.7 2.0 %fusion.5 = bf16[8,9,4,512]{3,1,2,0:T(8,128)(2,1)S(1)} fusion(bf16[4,512,192]{2,1,0:T(8,128)(2,1)} %bitcast.91, bf16[4,512,192]{2,1,0:T(8,128)(2,1)S(1)} %bitcast.89, bf16[8,9,192]{2,1,0:T(8,128)(2,1)S(1)} %get-tuple-element.8, bf16[8,9,192]{2,1,0:T(8,128)(2,1)S(1)} %get-tuple-element.7), kind=kOutput, calls=%fused_computation.11 | convolution fusion | flops 116649984 | bytes 1923072 | tf_op jit(solution)/shard_map/ncf,pqf->pncq/dot_general | solution.py:100
  74.7 0.3 copy.72
  75.0 1.0 reshape.230
  76.0 3.1 %all-to-all-done.4 = bf16[8,1,9]{2,1,0:T(2,128)(2,1)S(1)} async-done(((bf16[8,1,9]{2,1,0:T(2,128)(2,1)}), bf16[8,1,9]{2,1,0:T(2,128)(2,1)S(1)}, u32[]{:S(2)}, u32[]{:S(2)}) %all-to-all-start.4) | async-done | bytes 176 | tf_op jit(solution)/shard_map/all_to_all | solution.py:114
  79.1 3.5 %all-to-all-start.3 = ((bf16[8,9,2048]{2,1,0:T(8,128)(2,1)}), bf16[8,9,2048]{2,1,0:T(8,128)(2,1)S(1)}, u32[]{:S(2)}, u32[]{:S(2)}) async-start(bf16[8,9,2048]{2,1,0:T(8,128)(2,1)} %reshape.230), calls=%async_computation.3 | async-start | bytes 1048576 | tf_op jit(solution)/shard_map/all_to_all | solution.py:113
  82.6 0.3 copy.73
  83.0 0.2 select_reduce_fusion
  83.2 0.7 copy.67
  83.9 9.3 %all-to-all-done.3 = bf16[8,9,2048]{2,1,0:T(8,128)(2,1)S(1)} async-done(((bf16[8,9,2048]{2,1,0:T(8,128)(2,1)}), bf16[8,9,2048]{2,1,0:T(8,128)(2,1)S(1)}, u32[]{:S(2)}, u32[]{:S(2)}) %all-to-all-start.3) | async-done | bytes 294944 | tf_op jit(solution)/shard_map/all_to_all | solution.py:113
  93.3 1.5 %fusion = bf16[128,2048]{1,0:T(8,128)(2,1)} fusion(f32[2,9,2048]{2,1,0:T(8,128)S(1)} %convert_reduce_fusion, s32[2,9]{1,0:T(2,128)S(1)} %select_reduce_fusion.2, pred[2,9]{1,0:T(4,128)(4,1)S(1)} %get-tuple-element.19), kind=kOutput, calls=%fused_computation.4 | convolution fusion | flops 56889856 | bytes 671834 | tf_op jit(solution)/shard_map/dot_general | solution.py:124
  (59 shorter events, 1.6 us)
Async XLA Ops:
  7.2 3.1 %copy-start = (bf16[128,2048]{1,0:T(8,128)(2,1)S(1)}, bf16[128,2048]{1,0:T(8,128)(2,1)}, u32[]{:S(2)}) copy-start(bf16[128,2048]{1,0:T(8,128)(2,1)} %param.7) | copy-start | bytes 1572868
  7.2 3.7 %copy-start.1 = (bf16[128,2048]{1,0:T(8,128)(2,1)S(1)}, bf16[128,2048]{1,0:T(8,128)(2,1)}, u32[]{:S(2)}) copy-start(bf16[128,2048]{1,0:T(8,128)(2,1)} %param.8) | copy-start | bytes 1572868
  11.5 19.5 %copy-start.9 = (bf16[128,8]{0,1:T(8,128)(2,1)S(1)}, bf16[128,8]{0,1:T(8,128)(2,1)}, u32[]{:S(2)}) copy-start(bf16[128,8]{0,1:T(8,128)(2,1)} %param.10) | copy-start | bytes 6148
  11.6 22.4 %copy-start.5 = (bf16[1,2048,192]{1,2,0:T(8,128)(2,1)S(1)}, bf16[1,2048,192]{1,2,0:T(8,128)(2,1)}, u32[]{:S(2)}) copy-start(bf16[1,2048,192]{1,2,0:T(8,128)(2,1)} %param.11) | copy-start | bytes 2359300
  11.8 22.7 %copy-start.6 = (bf16[1,2048,192]{1,2,0:T(8,128)(2,1)S(1)}, bf16[1,2048,192]{1,2,0:T(8,128)(2,1)}, u32[]{:S(2)}) copy-start(bf16[1,2048,192]{1,2,0:T(8,128)(2,1)} %param.12) | copy-start | bytes 2359300
  12.5 14.6 %all-to-all-start.2 = ((bf16[8,9,512]{2,1,0:T(8,128)(2,1)}), bf16[8,9,512]{2,1,0:T(8,128)(2,1)S(1)}, u32[]{:S(2)}, u32[]{:S(2)}) async-start(bf16[8,9,512]{2,1,0:T(8,128)(2,1)} %reshape.192), calls=%async_computation.2 | async-start | bytes 262144 | tf_op jit(solution)/shard_map/all_to_all | solution.py:62
  27.1 11.4 %all-to-all-start.1 = ((bf16[8,9,512]{2,1,0:T(8,128)(2,1)}), bf16[8,9,512]{2,1,0:T(8,128)(2,1)}, u32[]{:S(2)}, u32[]{:S(2)}) async-start(bf16[8,9,512]{2,1,0:T(8,128)(2,1)} %reshape.191), calls=%async_computation.1 | async-start | bytes 262144 | tf_op jit(solution)/shard_map/all_to_all | solution.py:63
  31.3 12.4 %collective-permute-start.2 = (bf16[1,8,9,512]{3,2,1,0:T(8,128)(2,1)S(1)}, bf16[1,8,9,512]{3,2,1,0:T(8,128)(2,1)}, u32[]{:S(2)}, u32[]{:S(2)}) collective-permute-start(bf16[1,8,9,512]{3,2,1,0:T(8,128)(2,1)S(1)} %bitcast.93), channel_id=1, source_target_pairs={{0,2},{2,0},{4,6},{6,4},{8,10},{10,8},{12,14},{14,12},{1,3},{3,1},... | collective-permute-start | bytes 221192 | tf_op jit(solution)/shard_map/ppermute | solution.py:17
  34.5 20.1 %copy-start.2 = (bf16[1,2048,192]{2,1,0:T(8,128)(2,1)}, bf16[1,2048,192]{2,1,0:T(8,128)(2,1)S(1)}, u32[]{:S(2)}) copy-start(bf16[1,2048,192]{2,1,0:T(8,128)(2,1)S(1)} %copy.48) | copy-start | bytes 2359300
  35.0 19.6 %copy-start.4 = (bf16[1,2048,192]{2,1,0:T(8,128)(2,1)}, bf16[1,2048,192]{2,1,0:T(8,128)(2,1)S(1)}, u32[]{:S(2)}) copy-start(bf16[1,2048,192]{2,1,0:T(8,128)(2,1)S(1)} %copy.49) | copy-start | bytes 2359300
  38.4 11.5 %all-to-all-start = ((bf16[8,1,9]{2,1,0:T(2,128)(2,1)}), bf16[8,1,9]{2,1,0:T(2,128)(2,1)S(1)}, u32[]{:S(2)}, u32[]{:S(2)}) async-start(bf16[8,1,9]{2,1,0:T(2,128)(2,1)} %copy.45), calls=%async_computation | async-start | bytes 8192 | tf_op jit(solution)/shard_map/all_to_all | solution.py:64
  41.8 53.1 %reduce-scatter.8.cloned.1.call-start = ((), (), s32[]{:S(2)}) async-start(), calls=%async_computation.10 | async-start | bytes 1179648 | tf_op jit(solution)/shard_map/reduce_scatter | solution.py:139
  41.8 5.2 %collective-permute-start = (bf16[1,8,9,512]{3,2,1,0:T(8,128)(2,1)}, bf16[1,8,9,512]{3,2,1,0:T(8,128)(2,1)S(1)}, u32[]{:S(2)}, u32[]{:S(2)}) collective-permute-start(bf16[1,8,9,512]{3,2,1,0:T(8,128)(2,1)} %bitcast.5), channel_id=1, source_target_pairs={{0,2},{2,0},{4,6},{6,4},{8,10},{10,8},{12,14},{14,12},{1,3},{3,1},... | collective-permute-start | bytes 221192 | tf_op jit(solution)/shard_map/ppermute | solution.py:17
  44.7 8.0 %collective-permute-start.3 = (bf16[2,8,9,512]{3,2,1,0:T(8,128)(2,1)S(1)}, bf16[2,8,9,512]{3,2,1,0:T(8,128)(2,1)}, u32[]{:S(2)}, u32[]{:S(2)}) collective-permute-start(bf16[2,8,9,512]{3,2,1,0:T(8,128)(2,1)S(1)} %maximum_select_fusion.3), channel_id=1, source_target_pairs={{0,4},{4,0},{2,6},{6,2},{8,12},{12,8},{10,14},{14,10},{1,5},{5,1},... | collective-permute-start | bytes 442376 | tf_op jit(solution)/shard_map/ppermute | solution.py:17
  48.1 7.5 %collective-permute-start.1 = (bf16[2,8,9,512]{3,2,1,0:T(8,128)(2,1)S(1)}, bf16[2,8,9,512]{3,2,1,0:T(8,128)(2,1)}, u32[]{:S(2)}, u32[]{:S(2)}) collective-permute-start(bf16[2,8,9,512]{3,2,1,0:T(8,128)(2,1)S(1)} %maximum_select_fusion.2), channel_id=1, source_target_pairs={{0,4},{4,0},{2,6},{6,2},{8,12},{12,8},{10,14},{14,10},{1,5},{5,1},... | collective-permute-start | bytes 442376 | tf_op jit(solution)/shard_map/ppermute | solution.py:17
  57.7 1.6 %copy-start.7 = (bf16[1,192,2048]{2,1,0:T(8,128)(2,1)S(1)}, bf16[1,192,2048]{2,1,0:T(8,128)(2,1)}, u32[]{:S(2)}) copy-start(bf16[1,192,2048]{2,1,0:T(8,128)(2,1)} %param.13) | copy-start | bytes 2359300
  59.2 35.6 %reduce-scatter.6.cloned.1.call-start = ((), (), s32[]{:S(2)}) async-start(), calls=%async_computation.9 | async-start | bytes 1179648 | tf_op jit(solution)/shard_map/reduce_scatter | solution.py:136
  65.0 7.7 %copy-start.3 = (bf16[1,2048,192]{2,1,0:T(8,128)(2,1)S(1)}, bf16[1,2048,192]{2,1,0:T(8,128)(2,1)}, u32[]{:S(2)}) copy-start(bf16[1,2048,192]{2,1,0:T(8,128)(2,1)} %copy-done.2) | copy-start | bytes 2359300
  65.0 29.8 %reduce-scatter.4.cloned.1.call-start = ((), (), s32[]{:S(2)}) async-start(), calls=%async_computation.8 | async-start | bytes 1179648 | tf_op jit(solution)/shard_map/reduce_scatter | solution.py:133
  66.9 12.2 %all-to-all-start.4 = ((bf16[8,1,9]{2,1,0:T(2,128)(2,1)}), bf16[8,1,9]{2,1,0:T(2,128)(2,1)S(1)}, u32[]{:S(2)}, u32[]{:S(2)}) async-start(bf16[8,1,9]{2,1,0:T(2,128)(2,1)} %copy.54), calls=%async_computation.4 | async-start | bytes 8192 | tf_op jit(solution)/shard_map/all_to_all | solution.py:114
  74.7 7.9 %copy-start.8 = (pred[2,9,1024]{2,1,0:T(8,128)(4,1)S(1)}, pred[2,9,1024]{2,1,0:T(8,128)(4,1)}, u32[]{:S(2)}) copy-start(pred[2,9,1024]{2,1,0:T(8,128)(4,1)} %get-tuple-element.18) | copy-start | bytes 55300
  79.1 14.1 %all-to-all-start.3 = ((bf16[8,9,2048]{2,1,0:T(8,128)(2,1)}), bf16[8,9,2048]{2,1,0:T(8,128)(2,1)S(1)}, u32[]{:S(2)}, u32[]{:S(2)}) async-start(bf16[8,9,2048]{2,1,0:T(8,128)(2,1)} %reshape.230), calls=%async_computation.3 | async-start | bytes 1048576 | tf_op jit(solution)/shard_map/all_to_all | solution.py:113
Sparse Core Ops, SparseCore 0:
  59.4 9.4 reduce-scatter.7
  71.8 9.3 reduce-scatter.5
  84.0 9.4 reduce-scatter.3
where the time goes:
time: 102 us; the launch traced here: 101 us
  starting transfers between devices  31.2 us (31%)
  waiting for transfers between devices  27.1 us (27%)
  local copies, waits for them, and re-layouts  14.5 us (14%)
  between operations  14.1 us (14%)
  matrix products  10.1 us (10%)
  other arithmetic  4.39 us (4%)
    all_to_all x1, waiting for transfers between devices, body(): lax.all_to_all(full_rows, 'expert', split_axis=0, concat_axis=0, tiled=True)  9.32 us
    all_to_all x1, starting transfers between devices, body(): lax.all_to_all(split_input, 'expert', split_axis=0, concat_axis=0, tiled=...  7.25 us
    ppermute x4, starting transfers between devices, from_partner(): return lax.ppermute(block, axis, route)  7.24 us
    all_to_all x1, waiting for transfers between devices, body(): lax.all_to_all(split_input, 'expert', split_axis=0, concat_axis=0, tiled=...  6.61 us
    all_to_all x1, starting transfers between devices, body(): lax.all_to_all(combine_part, 'expert', split_axis=0, concat_axis=0, tiled...  5.76 us
    unnamed x26, local copies, waits for them, and re-layouts  4.77 us
    ppermute x4, waiting for transfers between devices, from_partner(): return lax.ppermute(block, axis, route)  4.54 us
    all_to_all x1, starting transfers between devices, body(): lax.all_to_all(split_grad, 'expert', split_axis=0, concat_axis=0, tiled=T...  4 us
  transfers between devices with their start and end apart: 12, of which 7 were waited for; matrix products, arithmetic and copies ran while one was open for 20% of the time, Pallas kernels for 0%

commit v1 on v0

v1 whole, which is shorter than its diff:
```python
import jax
import jax.numpy as jnp
from jax import lax
from jax.experimental import pallas as pl
from jax.experimental.pallas import tpu as pltpu
from jax.sharding import PartitionSpec as P

SPLIT = 4
MAIN = 8
TILE = 128
GROUP = 8
VMEM_LIMIT = 60 * 1024 * 1024
F32 = jnp.float32
BF16 = jnp.bfloat16


def iota(shape, axis):
    return lax.broadcasted_iota(jnp.int32, shape, axis)


def dot(a, b, contract):
    return lax.dot_general(a, b, ((contract[:1], contract[1:]), ((), ())), preferred_element_type=F32)


def places(picks, expert):
    named = [jnp.any(picks == e, axis=0, keepdims=True) for e in expert]
    table = jnp.concatenate([n.astype(F32) for n in named], axis=0)
    count, toks = table.shape
    pad = -count % 8
    if pad:
        table = jnp.concatenate([table, jnp.zeros((pad, toks), F32)], axis=0)
    before = (iota((toks, toks), 0) < iota((toks, toks), 1)).astype(BF16)
    rank = dot(table.astype(BF16), before, (1, 0))
    rank = jnp.where(table > 0, rank, -1.0)
    return [rank[i : i + 1] for i in range(count)]


def pack_kernel(where_ref, picks_ref, gates_ref, tok_ref, grad_ref, *outs):
    window = len(outs)
    quad = where_ref[0]
    picks = picks_ref[...]
    gates = gates_ref[...].astype(F32)
    features = tok_ref.shape[1]
    fold = features // MAIN
    experts = [quad ^ k for k in range(window)]
    ranks = places(picks, experts)
    toks = picks.shape[1]
    seat = iota((MAIN, toks), 0).astype(F32)
    mains = [(r == seat).astype(F32) for r in ranks]
    last = jnp.concatenate([(r == float(MAIN)).astype(F32) for r in ranks], axis=0)
    pad = -window % 8
    if pad:
        last = jnp.concatenate([last, jnp.zeros((pad, toks), F32)], axis=0)
    choose = jnp.concatenate(mains + [last], axis=0).astype(BF16)
    tok_rows = dot(choose, tok_ref[...], (1, 0))
    grad_rows = dot(choose, grad_ref[...], (1, 0))
    row = iota((MAIN, fold), 0)
    lane = iota((MAIN, TILE), 1)
    for k, out in enumerate(outs):
        top = slice(k * MAIN, (k + 1) * MAIN)
        out[:, :features] = jnp.concatenate([tok_rows[top], grad_rows[top]], axis=0).astype(BF16)
        folded = []
        for rows in (tok_rows, grad_rows):
            at = window * MAIN + k
            total = jnp.zeros((MAIN, fold), F32)
            for c in range(MAIN):
                total = jnp.where(row == c, rows[at : at + 1, c * fold : (c + 1) * fold], total)
            folded.append(total)
        out[:, features : features + fold] = jnp.concatenate(folded, axis=0).astype(BF16)
        weight = jnp.sum(jnp.where(picks == experts[k], gates, 0.0), axis=0, keepdims=True)
        seat_gate = jnp.sum(mains[k] * weight, axis=1, keepdims=True)
        last_gate = jnp.sum(last[k : k + 1] * weight, axis=1, keepdims=True)
        tile = jnp.where(lane == 0, seat_gate, jnp.where(lane == 1, last_gate, 0.0))
        out[:, features + fold :] = jnp.concatenate([tile, tile], axis=0).astype(BF16)


def expert_kernel(
    where_ref, z0, z1, z2, z3, wg_ref, wu_ref, wd_ref, m0, m1, m2, m3, keep_ref, hid_ref, send_ref
):
    features = wg_ref.shape[1]
    hidden = wg_ref.shape[0]
    fold = features // MAIN
    half = features // 2
    core = where_ref[1]
    zs, ms = (z0, z1, z2, z3), (m0, m1, m2, m3)
    pair = 2 * MAIN
    per = GROUP // SPLIT
    rows_in = per * pair
    groups = z0.shape[0] // rows_in

    def work(g):
        if groups == 1:
            src = slice(0, rows_in)
            dst = slice(0, per * MAIN)
            all_rows = slice(0, (GROUP + 1) * pair)
        else:
            src = pl.ds(pl.multiple_of(g * rows_in, rows_in), rows_in)
            dst = pl.ds(pl.multiple_of(g * per * MAIN, per * MAIN), per * MAIN)
            all_rows = pl.ds(pl.multiple_of(g * (GROUP + 1) * pair, pair), (GROUP + 1) * pair)
        main = [z[src, :features] for z in zs]
        bent = jnp.concatenate([z[src, features : features + fold] for z in zs], axis=0)
        tiles = [z[src, features + fold :].astype(F32) for z in zs]
        n = GROUP * pair
        r, q = iota((n, n), 0), iota((n, n), 1)
        swap = ((r & 8) == (q & 8)) & ((r >> 4) == (q & 7)) & ((r & 7) == (q >> 4))
        flat = dot(swap.astype(BF16), bent, (1, 0)).astype(BF16)
        ninth = jnp.concatenate([flat[c * pair : (c + 1) * pair] for c in range(MAIN)], axis=1)
        rows = jnp.concatenate(main + [ninth], axis=0)
        pre_gate = dot(rows, wg_ref[...], (1, 1))
        pre_up = dot(rows, wu_ref[...], (1, 1))
        back = dot(rows, wd_ref[...], (1, 1))
        pieces = GROUP + 1
        upper = lambda v: v.reshape(pieces, 2, MAIN, hidden)[:, 0].reshape(pieces * MAIN, hidden)
        lower = lambda v: v.reshape(pieces, 2, MAIN, hidden)[:, 1].reshape(pieces * MAIN, hidden)
        pre_gate, pre_up, back = upper(pre_gate), upper(pre_up), lower(back)
        columns = []
        last = jnp.zeros((MAIN, 1), F32)
        seat = iota((MAIN, 1), 0)
        for p in range(GROUP):
            tile = tiles[p // per][(p % per) * pair : (p % per) * pair + MAIN]
            columns.append(tile[:, 0:1])
            last = jnp.where(seat == p, tile[:, 1:2], last)
        gate = jnp.concatenate(columns + [last], axis=0)
        sig = 1.0 / (1.0 + jnp.exp(-pre_gate))
        silu = pre_gate * sig
        slope = sig * (1.0 + pre_gate * (1.0 - sig))
        act = silu * pre_up
        combine = jnp.sum(back * act, axis=1, keepdims=True)
        scaled = gate * act
        gated = gate * back
        g_gate = (gated * slope * pre_up).astype(BF16)
        g_up = (gated * silu).astype(BF16)
        part = dot(g_gate, wg_ref[...], (1, 0)) + dot(g_up, wu_ref[...], (1, 0))
        tail = part[GROUP * MAIN :].astype(BF16).astype(F32)
        stack = jnp.concatenate([tail[:, c * fold : (c + 1) * fold] for c in range(MAIN)], axis=0)
        n = GROUP * MAIN
        r, q = iota((n, n), 0), iota((n, n), 1)
        turn = ((r >> 3) == (q & 7)) & ((r & 7) == (q >> 3))
        folded = dot(turn.astype(BF16), stack.astype(BF16), (1, 0))
        lane = iota((MAIN, TILE), 1)
        notes = []
        for p in range(GROUP):
            at = GROUP * MAIN + p
            notes.append(
                jnp.where(
                    lane == 0,
                    combine[p * MAIN : (p + 1) * MAIN],
                    jnp.where(lane == 1, combine[at : at + 1], 0.0),
                )
            )
        for j, m in enumerate(ms):
            span = slice(j * per * MAIN, (j + 1) * per * MAIN)
            m[dst, :features] = part[span].astype(BF16)
            m[dst, features : features + fold] = folded[span].astype(BF16)
            m[dst, features + fold :] = jnp.concatenate(
                notes[j * per : (j + 1) * per], axis=0
            ).astype(BF16)
        none = jnp.zeros((pieces, MAIN, hidden), F32)

        def lay(v, place):
            v = v.astype(F32).reshape(pieces, MAIN, hidden)
            both = [v, none] if place == 0 else [none, v]
            return jnp.stack(both, axis=1).reshape(pieces * 2 * MAIN, hidden).astype(BF16)

        hid = [lay(g_gate, 0), lay(g_up, 0), lay(scaled, 1)]
        low, high = rows[:, :half], rows[:, half:]
        keep_ref[all_rows, :] = jnp.where(core == 0, low, high)
        send_ref[all_rows, :half] = jnp.where(core == 0, high, low)
        for i, h in enumerate(hid):
            hid_ref[all_rows, i * hidden : (i + 1) * hidden] = h
            send_ref[all_rows, half + i * hidden : half + (i + 1) * hidden] = h

    if groups == 1:
        work(0)
    else:
        lax.fori_loop(0, groups, lambda g, c: (work(g), c)[1], 0)


def weights_kernel(keep_ref, hid_ref, peer_ref, gate_ref, up_ref, down_ref):
    half = keep_ref.shape[1]
    hidden = gate_ref.shape[0]
    outs = (gate_ref, up_ref, down_ref)
    for i, out in enumerate(outs):
        cols = slice(i * hidden, (i + 1) * hidden)
        far = slice(half + i * hidden, half + (i + 1) * hidden)
        total = dot(hid_ref[:, cols], keep_ref[...], (0, 0))
        total = total + dot(peer_ref[:, far], peer_ref[:, :half], (0, 0))
        out[...] = total.astype(BF16)


def finish_kernel(where_ref, picks_ref, o0, o1, o2, o3, *rest):
    far, (grad_ref, comb_ref) = rest[:-2], rest[-2:]
    window = 1 + len(far)
    quad = where_ref[0]
    picks = picks_ref[...]
    experts = [quad ^ k for k in range(window)]
    ranks = places(picks, experts)
    features = grad_ref.shape[1]
    fold = features // MAIN
    toks = picks.shape[1]
    seat = iota((MAIN, toks), 0).astype(F32)
    mains = [(r == seat).astype(F32) for r in ranks]
    lasts = [(r == float(MAIN)).astype(F32) for r in ranks]
    blocks = [(0, o[:MAIN, :].astype(F32)) for o in (o0, o1, o2, o3)]
    blocks += [(1 + k, f[...].astype(F32)) for k, f in enumerate(far)]
    row = iota((MAIN, toks), 0)
    for c in range(MAIN):
        cols = slice(c * fold, (c + 1) * fold)
        left, right = [], []
        for k, v in blocks:
            left += [mains[k], jnp.where(row == c, lasts[k], 0.0)]
            right += [v[:, cols], v[:, features : features + fold]]
        left = jnp.concatenate(left, axis=0).astype(BF16)
        right = jnp.concatenate(right, axis=0).astype(BF16)
        grad_ref[:, cols] = dot(left, right, (0, 0)).astype(BF16)
    terms = [jnp.zeros((1, toks), F32) for _ in range(window)]
    for k, v in blocks:
        note = v[:, features + fold :]
        terms[k] = terms[k] + jnp.sum(mains[k] * note[:, 0:1], axis=0, keepdims=True)
        terms[k] = terms[k] + lasts[k] * note[0:1, 1:2]
    comb = jnp.zeros(picks.shape, F32)
    for k in range(window):
        comb = comb + jnp.where(picks == experts[k], terms[k], 0.0)
    comb_ref[...] = comb


VM = pl.BlockSpec(memory_space=pltpu.VMEM)
SM = pl.BlockSpec(memory_space=pltpu.SMEM)


def call(kernel, outs, name, in_specs, flops, nbytes):
    return pl.pallas_call(
        kernel,
        out_shape=[jax.ShapeDtypeStruct(s, t) for s, t in outs],
        in_specs=in_specs,
        out_specs=[VM] * len(outs),
        compiler_params=pltpu.CompilerParams(vmem_limit_bytes=VMEM_LIMIT),
        cost_estimate=pl.CostEstimate(flops=flops, bytes_accessed=nbytes, transcendentals=0),
        name=name,
    )


def swap_by(block, mask):
    count = lax.axis_size("expert")
    return lax.ppermute(block, "expert", [(i, i ^ mask) for i in range(count)])


def body(tokens, out_grad, choices, gates, gate_weight, up_weight, down_weight):
    members = lax.axis_size("expert")
    position = lax.axis_index("expert")
    core = lax.axis_index("dp")
    toks, features = tokens.shape
    hidden = gate_weight.shape[2]
    window = members // SPLIT
    fold = features // MAIN
    half = features // 2
    width = features + fold + TILE
    where = jnp.stack([position // SPLIT, core]).astype(jnp.int32)
    picks, gates_t = choices.T, gates.T
    wg, wu, wd = gate_weight[0].T, up_weight[0].T, down_weight[0]

    packed = call(
        pack_kernel,
        [((2 * MAIN, width), BF16)] * window,
        "pack",
        [SM, VM, VM, VM, VM],
        2 * (MAIN + 1) * window * toks * features * 2,
        4 * toks * features,
    )(where, picks, gates_t, tokens, out_grad)
    own, others = packed[0], packed[1:]
    arrived = [swap_by(o, SPLIT * (k + 1)) for k, o in enumerate(others)]
    near = [own] + [swap_by(own, j) for j in range(1, SPLIT)]
    from_far = arrived[0] if window == 2 else jnp.concatenate(arrived, axis=0)
    far = [from_far] + [swap_by(from_far, j) for j in range(1, SPLIT)]
    zs = [jnp.concatenate([a, b], axis=0) for a, b in zip(near, far)]

    groups = members // GROUP
    all_rows = groups * (GROUP + 1) * 2 * MAIN
    *messages, keep, hid, send = call(
        expert_kernel,
        [((window * MAIN, width), BF16)] * SPLIT
        + [((all_rows, half), BF16), ((all_rows, 3 * hidden), BF16), ((all_rows, half + 3 * hidden), BF16)],
        "expert",
        [SM] + [VM] * 7,
        2 * all_rows * features * hidden * 5,
        6 * features * hidden,
    )(where, *zs, wg, wu, wd)
    back = [messages[0]] + [swap_by(messages[j], j) for j in range(1, SPLIT)]
    total = sum(b[MAIN:].astype(F32) for b in back).astype(BF16)
    homes = [
        swap_by(total[k * MAIN : (k + 1) * MAIN], SPLIT * (k + 1)) for k in range(window - 1)
    ]
    peer = lax.ppermute(send, "dp", [(0, 1), (1, 0)])
    gate_grad, up_grad, down_grad = call(
        weights_kernel,
        [((hidden, half), BF16)] * 3,
        "weights",
        [VM] * 3,
        2 * 2 * all_rows * half * hidden * 3,
        6 * half * hidden,
    )(keep, hid, peer)
    in_grad, combine = call(
        finish_kernel,
        [((toks, features), BF16), ((choices.shape[1], toks), F32)],
        "finish",
        [SM] + [VM] * (SPLIT + window),
        2 * toks * features * 16 * (SPLIT + window),
        2 * toks * features,
    )(where, picks, *back, *homes)
    return (
        in_grad,
        combine.T,
        gate_grad.T[None],
        up_grad.T[None],
        down_grad[None],
    )


def solution(mesh):
    return jax.shard_map(
        body,
        mesh=mesh,
        in_specs=(
            P(("groups", "expert", "dp"), None),
            P(("groups", "expert", "dp"), None),
            P(("groups", "expert", "dp"), None),
            P(("groups", "expert", "dp"), None),
            P("expert", None, None),
            P("expert", None, None),
            P("expert", None, None),
        ),
        out_specs=(
            P(("groups", "expert", "dp"), None),
            P(("groups", "expert", "dp"), None),
            P(("groups", "expert"), "dp", None),
            P(("groups", "expert"), "dp", None),
            P(("groups", "expert"), None, "dp"),
        ),
        check_vma=False,
    )
```

time: 102 us -> 45.9 us (0.45)
  waiting for transfers between devices: 27.1 us -> 8.62 us
  between operations: 14.1 us -> 0.69 us
  starting transfers between devices: 31.2 us -> 17.8 us
  local copies, waits for them, and re-layouts: 14.5 us -> 1.38 us
  Pallas kernels: 0 us -> 11.9 us
  matrix products: 10.1 us -> 0 us
    all_to_all x5 -> x0, starting transfers between devices: 23.8 us -> none  [the longest x1 7.25 us: body(): lax.all_to_all(split_input, 'expert', split_axis=0, concat_axis=0, tiled=...]
    all_to_all x5 -> x0, waiting for transfers between devices: 22.5 us -> none  [the longest x1 9.32 us: body(): lax.all_to_all(full_rows, 'expert', split_axis=0, concat_axis=0, tiled=True)]
    pallas_call x0 -> x4, Pallas kernels: none -> 11.9 us  [the longest x1 4.53 us: body(): call(expert_kernel, [((window * MAIN, width), BF16)] * SPLIT + [((all_row...]
    ppermute x4 -> x12, starting transfers between devices: 7.24 us -> 17.8 us  [the longest x11 17.8 us: swap_by(): return lax.ppermute(block, 'expert', [(i, i ^ mask) for i in range(count)])]
    dot_general x6 -> x0, matrix products: 10.1 us -> none  [the longest x1 1.99 us: body(): jnp.einsum('ncf,pqf->pncq', grad_both, w_both, preferred_element_type=jnp...]
    ppermute x4 -> x12, waiting for transfers between devices: 4.54 us -> 8.62 us  [the longest x11 8.62 us: swap_by(): return lax.ppermute(block, 'expert', [(i, i ^ mask) for i in range(count)])]
    concatenate x1 -> x4, other arithmetic: 0.04 us -> 3.6 us  [body(): zs = [jnp.concatenate([a, b], axis=0) for a, b in zip(near, far)]]
    unnamed x26 -> x10, local copies, waits for them, and re-layouts: 4.77 us -> 1.38 us
  transfers between devices with their start and end apart: 12 -> 12, of which waited for: 7 -> 6; matrix products, arithmetic and copies ran while one was open for 20% -> 8% of each run, Pallas kernels for 0% -> 5%
where the time goes in v1:
time: 45.9 us; the launch traced here: 45.5 us
  starting transfers between devices  17.8 us (39%)
  Pallas kernels  11.9 us (26%)
  waiting for transfers between devices  8.62 us (19%)
  other arithmetic  5.07 us (11%)
  local copies, waits for them, and re-layouts  1.38 us (3%)
  between operations  0.69 us (2%)
    ppermute x11, starting transfers between devices, swap_by(): return lax.ppermute(block, 'expert', [(i, i ^ mask) for i in range(count)])  17.8 us
    ppermute x11, waiting for transfers between devices, swap_by(): return lax.ppermute(block, 'expert', [(i, i ^ mask) for i in range(count)])  8.62 us
    pallas_call x1, Pallas kernels, body(): call(expert_kernel, [((window * MAIN, width), BF16)] * SPLIT + [((all_row...  4.53 us
    concatenate x4, other arithmetic, body(): zs = [jnp.concatenate([a, b], axis=0) for a, b in zip(near, far)]  3.6 us
    pallas_call x1, Pallas kernels, body(): call(weights_kernel, [((hidden, half), BF16)] * 3, 'weights', [VM] * 3, 2...  2.79 us
    pallas_call x1, Pallas kernels, body(): call(pack_kernel, [((2 * MAIN, width), BF16)] * window, 'pack', [SM, VM,...  2.31 us
    pallas_call x1, Pallas kernels, body(): call(finish_kernel, [((toks, features), BF16), ((choices.shape[1], toks),...  2.29 us
    unnamed x10, local copies, waits for them, and re-layouts  1.38 us
  transfers between devices with their start and end apart: 12, of which 6 were waited for; matrix products, arithmetic and copies ran while one was open for 8% of the time, Pallas kernels for 5%

profile of v1, /device:TPU:0, one launch (start us, length us, event | category | flops | bytes accessed | tf_op | source)
XLA Modules:
  0.0 45.5 jit_solution(10195428884385567908)
XLA Ops:
  0.6 0.7 %pad_add_fusion.where_ref = s32[2]{0:T(128)} fusion(s32[1]{0:T(128)} %bitcast.1, s32[1]{0:T(128)} %bitcast), kind=kLoop, calls=%fused_computation.5 | loop fusion | flops 2 | bytes 16 | tf_op jit(solution)/shard_map/stack | solution.py:258
  1.3 2.3 %pack.1 = (bf16[16,2432]{1,0:T(8,128)(2,1)}, bf16[16,2432]{1,0:T(8,128)(2,1)}) custom-call(s32[2]{0:T(128)} %pad_add_fusion.where_ref, s32[8,128]{1,0:T(8,128)} %bitcast.22, bf16[8,128]{1,0:T(8,128)(2,1)} %bitcast.24, bf16[128,2048]{1,0:T(8,128)(2,1)} %tok_ref.1, bf16[128,2048]{1,0:T(8,128)(2,1)} %grad_ref.1), custom_call_target="tpu_custom_call" | custom-call | flops 18874368 | bytes 1048576 | tf_op jit(solution)/shard_map/pack/pallas_call | solution.py:262
  3.6 4.0 %collective-permute-start = (bf16[16,2432]{1,0:T(8,128)(2,1)}, bf16[16,2432]{1,0:T(8,128)(2,1)S(1)}, u32[]{:S(2)}, u32[]{:S(2)}) collective-permute-start(bf16[16,2432]{1,0:T(8,128)(2,1)} %get-tuple-element.20), channel_id=1, source_target_pairs={{0,8},{2,10},{4,12},{6,14},{8,0},{10,2},{12,4},{14,6},{1,9},{3,11}... | collective-permute-start | bytes 233480 | tf_op jit(solution)/shard_map/ppermute | solution.py:245
  7.7 1.6 %collective-permute-start.3 = (bf16[16,2432]{1,0:T(8,128)(2,1)}, bf16[16,2432]{1,0:T(8,128)(2,1)S(1)}, u32[]{:S(2)}, u32[]{:S(2)}) collective-permute-start(bf16[16,2432]{1,0:T(8,128)(2,1)} %get-tuple-element.19), channel_id=1, source_target_pairs={{0,4},{2,6},{4,0},{6,2},{8,12},{10,14},{12,8},{14,10},{1,5},{3,7},... | collective-permute-start | bytes 233480 | tf_op jit(solution)/shard_map/ppermute | solution.py:245
  9.2 1.4 %collective-permute-start.5 = (bf16[16,2432]{1,0:T(8,128)(2,1)}, bf16[16,2432]{1,0:T(8,128)(2,1)S(1)}, u32[]{:S(2)}, u32[]{:S(2)}) collective-permute-start(bf16[16,2432]{1,0:T(8,128)(2,1)} %get-tuple-element.19), channel_id=1, source_target_pairs={{0,6},{2,4},{4,2},{6,0},{8,14},{10,12},{12,10},{14,8},{1,7},{3,5},... | collective-permute-start | bytes 233480 | tf_op jit(solution)/shard_map/ppermute | solution.py:245
  10.6 0.5 %collective-permute-start.1 = (bf16[16,2432]{1,0:T(8,128)(2,1)}, bf16[16,2432]{1,0:T(8,128)(2,1)S(1)}, u32[]{:S(2)}, u32[]{:S(2)}) collective-permute-start(bf16[16,2432]{1,0:T(8,128)(2,1)} %get-tuple-element.19), channel_id=1, source_target_pairs={{0,2},{2,0},{4,6},{6,4},{8,10},{10,8},{12,14},{14,12},{1,3},{3,1},... | collective-permute-start | bytes 233480 | tf_op jit(solution)/shard_map/ppermute | solution.py:245
  11.1 0.2 collective-permute-done
  11.4 1.4 %collective-permute-start.4 = (bf16[16,2432]{1,0:T(8,128)(2,1)S(1)}, bf16[16,2432]{1,0:T(8,128)(2,1)S(1)}, u32[]{:S(2)}, u32[]{:S(2)}) collective-permute-start(bf16[16,2432]{1,0:T(8,128)(2,1)S(1)} %collective-permute-done), channel_id=1, source_target_pairs={{0,4},{2,6},{4,0},{6,2},{8,12},{10,14},{12,8},{14,10},{1,5},{3,7},... | collective-permute-start | bytes 233480 | tf_op jit(solution)/shard_map/ppermute | solution.py:245
  12.7 2.0 %collective-permute-start.6 = (bf16[16,2432]{1,0:T(8,128)(2,1)S(1)}, bf16[16,2432]{1,0:T(8,128)(2,1)S(1)}, u32[]{:S(2)}, u32[]{:S(2)}) collective-permute-start(bf16[16,2432]{1,0:T(8,128)(2,1)S(1)} %collective-permute-done), channel_id=1, source_target_pairs={{0,6},{2,4},{4,2},{6,0},{8,14},{10,12},{12,10},{14,8},{1,7},{3,5},... | collective-permute-start | bytes 233480 | tf_op jit(solution)/shard_map/ppermute | solution.py:245
  14.8 1.6 %pad_maximum_fusion.z0 = bf16[32,2432]{1,0:T(8,128)(2,1)} fusion(bf16[16,2432]{1,0:T(8,128)(2,1)S(1)} %collective-permute-done, bf16[16,2432]{1,0:T(8,128)(2,1)} %get-tuple-element.19), kind=kLoop, calls=%fused_computation | loop fusion | flops 311296 | bytes 311296 | tf_op jit(solution)/shard_map/concatenate | solution.py:275
  16.3 0.0 collective-permute-done.3
  16.3 0.1 collective-permute-start.2
  16.4 0.0 collective-permute-done.4
  16.4 0.7 %pad_maximum_fusion.2.z2 = bf16[32,2432]{1,0:T(8,128)(2,1)} fusion(bf16[16,2432]{1,0:T(8,128)(2,1)S(1)} %collective-permute-done.4, bf16[16,2432]{1,0:T(8,128)(2,1)S(1)} %collective-permute-done.3), kind=kLoop, calls=%fused_computation.2 | loop fusion | flops 311296 | bytes 311296 | tf_op jit(solution)/shard_map/concatenate | solution.py:275
  17.1 0.0 collective-permute-done.5
  17.1 1.4 %collective-permute-done.6 = bf16[16,2432]{1,0:T(8,128)(2,1)S(1)} collective-permute-done((bf16[16,2432]{1,0:T(8,128)(2,1)S(1)}, bf16[16,2432]{1,0:T(8,128)(2,1)S(1)}, u32[]{:S(2)}, u32[]{:S(2)}) %collective-permute-start.6) | collective-permute-done | bytes 77856 | tf_op jit(solution)/shard_map/ppermute | solution.py:245
  18.5 0.7 %pad_maximum_fusion.3.z3 = bf16[32,2432]{1,0:T(8,128)(2,1)} fusion(bf16[16,2432]{1,0:T(8,128)(2,1)S(1)} %collective-permute-done.6, bf16[16,2432]{1,0:T(8,128)(2,1)S(1)} %collective-permute-done.5), kind=kLoop, calls=%fused_computation.3 | loop fusion | flops 311296 | bytes 311296 | tf_op jit(solution)/shard_map/concatenate | solution.py:275
  19.2 0.0 collective-permute-done.1
  19.2 1.6 %collective-permute-done.2 = bf16[16,2432]{1,0:T(8,128)(2,1)S(1)} collective-permute-done((bf16[16,2432]{1,0:T(8,128)(2,1)S(1)}, bf16[16,2432]{1,0:T(8,128)(2,1)S(1)}, u32[]{:S(2)}, u32[]{:S(2)}) %collective-permute-start.2) | collective-permute-done | bytes 77856 | tf_op jit(solution)/shard_map/ppermute | solution.py:245
  20.7 0.7 %pad_maximum_fusion.1.z1 = bf16[32,2432]{1,0:T(8,128)(2,1)} fusion(bf16[16,2432]{1,0:T(8,128)(2,1)S(1)} %collective-permute-done.2, bf16[16,2432]{1,0:T(8,128)(2,1)S(1)} %collective-permute-done.1), kind=kLoop, calls=%fused_computation.1 | loop fusion | flops 311296 | bytes 311296 | tf_op jit(solution)/shard_map/concatenate | solution.py:275
  21.4 4.5 %expert.1 = (bf16[16,2432]{1,0:T(8,128)(2,1)}, bf16[16,2432]{1,0:T(8,128)(2,1)}, bf16[16,2432]{1,0:T(8,128)(2,1)}, bf16[16,2432]{1,0:T(8,128)(2,1)}, bf16[144,10...) custom-call(s32[2]{0:T(128)} %pad_add_fusion.where_ref, bf16[32,2432]{1,0:T(8,128)(2,1)} %pad_maximum_fusion.z0, ...), custom_call_target="tpu_custom_call" | custom-call | flops 566231040 | bytes 2359296 | tf_op jit(solution)/shard_map/expert/pallas_call | solution.py:279
  25.9 0.1 collective-permute-start.7
  26.0 1.4 %collective-permute-start.8 = (bf16[16,2432]{1,0:T(8,128)(2,1)}, bf16[16,2432]{1,0:T(8,128)(2,1)S(1)}, u32[]{:S(2)}, u32[]{:S(2)}) collective-permute-start(bf16[16,2432]{1,0:T(8,128)(2,1)} %get-tuple-element.23), channel_id=1, source_target_pairs={{0,4},{2,6},{4,0},{6,2},{8,12},{10,14},{12,8},{14,10},{1,5},{3,7},... | collective-permute-start | bytes 233480 | tf_op jit(solution)/shard_map/ppermute | solution.py:245
  27.4 2.0 %collective-permute-start.9 = (bf16[16,2432]{1,0:T(8,128)(2,1)}, bf16[16,2432]{1,0:T(8,128)(2,1)S(1)}, u32[]{:S(2)}, u32[]{:S(2)}) collective-permute-start(bf16[16,2432]{1,0:T(8,128)(2,1)} %get-tuple-element.24), channel_id=1, source_target_pairs={{0,6},{2,4},{4,2},{6,0},{8,14},{10,12},{12,10},{14,8},{1,7},{3,5},... | collective-permute-start | bytes 233480 | tf_op jit(solution)/shard_map/ppermute | solution.py:245
  29.4 0.0 collective-permute-start.11
  29.4 1.6 %collective-permute-done.7.o1 = bf16[16,2432]{1,0:T(8,128)(2,1)S(1)} collective-permute-done((bf16[16,2432]{1,0:T(8,128)(2,1)}, bf16[16,2432]{1,0:T(8,128)(2,1)S(1)}, u32[]{:S(2)}, u32[]{:S(2)}) %collective-permute-start.7) | collective-permute-done | bytes 77856 | tf_op jit(solution)/shard_map/ppermute | solution.py:245
  31.1 0.0 copy-start
  31.1 0.0 collective-permute-done.8.o2
  31.1 0.0 copy-start.1
  31.1 1.8 %collective-permute-done.9.o3 = bf16[16,2432]{1,0:T(8,128)(2,1)S(1)} collective-permute-done((bf16[16,2432]{1,0:T(8,128)(2,1)}, bf16[16,2432]{1,0:T(8,128)(2,1)S(1)}, u32[]{:S(2)}, u32[]{:S(2)}) %collective-permute-start.9) | collective-permute-done | bytes 77856 | tf_op jit(solution)/shard_map/ppermute | solution.py:245
  32.9 0.0 copy-start.2
  32.9 0.8 %add_convert_fusion = bf16[8,2432]{1,0:T(8,128)(2,1)S(1)} fusion(bf16[16,2432]{1,0:T(8,128)(2,1)S(1)} %collective-permute-done.9.o3, bf16[16,2432]{1,0:T(8,128)(2,1)S(1)} %collective-permute-done.8.o2, bf16[16,2432]{1,0:T(8,128)(2,1)S(1)} %collective-permute-done.7.o1, bf16[16,2432]{1,0:T(8,128)(2,1)} %get-tuple-element.21.o0), kind=kLoop, calls=%fused_computation.4 | loop fusion | flops 155648 | bytes 194560 | tf_op jit(solution)/shard_map/convert_element_type | solution.py:289
  33.7 0.0 copy-done
  33.7 0.0 copy-done.1
  33.7 3.3 %collective-permute-start.10 = (bf16[8,2432]{1,0:T(8,128)(2,1)S(1)}, bf16[8,2432]{1,0:T(8,128)(2,1)S(1)}, u32[]{:S(2)}, u32[]{:S(2)}) collective-permute-start(bf16[8,2432]{1,0:T(8,128)(2,1)S(1)} %add_convert_fusion), channel_id=1, source_target_pairs={{0,8},{2,10},{4,12},{6,14},{8,0},{10,2},{12,4},{14,6},{1,9},{3,11}... | collective-permute-start | bytes 116744 | tf_op jit(solution)/shard_map/ppermute | solution.py:245
  37.1 2.0 %collective-permute-done.10.rest_0_ = bf16[8,2432]{1,0:T(8,128)(2,1)S(1)} collective-permute-done((bf16[8,2432]{1,0:T(8,128)(2,1)S(1)}, bf16[8,2432]{1,0:T(8,128)(2,1)S(1)}, u32[]{:S(2)}, u32[]{:S(2)}) %collective-permute-start.10) | collective-permute-done | bytes 38944 | tf_op jit(solution)/shard_map/ppermute | solution.py:245
  39.0 0.0 copy-done.2
  39.0 0.0 copy-start.3
  39.0 0.6 %copy-done.3 = bf16[8,2432]{1,0:T(8,128)(2,1)} copy-done((bf16[8,2432]{1,0:T(8,128)(2,1)}, bf16[8,2432]{1,0:T(8,128)(2,1)S(1)}, u32[]{:S(2)}) %copy-start.3) | copy-done | bytes 38936
  39.6 2.3 %finish.1 = (bf16[128,2048]{1,0:T(8,128)(2,1)}, f32[8,128]{1,0:T(8,128)}) custom-call(s32[2]{0:T(128)} %pad_add_fusion.where_ref, s32[8,128]{1,0:T(8,128)} %bitcast.23, bf16[16,2432]{1,0:T(8,128)(2,1)} %get-tuple-element.21.o0, bf16[16,2432]{1,0:T(8,128)(2,1)} %copy-done, bf16[16,2432]{1,0:T(8,128)(2,1)} %copy-done.1, bf16[16,2432]{1,0:T(8,128)(2,1)} %copy-done.2, ...), custom_call_target="tpu_custom_call" | custom-call | flops 50331648 | bytes 524288 | tf_op jit(solution)/shard_map/finish/pallas_call | solution.py:302
  41.9 0.0 collective-permute-done.11.peer_ref
  41.9 0.0 copy-start.4
  41.9 0.8 %copy-done.4 = bf16[144,1600]{1,0:T(8,128)(2,1)} copy-done((bf16[144,1600]{1,0:T(8,128)(2,1)}, bf16[144,1600]{1,0:T(8,128)(2,1)S(1)}, u32[]{:S(2)}) %copy-start.4) | copy-done | bytes 460824
  42.7 2.8 %weights.1 = (bf16[192,1024]{1,0:T(8,128)(2,1)}, bf16[192,1024]{1,0:T(8,128)(2,1)}, bf16[192,1024]{1,0:T(8,128)(2,1)}) custom-call(bf16[144,1024]{1,0:T(8,128)(2,1)} %get-tuple-element.27.keep_ref, bf16[144,576]{1,0:T(8,128)(2,1)} %get-tuple-element.28.hid_ref, bf16[144,1600]{1,0:T(8,128)(2,1)} %copy-done.4), custom_call_target="tpu_custom_call" | custom-call | flops 339738624 | bytes 1179648 | tf_op jit(solution)/shard_map/weights/pallas_call | solution.py:294
Async XLA Ops:
  3.6 7.7 %collective-permute-start = (bf16[16,2432]{1,0:T(8,128)(2,1)}, bf16[16,2432]{1,0:T(8,128)(2,1)S(1)}, u32[]{:S(2)}, u32[]{:S(2)}) collective-permute-start(bf16[16,2432]{1,0:T(8,128)(2,1)} %get-tuple-element.20), channel_id=1, source_target_pairs={{0,8},{2,10},{4,12},{6,14},{8,0},{10,2},{12,4},{14,6},{1,9},{3,11}... | collective-permute-start | bytes 233480 | tf_op jit(solution)/shard_map/ppermute | solution.py:245
  7.7 8.7 %collective-permute-start.3 = (bf16[16,2432]{1,0:T(8,128)(2,1)}, bf16[16,2432]{1,0:T(8,128)(2,1)S(1)}, u32[]{:S(2)}, u32[]{:S(2)}) collective-permute-start(bf16[16,2432]{1,0:T(8,128)(2,1)} %get-tuple-element.19), channel_id=1, source_target_pairs={{0,4},{2,6},{4,0},{6,2},{8,12},{10,14},{12,8},{14,10},{1,5},{3,7},... | collective-permute-start | bytes 233480 | tf_op jit(solution)/shard_map/ppermute | solution.py:245
  9.2 7.9 %collective-permute-start.5 = (bf16[16,2432]{1,0:T(8,128)(2,1)}, bf16[16,2432]{1,0:T(8,128)(2,1)S(1)}, u32[]{:S(2)}, u32[]{:S(2)}) collective-permute-start(bf16[16,2432]{1,0:T(8,128)(2,1)} %get-tuple-element.19), channel_id=1, source_target_pairs={{0,6},{2,4},{4,2},{6,0},{8,14},{10,12},{12,10},{14,8},{1,7},{3,5},... | collective-permute-start | bytes 233480 | tf_op jit(solution)/shard_map/ppermute | solution.py:245
  10.6 8.6 %collective-permute-start.1 = (bf16[16,2432]{1,0:T(8,128)(2,1)}, bf16[16,2432]{1,0:T(8,128)(2,1)S(1)}, u32[]{:S(2)}, u32[]{:S(2)}) collective-permute-start(bf16[16,2432]{1,0:T(8,128)(2,1)} %get-tuple-element.19), channel_id=1, source_target_pairs={{0,2},{2,0},{4,6},{6,4},{8,10},{10,8},{12,14},{14,12},{1,3},{3,1},... | collective-permute-start | bytes 233480 | tf_op jit(solution)/shard_map/ppermute | solution.py:245
  11.4 5.1 %collective-permute-start.4 = (bf16[16,2432]{1,0:T(8,128)(2,1)S(1)}, bf16[16,2432]{1,0:T(8,128)(2,1)S(1)}, u32[]{:S(2)}, u32[]{:S(2)}) collective-permute-start(bf16[16,2432]{1,0:T(8,128)(2,1)S(1)} %collective-permute-done), channel_id=1, source_target_pairs={{0,4},{2,6},{4,0},{6,2},{8,12},{10,14},{12,8},{14,10},{1,5},{3,7},... | collective-permute-start | bytes 233480 | tf_op jit(solution)/shard_map/ppermute | solution.py:245
  12.7 5.7 %collective-permute-start.6 = (bf16[16,2432]{1,0:T(8,128)(2,1)S(1)}, bf16[16,2432]{1,0:T(8,128)(2,1)S(1)}, u32[]{:S(2)}, u32[]{:S(2)}) collective-permute-start(bf16[16,2432]{1,0:T(8,128)(2,1)S(1)} %collective-permute-done), channel_id=1, source_target_pairs={{0,6},{2,4},{4,2},{6,0},{8,14},{10,12},{12,10},{14,8},{1,7},{3,5},... | collective-permute-start | bytes 233480 | tf_op jit(solution)/shard_map/ppermute | solution.py:245
  16.3 4.4 %collective-permute-start.2 = (bf16[16,2432]{1,0:T(8,128)(2,1)S(1)}, bf16[16,2432]{1,0:T(8,128)(2,1)S(1)}, u32[]{:S(2)}, u32[]{:S(2)}) collective-permute-start(bf16[16,2432]{1,0:T(8,128)(2,1)S(1)} %collective-permute-done), channel_id=1, source_target_pairs={{0,2},{2,0},{4,6},{6,4},{8,10},{10,8},{12,14},{14,12},{1,3},{3,1},... | collective-permute-start | bytes 233480 | tf_op jit(solution)/shard_map/ppermute | solution.py:245
  25.9 5.1 %collective-permute-start.7 = (bf16[16,2432]{1,0:T(8,128)(2,1)}, bf16[16,2432]{1,0:T(8,128)(2,1)S(1)}, u32[]{:S(2)}, u32[]{:S(2)}) collective-permute-start(bf16[16,2432]{1,0:T(8,128)(2,1)} %get-tuple-element.22), channel_id=1, source_target_pairs={{0,2},{2,0},{4,6},{6,4},{8,10},{10,8},{12,14},{14,12},{1,3},{3,1},... | collective-permute-start | bytes 233480 | tf_op jit(solution)/shard_map/ppermute | solution.py:245
  26.0 5.0 %collective-permute-start.8 = (bf16[16,2432]{1,0:T(8,128)(2,1)}, bf16[16,2432]{1,0:T(8,128)(2,1)S(1)}, u32[]{:S(2)}, u32[]{:S(2)}) collective-permute-start(bf16[16,2432]{1,0:T(8,128)(2,1)} %get-tuple-element.23), channel_id=1, source_target_pairs={{0,4},{2,6},{4,0},{6,2},{8,12},{10,14},{12,8},{14,10},{1,5},{3,7},... | collective-permute-start | bytes 233480 | tf_op jit(solution)/shard_map/ppermute | solution.py:245
  27.4 5.5 %collective-permute-start.9 = (bf16[16,2432]{1,0:T(8,128)(2,1)}, bf16[16,2432]{1,0:T(8,128)(2,1)S(1)}, u32[]{:S(2)}, u32[]{:S(2)}) collective-permute-start(bf16[16,2432]{1,0:T(8,128)(2,1)} %get-tuple-element.24), channel_id=1, source_target_pairs={{0,6},{2,4},{4,2},{6,0},{8,14},{10,12},{12,10},{14,8},{1,7},{3,5},... | collective-permute-start | bytes 233480 | tf_op jit(solution)/shard_map/ppermute | solution.py:245
  29.4 12.5 %collective-permute-start.11 = (bf16[144,1600]{1,0:T(8,128)(2,1)}, bf16[144,1600]{1,0:T(8,128)(2,1)S(1)}, u32[]{:S(2)}, u32[]{:S(2)}) collective-permute-start(bf16[144,1600]{1,0:T(8,128)(2,1)} %get-tuple-element.29), channel_id=1, source_target_pairs={{0,1},{1,0},{2,3},{3,2},{4,5},{5,4},{6,7},{7,6},{8,9},{9,8},{10,11... | collective-permute-start | bytes 1382408 | tf_op jit(solution)/shard_map/ppermute | solution.py:293
  31.1 2.6 %copy-start = (bf16[16,2432]{1,0:T(8,128)(2,1)}, bf16[16,2432]{1,0:T(8,128)(2,1)S(1)}, u32[]{:S(2)}) copy-start(bf16[16,2432]{1,0:T(8,128)(2,1)S(1)} %collective-permute-done.7.o1) | copy-start | bytes 233476
  31.1 2.7 %copy-start.1 = (bf16[16,2432]{1,0:T(8,128)(2,1)}, bf16[16,2432]{1,0:T(8,128)(2,1)S(1)}, u32[]{:S(2)}) copy-start(bf16[16,2432]{1,0:T(8,128)(2,1)S(1)} %collective-permute-done.8.o2) | copy-start | bytes 233476
  32.9 6.1 %copy-start.2 = (bf16[16,2432]{1,0:T(8,128)(2,1)}, bf16[16,2432]{1,0:T(8,128)(2,1)S(1)}, u32[]{:S(2)}) copy-start(bf16[16,2432]{1,0:T(8,128)(2,1)S(1)} %collective-permute-done.9.o3) | copy-start | bytes 233476
  33.7 5.3 %collective-permute-start.10 = (bf16[8,2432]{1,0:T(8,128)(2,1)S(1)}, bf16[8,2432]{1,0:T(8,128)(2,1)S(1)}, u32[]{:S(2)}, u32[]{:S(2)}) collective-permute-start(bf16[8,2432]{1,0:T(8,128)(2,1)S(1)} %add_convert_fusion), channel_id=1, source_target_pairs={{0,8},{2,10},{4,12},{6,14},{8,0},{10,2},{12,4},{14,6},{1,9},{3,11}... | collective-permute-start | bytes 116744 | tf_op jit(solution)/shard_map/ppermute | solution.py:245
  39.0 0.6 %copy-start.3 = (bf16[8,2432]{1,0:T(8,128)(2,1)}, bf16[8,2432]{1,0:T(8,128)(2,1)S(1)}, u32[]{:S(2)}) copy-start(bf16[8,2432]{1,0:T(8,128)(2,1)S(1)} %collective-permute-done.10.rest_0_) | copy-start | bytes 116740
  41.9 0.8 %copy-start.4 = (bf16[144,1600]{1,0:T(8,128)(2,1)}, bf16[144,1600]{1,0:T(8,128)(2,1)S(1)}, u32[]{:S(2)}) copy-start(bf16[144,1600]{1,0:T(8,128)(2,1)S(1)} %collective-permute-done.11.peer_ref) | copy-start | bytes 1382404

commit v2 on v1

--- a/solution.py
+++ b/solution.py
@@ -9,7 +9,8 @@
 MAIN = 8
 TILE = 128
 GROUP = 8
-VMEM_LIMIT = 60 * 1024 * 1024
+MIB = 1024 * 1024
+VMEM_LIMIT = 60 * MIB
 F32 = jnp.float32
 BF16 = jnp.bfloat16
 
@@ -35,9 +36,20 @@
     return [rank[i : i + 1] for i in range(count)]
 
 
-def pack_kernel(where_ref, picks_ref, gates_ref, tok_ref, grad_ref, *outs):
+def pack_kernel(picks_hbm, gates_hbm, tok_hbm, grad_hbm, *refs):
+    outs, (picks_ref, gates_ref, tok_ref, grad_ref, sems) = refs[:-5], refs[-5:]
+    loads = [
+        pltpu.make_async_copy(src, dst, sems.at[i])
+        for i, (src, dst) in enumerate(
+            [(picks_hbm, picks_ref), (gates_hbm, gates_ref), (tok_hbm, tok_ref), (grad_hbm, grad_ref)]
+        )
+    ]
+    for load in loads:
+        load.start()
     window = len(outs)
-    quad = where_ref[0]
+    loads[0].wait()
+    loads[1].wait()
+    quad = lax.axis_index("expert") // SPLIT
     picks = picks_ref[...]
     gates = gates_ref[...].astype(F32)
     features = tok_ref.shape[1]
@@ -52,7 +64,9 @@
     if pad:
         last = jnp.concatenate([last, jnp.zeros((pad, toks), F32)], axis=0)
     choose = jnp.concatenate(mains + [last], axis=0).astype(BF16)
+    loads[2].wait()
     tok_rows = dot(choose, tok_ref[...], (1, 0))
+    loads[3].wait()
     grad_rows = dot(choose, grad_ref[...], (1, 0))
     row = iota((MAIN, fold), 0)
     lane = iota((MAIN, TILE), 1)
@@ -74,19 +88,31 @@
         out[:, features + fold :] = jnp.concatenate([tile, tile], axis=0).astype(BF16)
 
 
-def expert_kernel(
-    where_ref, z0, z1, z2, z3, wg_ref, wu_ref, wd_ref, m0, m1, m2, m3, keep_ref, hid_ref, send_ref
-):
+def fetch_kernel(gate_hbm, up_hbm, down_hbm, *refs):
+    outs, sems = refs[-4:-1], refs[-1]
+    loads = [
+        pltpu.make_async_copy(src, dst, sems.at[i])
+        for i, (src, dst) in enumerate(zip((gate_hbm, up_hbm, down_hbm), outs))
+    ]
+    for load in loads:
+        load.start()
+    for load in loads:
+        load.wait()
+
+
+def expert_kernel(*refs):
+    wg_ref, wu_ref, wd_ref, m0, m1, m2, m3, keep_ref, hid_ref, send_ref = refs[-10:]
+    zs, ms = refs[:-10], (m0, m1, m2, m3)
     features = wg_ref.shape[1]
     hidden = wg_ref.shape[0]
     fold = features // MAIN
     half = features // 2
-    core = where_ref[1]
-    zs, ms = (z0, z1, z2, z3), (m0, m1, m2, m3)
+    core = lax.axis_index("dp")
     pair = 2 * MAIN
     per = GROUP // SPLIT
-    rows_in = per * pair
-    groups = z0.shape[0] // rows_in
+    held = GROUP // len(zs)
+    rows_in = held * pair
+    groups = zs[0].shape[0] // rows_in
 
     def work(g):
         if groups == 1:
@@ -117,7 +143,7 @@
         last = jnp.zeros((MAIN, 1), F32)
         seat = iota((MAIN, 1), 0)
         for p in range(GROUP):
-            tile = tiles[p // per][(p % per) * pair : (p % per) * pair + MAIN]
+            tile = tiles[p // held][(p % held) * pair : (p % held) * pair + MAIN]
             columns.append(tile[:, 0:1])
             last = jnp.where(seat == p, tile[:, 1:2], last)
         gate = jnp.concatenate(columns + [last], axis=0)
@@ -188,10 +214,10 @@
         out[...] = total.astype(BF16)
 
 
-def finish_kernel(where_ref, picks_ref, o0, o1, o2, o3, *rest):
+def finish_kernel(picks_ref, o0, o1, o2, o3, *rest):
     far, (grad_ref, comb_ref) = rest[:-2], rest[-2:]
     window = 1 + len(far)
-    quad = where_ref[0]
+    quad = lax.axis_index("expert") // SPLIT
     picks = picks_ref[...]
     experts = [quad ^ k for k in range(window)]
     ranks = places(picks, experts)
@@ -225,19 +251,26 @@
 
 
 VM = pl.BlockSpec(memory_space=pltpu.VMEM)
-SM = pl.BlockSpec(memory_space=pltpu.SMEM)
-
-
-def call(kernel, outs, name, in_specs, flops, nbytes):
+HBM = pl.BlockSpec(memory_space=pltpu.HBM)
+ANY = pl.BlockSpec(memory_space=pl.ANY)
+
+
+def call(kernel, outs, name, args, flops, nbytes, room, specs=None, scratch=()):
+    specs = specs or [VM] * len(args)
+    args = [
+        pltpu.with_memory_space_constraint(a, pltpu.HBM) if s is HBM else a
+        for a, s in zip(args, specs)
+    ]
     return pl.pallas_call(
         kernel,
         out_shape=[jax.ShapeDtypeStruct(s, t) for s, t in outs],
-        in_specs=in_specs,
+        in_specs=specs,
         out_specs=[VM] * len(outs),
-        compiler_params=pltpu.CompilerParams(vmem_limit_bytes=VMEM_LIMIT),
+        scratch_shapes=list(scratch),
+        compiler_params=pltpu.CompilerParams(vmem_limit_bytes=min(VMEM_LIMIT, room * MIB)),
         cost_estimate=pl.CostEstimate(flops=flops, bytes_accessed=nbytes, transcendentals=0),
         name=name,
-    )
+    )(*args)
 
 
 def swap_by(block, mask):
@@ -247,66 +280,88 @@
 
 def body(tokens, out_grad, choices, gates, gate_weight, up_weight, down_weight):
     members = lax.axis_size("expert")
-    position = lax.axis_index("expert")
-    core = lax.axis_index("dp")
     toks, features = tokens.shape
     hidden = gate_weight.shape[2]
     window = members // SPLIT
     fold = features // MAIN
     half = features // 2
     width = features + fold + TILE
-    where = jnp.stack([position // SPLIT, core]).astype(jnp.int32)
     picks, gates_t = choices.T, gates.T
     wg, wu, wd = gate_weight[0].T, up_weight[0].T, down_weight[0]
+    groups = members // GROUP
 
     packed = call(
         pack_kernel,
         [((2 * MAIN, width), BF16)] * window,
         "pack",
-        [SM, VM, VM, VM, VM],
+        (picks, gates_t, tokens, out_grad),
         2 * (MAIN + 1) * window * toks * features * 2,
         4 * toks * features,
-    )(where, picks, gates_t, tokens, out_grad)
+        6 + window,
+        [HBM] * 4,
+        [pltpu.VMEM(v.shape, v.dtype) for v in (picks, gates_t, tokens, out_grad)]
+        + [pltpu.SemaphoreType.DMA((4,))],
+    )
     own, others = packed[0], packed[1:]
     arrived = [swap_by(o, SPLIT * (k + 1)) for k, o in enumerate(others)]
     near = [own] + [swap_by(own, j) for j in range(1, SPLIT)]
+    held = call(
+        fetch_kernel,
+        [(w.shape, BF16) for w in (wg, wu, wd)],
+        "fetch",
+        (wg, wu, wd, *near[1:]),
+        0,
+        6 * features * hidden,
+        4,
+        [HBM] * 3 + [ANY] * (SPLIT - 1),
+        [pltpu.SemaphoreType.DMA((3,))],
+    )
     from_far = arrived[0] if window == 2 else jnp.concatenate(arrived, axis=0)
     far = [from_far] + [swap_by(from_far, j) for j in range(1, SPLIT)]
-    zs = [jnp.concatenate([a, b], axis=0) for a, b in zip(near, far)]
-
-    groups = members // GROUP
+    pairs = list(zip(near, far))
+    if groups == 1:
+        zs = [z for pair in pairs for z in pair]
+    else:
+        zs = [jnp.concatenate(pair, axis=0) for pair in pairs]
+
     all_rows = groups * (GROUP + 1) * 2 * MAIN
     *messages, keep, hid, send = call(
         expert_kernel,
         [((window * MAIN, width), BF16)] * SPLIT
         + [((all_rows, half), BF16), ((all_rows, 3 * hidden), BF16), ((all_rows, half + 3 * hidden), BF16)],
         "expert",
-        [SM] + [VM] * 7,
+        (*zs, *held),
         2 * all_rows * features * hidden * 5,
         6 * features * hidden,
-    )(where, *zs, wg, wu, wd)
+        10 + 6 * groups,
+    )
     back = [messages[0]] + [swap_by(messages[j], j) for j in range(1, SPLIT)]
-    total = sum(b[MAIN:].astype(F32) for b in back).astype(BF16)
-    homes = [
-        swap_by(total[k * MAIN : (k + 1) * MAIN], SPLIT * (k + 1)) for k in range(window - 1)
-    ]
     peer = lax.ppermute(send, "dp", [(0, 1), (1, 0)])
     gate_grad, up_grad, down_grad = call(
         weights_kernel,
         [((hidden, half), BF16)] * 3,
         "weights",
-        [VM] * 3,
+        (keep, hid, peer),
         2 * 2 * all_rows * half * hidden * 3,
         6 * half * hidden,
-    )(keep, hid, peer)
+        6 + 2 * groups,
+    )
+    *back, gate_grad, up_grad, down_grad = lax.optimization_barrier(
+        (*back, gate_grad, up_grad, down_grad)
+    )
+    total = sum(b[MAIN:].astype(F32) for b in back).astype(BF16)
+    homes = [
+        swap_by(total[k * MAIN : (k + 1) * MAIN], SPLIT * (k + 1)) for k in range(window - 1)
+    ]
     in_grad, combine = call(
         finish_kernel,
         [((toks, features), BF16), ((choices.shape[1], toks), F32)],
         "finish",
-        [SM] + [VM] * (SPLIT + window),
+        (picks, *back, *homes),
         2 * toks * features * 16 * (SPLIT + window),
         2 * toks * features,
-    )(where, picks, *back, *homes)
+        6 + window,
+    )
     return (
         in_grad,
         combine.T,

time: 45.9 us -> 33.5 us (0.73)
  other arithmetic: 5.07 us -> 0.02 us
  Pallas kernels: 11.9 us -> 7.77 us
  waiting for transfers between devices: 8.62 us -> 6.74 us
  local copies, waits for them, and re-layouts: 1.38 us -> 0.01 us
    pallas_call x4 -> x5, Pallas kernels: 11.9 us -> 7.77 us  [call(): pl.pallas_call(kernel, out_shape=[jax.ShapeDtypeStruct(s, t) for s, t in...]
    concatenate x4 -> x0, other arithmetic: 3.6 us -> none  [body(): zs = [jnp.concatenate([a, b], axis=0) for a, b in zip(near, far)]]
    ppermute x11, waiting for transfers between devices: 8.62 us -> 6.74 us  [swap_by(): return lax.ppermute(block, 'expert', [(i, i ^ mask) for i in range(count)])]
    unnamed x10 -> x2, local copies, waits for them, and re-layouts: 1.38 us -> 0.01 us
    convert_element_type x1, other arithmetic: 0.8 us -> 0.02 us  [body(): total = sum((b[MAIN:].astype(F32) for b in back)).astype(BF16)]
    another operation x1 -> x0, other arithmetic: 0.67 us -> none  [body(): where = jnp.stack([position // SPLIT, core]).astype(jnp.int32)]
  transfers between devices with their start and end apart: 12 -> 12, of which waited for: 6 -> 7; matrix products, arithmetic and copies ran while one was open for 8% -> 0% of each run, Pallas kernels for 5% -> 10%
where the time goes in v2:
time: 33.5 us; the launch traced here: 33.3 us
  starting transfers between devices  18.1 us (54%)
  Pallas kernels  7.77 us (23%)
  waiting for transfers between devices  6.74 us (20%)
  between operations  0.69 us (2%)
    ppermute x11, starting transfers between devices, swap_by(): return lax.ppermute(block, 'expert', [(i, i ^ mask) for i in range(count)])  18 us
    pallas_call x5, Pallas kernels, call(): pl.pallas_call(kernel, out_shape=[jax.ShapeDtypeStruct(s, t) for s, t in...  7.77 us
    ppermute x11, waiting for transfers between devices, swap_by(): return lax.ppermute(block, 'expert', [(i, i ^ mask) for i in range(count)])  6.74 us
  transfers between devices with their start and end apart: 12, of which 7 were waited for; matrix products, arithmetic and copies ran while one was open for 0% of the time, Pallas kernels for 10%

profile of v2, /device:TPU:0, one launch (start us, length us, event | category | flops | bytes accessed | tf_op | source)
XLA Modules:
  0.0 33.3 jit_solution(11570412237061907911)
XLA Ops:
  0.6 1.5 %pack.1 = (bf16[16,2432]{1,0:T(8,128)(2,1)S(1)}, bf16[16,2432]{1,0:T(8,128)(2,1)S(1)}) custom-call(s32[8,128]{1,0:T(8,128)} %bitcast.17, bf16[8,128]{1,0:T(8,128)(2,1)} %bitcast.22, bf16[128,2048]{1,0:T(8,128)(2,1)} %tok_hbm.1, bf16[128,2048]{1,0:T(8,128)(2,1)} %grad_hbm.1), custom_call_target="tpu_custom_call" | custom-call | flops 18874368 | bytes 1048576 | tf_op jit(solution)/shard_map/pack/pallas_call | solution.py:264
  2.2 4.1 %collective-permute-start = (bf16[16,2432]{1,0:T(8,128)(2,1)S(1)}, bf16[16,2432]{1,0:T(8,128)(2,1)S(1)}, u32[]{:S(2)}, u32[]{:S(2)}) collective-permute-start(bf16[16,2432]{1,0:T(8,128)(2,1)S(1)} %get-tuple-element.30), channel_id=1, source_target_pairs={{0,8},{2,10},{4,12},{6,14},{8,0},{10,2},{12,4},{14,6},{1,9},{3,11}... | collective-permute-start | bytes 233480 | tf_op jit(solution)/shard_map/ppermute | solution.py:278
  6.3 2.5 %collective-permute-start.5 = (bf16[16,2432]{1,0:T(8,128)(2,1)S(1)}, bf16[16,2432]{1,0:T(8,128)(2,1)S(1)}, u32[]{:S(2)}, u32[]{:S(2)}) collective-permute-start(bf16[16,2432]{1,0:T(8,128)(2,1)S(1)} %get-tuple-element.29.refs_0_), channel_id=1, source_target_pairs={{0,6},{2,4},{4,2},{6,0},{8,14},{10,12},{12,10},{14,8},{1,7},{3,5},... | collective-permute-start | bytes 233480 | tf_op jit(solution)/shard_map/ppermute | solution.py:278
  8.8 0.4 %collective-permute-start.3 = (bf16[16,2432]{1,0:T(8,128)(2,1)S(1)}, bf16[16,2432]{1,0:T(8,128)(2,1)S(1)}, u32[]{:S(2)}, u32[]{:S(2)}) collective-permute-start(bf16[16,2432]{1,0:T(8,128)(2,1)S(1)} %get-tuple-element.29.refs_0_), channel_id=1, source_target_pairs={{0,4},{2,6},{4,0},{6,2},{8,12},{10,14},{12,8},{14,10},{1,5},{3,7},... | collective-permute-start | bytes 233480 | tf_op jit(solution)/shard_map/ppermute | solution.py:278
  9.2 0.5 %collective-permute-start.1 = (bf16[16,2432]{1,0:T(8,128)(2,1)S(1)}, bf16[16,2432]{1,0:T(8,128)(2,1)S(1)}, u32[]{:S(2)}, u32[]{:S(2)}) collective-permute-start(bf16[16,2432]{1,0:T(8,128)(2,1)S(1)} %get-tuple-element.29.refs_0_), channel_id=1, source_target_pairs={{0,2},{2,0},{4,6},{6,4},{8,10},{10,8},{12,14},{14,12},{1,3},{3,1},... | collective-permute-start | bytes 233480 | tf_op jit(solution)/shard_map/ppermute | solution.py:278
  9.8 0.0 collective-permute-done.refs_1_
  9.8 2.5 %collective-permute-start.6 = (bf16[16,2432]{1,0:T(8,128)(2,1)S(1)}, bf16[16,2432]{1,0:T(8,128)(2,1)S(1)}, u32[]{:S(2)}, u32[]{:S(2)}) collective-permute-start(bf16[16,2432]{1,0:T(8,128)(2,1)S(1)} %collective-permute-done.refs_1_), channel_id=1, source_target_pairs={{0,6},{2,4},{4,2},{6,0},{8,14},{10,12},{12,10},{14,8},{1,7},{3,5},... | collective-permute-start | bytes 233480 | tf_op jit(solution)/shard_map/ppermute | solution.py:278
  12.3 0.8 %collective-permute-start.4 = (bf16[16,2432]{1,0:T(8,128)(2,1)S(1)}, bf16[16,2432]{1,0:T(8,128)(2,1)S(1)}, u32[]{:S(2)}, u32[]{:S(2)}) collective-permute-start(bf16[16,2432]{1,0:T(8,128)(2,1)S(1)} %collective-permute-done.refs_1_), channel_id=1, source_target_pairs={{0,4},{2,6},{4,0},{6,2},{8,12},{10,14},{12,8},{14,10},{1,5},{3,7},... | collective-permute-start | bytes 233480 | tf_op jit(solution)/shard_map/ppermute | solution.py:278
  13.2 0.0 collective-permute-done.5.refs_2_.refs_6_
  13.2 0.7 %collective-permute-start.2 = (bf16[16,2432]{1,0:T(8,128)(2,1)S(1)}, bf16[16,2432]{1,0:T(8,128)(2,1)S(1)}, u32[]{:S(2)}, u32[]{:S(2)}) collective-permute-start(bf16[16,2432]{1,0:T(8,128)(2,1)S(1)} %collective-permute-done.refs_1_), channel_id=1, source_target_pairs={{0,2},{2,0},{4,6},{6,4},{8,10},{10,8},{12,14},{14,12},{1,3},{3,1},... | collective-permute-start | bytes 233480 | tf_op jit(solution)/shard_map/ppermute | solution.py:278
  13.9 0.1 collective-permute-done.3.refs_1_.refs_4_
  14.0 0.9 %collective-permute-done.1.refs_0_.refs_2_ = bf16[16,2432]{1,0:T(8,128)(2,1)S(1)} collective-permute-done((bf16[16,2432]{1,0:T(8,128)(2,1)S(1)}, bf16[16,2432]{1,0:T(8,128)(2,1)S(1)}, u32[]{:S(2)}, u32[]{:S(2)}) %collective-permute-start.1) | collective-permute-done | bytes 77856 | tf_op jit(solution)/shard_map/ppermute | solution.py:278
  14.9 1.6 %fetch.1 = (bf16[192,2048]{1,0:T(8,128)(2,1)S(1)}, bf16[192,2048]{1,0:T(8,128)(2,1)S(1)}, bf16[192,2048]{1,0:T(8,128)(2,1)S(1)}) custom-call(bf16[192,2048]{1,0:T(8,128)(2,1)} %bitcast.19, bf16[192,2048]{1,0:T(8,128)(2,1)} %bitcast.20, bf16[192,2048]{1,0:T(8,128)(2,1)} %bitcast.21, bf16[16,2432]{1,0:T(8,128)(2,1)S(1)} %collective-permute-done.1.refs_0_.refs_2_, ...), custom_call_target="tpu_custom_call" | custom-call | bytes 2359296 | tf_op jit(solution)/shard_map/fetch/pallas_call | solution.py:264
  16.5 0.0 collective-permute-done.6.refs_7_
  16.5 0.2 collective-permute-done.4.refs_5_
  16.7 0.8 %collective-permute-done.2.refs_3_ = bf16[16,2432]{1,0:T(8,128)(2,1)S(1)} collective-permute-done((bf16[16,2432]{1,0:T(8,128)(2,1)S(1)}, bf16[16,2432]{1,0:T(8,128)(2,1)S(1)}, u32[]{:S(2)}, u32[]{:S(2)}) %collective-permute-start.2) | collective-permute-done | bytes 77856 | tf_op jit(solution)/shard_map/ppermute | solution.py:278
  17.6 1.8 %expert.1 = (bf16[16,2432]{1,0:T(8,128)(2,1)S(1)}, bf16[16,2432]{1,0:T(8,128)(2,1)S(1)}, bf16[16,2432]{1,0:T(8,128)(2,1)S(1)}, bf16[16,2432]{1,0:T(8,128)(2,1)S(...) custom-call(bf16[16,2432]{1,0:T(8,128)(2,1)S(1)} %get-tuple-element.29.refs_0_, ...), custom_call_target="tpu_custom_call" | custom-call | flops 566231040 | bytes 2359296 | tf_op jit(solution)/shard_map/expert/pallas_call | solution.py:264
  19.3 0.1 collective-permute-start.10
  19.4 0.8 %collective-permute-start.7 = (bf16[16,2432]{1,0:T(8,128)(2,1)S(1)}, bf16[16,2432]{1,0:T(8,128)(2,1)S(1)}, u32[]{:S(2)}, u32[]{:S(2)}) collective-permute-start(bf16[16,2432]{1,0:T(8,128)(2,1)S(1)} %get-tuple-element.35), channel_id=1, source_target_pairs={{0,2},{2,0},{4,6},{6,4},{8,10},{10,8},{12,14},{14,12},{1,3},{3,1},... | collective-permute-start | bytes 233480 | tf_op jit(solution)/shard_map/ppermute | solution.py:278
  20.2 1.0 %collective-permute-start.8 = (bf16[16,2432]{1,0:T(8,128)(2,1)S(1)}, bf16[16,2432]{1,0:T(8,128)(2,1)S(1)}, u32[]{:S(2)}, u32[]{:S(2)}) collective-permute-start(bf16[16,2432]{1,0:T(8,128)(2,1)S(1)} %get-tuple-element.36), channel_id=1, source_target_pairs={{0,4},{2,6},{4,0},{6,2},{8,12},{10,14},{12,8},{14,10},{1,5},{3,7},... | collective-permute-start | bytes 233480 | tf_op jit(solution)/shard_map/ppermute | solution.py:278
  21.2 1.8 %collective-permute-start.9 = (bf16[16,2432]{1,0:T(8,128)(2,1)S(1)}, bf16[16,2432]{1,0:T(8,128)(2,1)S(1)}, u32[]{:S(2)}, u32[]{:S(2)}) collective-permute-start(bf16[16,2432]{1,0:T(8,128)(2,1)S(1)} %get-tuple-element.37), channel_id=1, source_target_pairs={{0,6},{2,4},{4,2},{6,0},{8,14},{10,12},{12,10},{14,8},{1,7},{3,5},... | collective-permute-start | bytes 233480 | tf_op jit(solution)/shard_map/ppermute | solution.py:278
  23.0 0.0 collective-permute-done.10.peer_ref
  23.0 1.6 %weights.1 = (bf16[192,1024]{1,0:T(8,128)(2,1)}, bf16[192,1024]{1,0:T(8,128)(2,1)}, bf16[192,1024]{1,0:T(8,128)(2,1)}) custom-call(bf16[144,1024]{1,0:T(8,128)(2,1)S(1)} %get-tuple-element.38.keep_ref, bf16[144,576]{1,0:T(8,128)(2,1)S(1)} %get-tuple-element.39.hid_ref, bf16[144,1600]{1,0:T(8,128)(2,1)S(1)} %collective-permute-done.10.peer_ref), custom_call_target="tpu_custom_call" | custom-call | flops 339738624 | bytes 1179648 | tf_op jit(solution)/shard_map/weights/pallas_call | solution.py:264
  24.6 0.0 collective-permute-done.7.o1
  24.6 0.1 collective-permute-done.8.o2
  24.7 2.4 %collective-permute-done.9.o3 = bf16[16,2432]{1,0:T(8,128)(2,1)S(1)} collective-permute-done((bf16[16,2432]{1,0:T(8,128)(2,1)S(1)}, bf16[16,2432]{1,0:T(8,128)(2,1)S(1)}, u32[]{:S(2)}, u32[]{:S(2)}) %collective-permute-start.9) | collective-permute-done | bytes 77856 | tf_op jit(solution)/shard_map/ppermute | solution.py:278
  27.0 0.0 copy-start
  27.1 2.7 %collective-permute-start.11 = (bf16[8,2432]{1,0:T(8,128)(2,1)S(1)}, bf16[8,2432]{1,0:T(8,128)(2,1)S(1)}, u32[]{:S(2)}, u32[]{:S(2)}) collective-permute-start(bf16[8,2432]{1,0:T(8,128)(2,1)S(1)} %add_convert_fusion), channel_id=1, source_target_pairs={{0,8},{2,10},{4,12},{6,14},{8,0},{10,2},{12,4},{14,6},{1,9},{3,11}... | collective-permute-start | bytes 116744 | tf_op jit(solution)/shard_map/ppermute | solution.py:278
  29.8 2.2 %collective-permute-done.11.rest_0_ = bf16[8,2432]{1,0:T(8,128)(2,1)S(1)} collective-permute-done((bf16[8,2432]{1,0:T(8,128)(2,1)S(1)}, bf16[8,2432]{1,0:T(8,128)(2,1)S(1)}, u32[]{:S(2)}, u32[]{:S(2)}) %collective-permute-start.11) | collective-permute-done | bytes 38944 | tf_op jit(solution)/shard_map/ppermute | solution.py:278
  32.0 0.0 copy-done
  32.0 1.3 %finish.1 = (bf16[128,2048]{1,0:T(8,128)(2,1)}, f32[8,128]{1,0:T(8,128)}) custom-call(s32[8,128]{1,0:T(8,128)S(1)} %bitcast.18, bf16[16,2432]{1,0:T(8,128)(2,1)S(1)} %get-tuple-element.44.o0, bf16[16,2432]{1,0:T(8,128)(2,1)S(1)} %collective-permute-done.7.o1, bf16[16,2432]{1,0:T(8,128)(2,1)S(1)} %collective-permute-done.8.o2, ...), custom_call_target="tpu_custom_call" | custom-call | flops 50331648 | bytes 524288 | tf_op jit(solution)/shard_map/finish/pallas_call | solution.py:264
  (1 shorter events, 0.0 us)
Async XLA Ops:
  2.2 7.6 %collective-permute-start = (bf16[16,2432]{1,0:T(8,128)(2,1)S(1)}, bf16[16,2432]{1,0:T(8,128)(2,1)S(1)}, u32[]{:S(2)}, u32[]{:S(2)}) collective-permute-start(bf16[16,2432]{1,0:T(8,128)(2,1)S(1)} %get-tuple-element.30), channel_id=1, source_target_pairs={{0,8},{2,10},{4,12},{6,14},{8,0},{10,2},{12,4},{14,6},{1,9},{3,11}... | collective-permute-start | bytes 233480 | tf_op jit(solution)/shard_map/ppermute | solution.py:278
  6.3 6.9 %collective-permute-start.5 = (bf16[16,2432]{1,0:T(8,128)(2,1)S(1)}, bf16[16,2432]{1,0:T(8,128)(2,1)S(1)}, u32[]{:S(2)}, u32[]{:S(2)}) collective-permute-start(bf16[16,2432]{1,0:T(8,128)(2,1)S(1)} %get-tuple-element.29.refs_0_), channel_id=1, source_target_pairs={{0,6},{2,4},{4,2},{6,0},{8,14},{10,12},{12,10},{14,8},{1,7},{3,5},... | collective-permute-start | bytes 233480 | tf_op jit(solution)/shard_map/ppermute | solution.py:278
  8.8 5.2 %collective-permute-start.3 = (bf16[16,2432]{1,0:T(8,128)(2,1)S(1)}, bf16[16,2432]{1,0:T(8,128)(2,1)S(1)}, u32[]{:S(2)}, u32[]{:S(2)}) collective-permute-start(bf16[16,2432]{1,0:T(8,128)(2,1)S(1)} %get-tuple-element.29.refs_0_), channel_id=1, source_target_pairs={{0,4},{2,6},{4,0},{6,2},{8,12},{10,14},{12,8},{14,10},{1,5},{3,7},... | collective-permute-start | bytes 233480 | tf_op jit(solution)/shard_map/ppermute | solution.py:278
  9.2 5.7 %collective-permute-start.1 = (bf16[16,2432]{1,0:T(8,128)(2,1)S(1)}, bf16[16,2432]{1,0:T(8,128)(2,1)S(1)}, u32[]{:S(2)}, u32[]{:S(2)}) collective-permute-start(bf16[16,2432]{1,0:T(8,128)(2,1)S(1)} %get-tuple-element.29.refs_0_), channel_id=1, source_target_pairs={{0,2},{2,0},{4,6},{6,4},{8,10},{10,8},{12,14},{14,12},{1,3},{3,1},... | collective-permute-start | bytes 233480 | tf_op jit(solution)/shard_map/ppermute | solution.py:278
  9.8 6.7 %collective-permute-start.6 = (bf16[16,2432]{1,0:T(8,128)(2,1)S(1)}, bf16[16,2432]{1,0:T(8,128)(2,1)S(1)}, u32[]{:S(2)}, u32[]{:S(2)}) collective-permute-start(bf16[16,2432]{1,0:T(8,128)(2,1)S(1)} %collective-permute-done.refs_1_), channel_id=1, source_target_pairs={{0,6},{2,4},{4,2},{6,0},{8,14},{10,12},{12,10},{14,8},{1,7},{3,5},... | collective-permute-start | bytes 233480 | tf_op jit(solution)/shard_map/ppermute | solution.py:278
  12.3 4.4 %collective-permute-start.4 = (bf16[16,2432]{1,0:T(8,128)(2,1)S(1)}, bf16[16,2432]{1,0:T(8,128)(2,1)S(1)}, u32[]{:S(2)}, u32[]{:S(2)}) collective-permute-start(bf16[16,2432]{1,0:T(8,128)(2,1)S(1)} %collective-permute-done.refs_1_), channel_id=1, source_target_pairs={{0,4},{2,6},{4,0},{6,2},{8,12},{10,14},{12,8},{14,10},{1,5},{3,7},... | collective-permute-start | bytes 233480 | tf_op jit(solution)/shard_map/ppermute | solution.py:278
  13.2 4.4 %collective-permute-start.2 = (bf16[16,2432]{1,0:T(8,128)(2,1)S(1)}, bf16[16,2432]{1,0:T(8,128)(2,1)S(1)}, u32[]{:S(2)}, u32[]{:S(2)}) collective-permute-start(bf16[16,2432]{1,0:T(8,128)(2,1)S(1)} %collective-permute-done.refs_1_), channel_id=1, source_target_pairs={{0,2},{2,0},{4,6},{6,4},{8,10},{10,8},{12,14},{14,12},{1,3},{3,1},... | collective-permute-start | bytes 233480 | tf_op jit(solution)/shard_map/ppermute | solution.py:278
  19.3 3.6 %collective-permute-start.10 = (bf16[144,1600]{1,0:T(8,128)(2,1)S(1)}, bf16[144,1600]{1,0:T(8,128)(2,1)S(1)}, u32[]{:S(2)}, u32[]{:S(2)}) collective-permute-start(bf16[144,1600]{1,0:T(8,128)(2,1)S(1)} %get-tuple-element.40), channel_id=1, source_target_pairs={{0,1},{1,0},{2,3},{3,2},{4,5},{5,4},{6,7},{7,6},{8,9},{9,8},{10,11... | collective-permute-start | bytes 1382408 | tf_op jit(solution)/shard_map/ppermute | solution.py:339
  19.4 5.1 %collective-permute-start.7 = (bf16[16,2432]{1,0:T(8,128)(2,1)S(1)}, bf16[16,2432]{1,0:T(8,128)(2,1)S(1)}, u32[]{:S(2)}, u32[]{:S(2)}) collective-permute-start(bf16[16,2432]{1,0:T(8,128)(2,1)S(1)} %get-tuple-element.35), channel_id=1, source_target_pairs={{0,2},{2,0},{4,6},{6,4},{8,10},{10,8},{12,14},{14,12},{1,3},{3,1},... | collective-permute-start | bytes 233480 | tf_op jit(solution)/shard_map/ppermute | solution.py:278
  20.2 4.5 %collective-permute-start.8 = (bf16[16,2432]{1,0:T(8,128)(2,1)S(1)}, bf16[16,2432]{1,0:T(8,128)(2,1)S(1)}, u32[]{:S(2)}, u32[]{:S(2)}) collective-permute-start(bf16[16,2432]{1,0:T(8,128)(2,1)S(1)} %get-tuple-element.36), channel_id=1, source_target_pairs={{0,4},{2,6},{4,0},{6,2},{8,12},{10,14},{12,8},{14,10},{1,5},{3,7},... | collective-permute-start | bytes 233480 | tf_op jit(solution)/shard_map/ppermute | solution.py:278
  21.2 5.9 %collective-permute-start.9 = (bf16[16,2432]{1,0:T(8,128)(2,1)S(1)}, bf16[16,2432]{1,0:T(8,128)(2,1)S(1)}, u32[]{:S(2)}, u32[]{:S(2)}) collective-permute-start(bf16[16,2432]{1,0:T(8,128)(2,1)S(1)} %get-tuple-element.37), channel_id=1, source_target_pairs={{0,6},{2,4},{4,2},{6,0},{8,14},{10,12},{12,10},{14,8},{1,7},{3,5},... | collective-permute-start | bytes 233480 | tf_op jit(solution)/shard_map/ppermute | solution.py:278
  27.0 5.0 %copy-start = (s32[128,8]{0,1:T(8,128)S(1)}, s32[128,8]{0,1:T(8,128)}, u32[]{:S(2)}) copy-start(s32[128,8]{0,1:T(8,128)} %param.9) | copy-start | bytes 12292
  27.1 4.9 %collective-permute-start.11 = (bf16[8,2432]{1,0:T(8,128)(2,1)S(1)}, bf16[8,2432]{1,0:T(8,128)(2,1)S(1)}, u32[]{:S(2)}, u32[]{:S(2)}) collective-permute-start(bf16[8,2432]{1,0:T(8,128)(2,1)S(1)} %add_convert_fusion), channel_id=1, source_target_pairs={{0,8},{2,10},{4,12},{6,14},{8,0},{10,2},{12,4},{14,6},{1,9},{3,11}... | collective-permute-start | bytes 116744 | tf_op jit(solution)/shard_map/ppermute | solution.py:278

commit v3 on v2

--- a/solution.py
+++ b/solution.py
@@ -346,9 +346,10 @@
         6 * half * hidden,
         6 + 2 * groups,
     )
-    *back, gate_grad, up_grad, down_grad = lax.optimization_barrier(
-        (*back, gate_grad, up_grad, down_grad)
-    )
+    gate_grad, up_grad, down_grad, *back = lax.optimization_barrier(
+        (gate_grad, up_grad, down_grad, *back[::-1])
+    )
+    back = back[::-1]
     total = sum(b[MAIN:].astype(F32) for b in back).astype(BF16)
     homes = [
         swap_by(total[k * MAIN : (k + 1) * MAIN], SPLIT * (k + 1)) for k in range(window - 1)

time: 33.5 us -> 33.4 us (level)
  starting transfers between devices: 18.1 us -> 17.5 us
  waiting for transfers between devices: 6.74 us -> 7.2 us
    ppermute x11, starting transfers between devices: 18 us -> 17.5 us  [swap_by(): return lax.ppermute(block, 'expert', [(i, i ^ mask) for i in range(count)])]
    ppermute x11, waiting for transfers between devices: 6.74 us -> 7.2 us  [swap_by(): return lax.ppermute(block, 'expert', [(i, i ^ mask) for i in range(count)])]
  transfers between devices with their start and end apart: 12 -> 12, of which waited for: 7 -> 8; matrix products, arithmetic and copies ran while one was open for 0% -> 0% of each run, Pallas kernels for 10% -> 10%
where the time goes in v3:
time: 33.4 us; the launch traced here: 33.2 us
  starting transfers between devices  17.5 us (52%)
  Pallas kernels  7.77 us (23%)
  waiting for transfers between devices  7.2 us (22%)
  between operations  0.69 us (2%)
    ppermute x11, starting transfers between devices, swap_by(): return lax.ppermute(block, 'expert', [(i, i ^ mask) for i in range(count)])  17.5 us
    pallas_call x5, Pallas kernels, call(): pl.pallas_call(kernel, out_shape=[jax.ShapeDtypeStruct(s, t) for s, t in...  7.77 us
    ppermute x11, waiting for transfers between devices, swap_by(): return lax.ppermute(block, 'expert', [(i, i ^ mask) for i in range(count)])  7.2 us
  transfers between devices with their start and end apart: 12, of which 8 were waited for; matrix products, arithmetic and copies ran while one was open for 0% of the time, Pallas kernels for 10%

profile of v3, /device:TPU:0, one launch (start us, length us, event | category | flops | bytes accessed | tf_op | source)
XLA Modules:
  0.0 33.2 jit_solution(18182867455407052439)
XLA Ops:
  0.6 1.5 %pack.1 = (bf16[16,2432]{1,0:T(8,128)(2,1)S(1)}, bf16[16,2432]{1,0:T(8,128)(2,1)S(1)}) custom-call(s32[8,128]{1,0:T(8,128)} %bitcast.17, bf16[8,128]{1,0:T(8,128)(2,1)} %bitcast.22, bf16[128,2048]{1,0:T(8,128)(2,1)} %tok_hbm.1, bf16[128,2048]{1,0:T(8,128)(2,1)} %grad_hbm.1), custom_call_target="tpu_custom_call" | custom-call | flops 18874368 | bytes 1048576 | tf_op jit(solution)/shard_map/pack/pallas_call | solution.py:264
  2.2 4.1 %collective-permute-start = (bf16[16,2432]{1,0:T(8,128)(2,1)S(1)}, bf16[16,2432]{1,0:T(8,128)(2,1)S(1)}, u32[]{:S(2)}, u32[]{:S(2)}) collective-permute-start(bf16[16,2432]{1,0:T(8,128)(2,1)S(1)} %get-tuple-element.30), channel_id=1, source_target_pairs={{0,8},{2,10},{4,12},{6,14},{8,0},{10,2},{12,4},{14,6},{1,9},{3,11}... | collective-permute-start | bytes 233480 | tf_op jit(solution)/shard_map/ppermute | solution.py:278
  6.3 2.5 %collective-permute-start.5 = (bf16[16,2432]{1,0:T(8,128)(2,1)S(1)}, bf16[16,2432]{1,0:T(8,128)(2,1)S(1)}, u32[]{:S(2)}, u32[]{:S(2)}) collective-permute-start(bf16[16,2432]{1,0:T(8,128)(2,1)S(1)} %get-tuple-element.29.refs_0_), channel_id=1, source_target_pairs={{0,6},{2,4},{4,2},{6,0},{8,14},{10,12},{12,10},{14,8},{1,7},{3,5},... | collective-permute-start | bytes 233480 | tf_op jit(solution)/shard_map/ppermute | solution.py:278
  8.8 0.4 %collective-permute-start.3 = (bf16[16,2432]{1,0:T(8,128)(2,1)S(1)}, bf16[16,2432]{1,0:T(8,128)(2,1)S(1)}, u32[]{:S(2)}, u32[]{:S(2)}) collective-permute-start(bf16[16,2432]{1,0:T(8,128)(2,1)S(1)} %get-tuple-element.29.refs_0_), channel_id=1, source_target_pairs={{0,4},{2,6},{4,0},{6,2},{8,12},{10,14},{12,8},{14,10},{1,5},{3,7},... | collective-permute-start | bytes 233480 | tf_op jit(solution)/shard_map/ppermute | solution.py:278
  9.2 0.5 %collective-permute-start.1 = (bf16[16,2432]{1,0:T(8,128)(2,1)S(1)}, bf16[16,2432]{1,0:T(8,128)(2,1)S(1)}, u32[]{:S(2)}, u32[]{:S(2)}) collective-permute-start(bf16[16,2432]{1,0:T(8,128)(2,1)S(1)} %get-tuple-element.29.refs_0_), channel_id=1, source_target_pairs={{0,2},{2,0},{4,6},{6,4},{8,10},{10,8},{12,14},{14,12},{1,3},{3,1},... | collective-permute-start | bytes 233480 | tf_op jit(solution)/shard_map/ppermute | solution.py:278
  9.8 0.0 collective-permute-done.refs_1_
  9.8 2.5 %collective-permute-start.6 = (bf16[16,2432]{1,0:T(8,128)(2,1)S(1)}, bf16[16,2432]{1,0:T(8,128)(2,1)S(1)}, u32[]{:S(2)}, u32[]{:S(2)}) collective-permute-start(bf16[16,2432]{1,0:T(8,128)(2,1)S(1)} %collective-permute-done.refs_1_), channel_id=1, source_target_pairs={{0,6},{2,4},{4,2},{6,0},{8,14},{10,12},{12,10},{14,8},{1,7},{3,5},... | collective-permute-start | bytes 233480 | tf_op jit(solution)/shard_map/ppermute | solution.py:278
  12.3 0.8 %collective-permute-start.4 = (bf16[16,2432]{1,0:T(8,128)(2,1)S(1)}, bf16[16,2432]{1,0:T(8,128)(2,1)S(1)}, u32[]{:S(2)}, u32[]{:S(2)}) collective-permute-start(bf16[16,2432]{1,0:T(8,128)(2,1)S(1)} %collective-permute-done.refs_1_), channel_id=1, source_target_pairs={{0,4},{2,6},{4,0},{6,2},{8,12},{10,14},{12,8},{14,10},{1,5},{3,7},... | collective-permute-start | bytes 233480 | tf_op jit(solution)/shard_map/ppermute | solution.py:278
  13.2 0.0 collective-permute-done.5.refs_2_.refs_6_
  13.2 0.7 %collective-permute-start.2 = (bf16[16,2432]{1,0:T(8,128)(2,1)S(1)}, bf16[16,2432]{1,0:T(8,128)(2,1)S(1)}, u32[]{:S(2)}, u32[]{:S(2)}) collective-permute-start(bf16[16,2432]{1,0:T(8,128)(2,1)S(1)} %collective-permute-done.refs_1_), channel_id=1, source_target_pairs={{0,2},{2,0},{4,6},{6,4},{8,10},{10,8},{12,14},{14,12},{1,3},{3,1},... | collective-permute-start | bytes 233480 | tf_op jit(solution)/shard_map/ppermute | solution.py:278
  13.9 0.1 collective-permute-done.3.refs_1_.refs_4_
  14.0 0.9 %collective-permute-done.1.refs_0_.refs_2_ = bf16[16,2432]{1,0:T(8,128)(2,1)S(1)} collective-permute-done((bf16[16,2432]{1,0:T(8,128)(2,1)S(1)}, bf16[16,2432]{1,0:T(8,128)(2,1)S(1)}, u32[]{:S(2)}, u32[]{:S(2)}) %collective-permute-start.1) | collective-permute-done | bytes 77856 | tf_op jit(solution)/shard_map/ppermute | solution.py:278
  14.9 1.6 %fetch.1 = (bf16[192,2048]{1,0:T(8,128)(2,1)S(1)}, bf16[192,2048]{1,0:T(8,128)(2,1)S(1)}, bf16[192,2048]{1,0:T(8,128)(2,1)S(1)}) custom-call(bf16[192,2048]{1,0:T(8,128)(2,1)} %bitcast.19, bf16[192,2048]{1,0:T(8,128)(2,1)} %bitcast.20, bf16[192,2048]{1,0:T(8,128)(2,1)} %bitcast.21, bf16[16,2432]{1,0:T(8,128)(2,1)S(1)} %collective-permute-done.1.refs_0_.refs_2_, ...), custom_call_target="tpu_custom_call" | custom-call | bytes 2359296 | tf_op jit(solution)/shard_map/fetch/pallas_call | solution.py:264
  16.5 0.0 collective-permute-done.6.refs_7_
  16.5 0.2 collective-permute-done.4.refs_5_
  16.7 0.8 %collective-permute-done.2.refs_3_ = bf16[16,2432]{1,0:T(8,128)(2,1)S(1)} collective-permute-done((bf16[16,2432]{1,0:T(8,128)(2,1)S(1)}, bf16[16,2432]{1,0:T(8,128)(2,1)S(1)}, u32[]{:S(2)}, u32[]{:S(2)}) %collective-permute-start.2) | collective-permute-done | bytes 77856 | tf_op jit(solution)/shard_map/ppermute | solution.py:278
  17.6 1.8 %expert.1 = (bf16[16,2432]{1,0:T(8,128)(2,1)S(1)}, bf16[16,2432]{1,0:T(8,128)(2,1)S(1)}, bf16[16,2432]{1,0:T(8,128)(2,1)S(1)}, bf16[16,2432]{1,0:T(8,128)(2,1)S(...) custom-call(bf16[16,2432]{1,0:T(8,128)(2,1)S(1)} %get-tuple-element.29.refs_0_, ...), custom_call_target="tpu_custom_call" | custom-call | flops 566231040 | bytes 2359296 | tf_op jit(solution)/shard_map/expert/pallas_call | solution.py:264
  19.3 0.1 collective-permute-start.7
  19.4 1.2 %collective-permute-start.8 = (bf16[16,2432]{1,0:T(8,128)(2,1)S(1)}, bf16[16,2432]{1,0:T(8,128)(2,1)S(1)}, u32[]{:S(2)}, u32[]{:S(2)}) collective-permute-start(bf16[16,2432]{1,0:T(8,128)(2,1)S(1)} %get-tuple-element.40), channel_id=1, source_target_pairs={{0,6},{2,4},{4,2},{6,0},{8,14},{10,12},{12,10},{14,8},{1,7},{3,5},... | collective-permute-start | bytes 233480 | tf_op jit(solution)/shard_map/ppermute | solution.py:278
  20.6 1.1 %collective-permute-start.9 = (bf16[16,2432]{1,0:T(8,128)(2,1)S(1)}, bf16[16,2432]{1,0:T(8,128)(2,1)S(1)}, u32[]{:S(2)}, u32[]{:S(2)}) collective-permute-start(bf16[16,2432]{1,0:T(8,128)(2,1)S(1)} %get-tuple-element.41), channel_id=1, source_target_pairs={{0,4},{2,6},{4,0},{6,2},{8,12},{10,14},{12,8},{14,10},{1,5},{3,7},... | collective-permute-start | bytes 233480 | tf_op jit(solution)/shard_map/ppermute | solution.py:278
  21.7 1.3 %collective-permute-start.10 = (bf16[16,2432]{1,0:T(8,128)(2,1)S(1)}, bf16[16,2432]{1,0:T(8,128)(2,1)S(1)}, u32[]{:S(2)}, u32[]{:S(2)}) collective-permute-start(bf16[16,2432]{1,0:T(8,128)(2,1)S(1)} %get-tuple-element.42), channel_id=1, source_target_pairs={{0,2},{2,0},{4,6},{6,4},{8,10},{10,8},{12,14},{14,12},{1,3},{3,1},... | collective-permute-start | bytes 233480 | tf_op jit(solution)/shard_map/ppermute | solution.py:278
  23.0 0.0 collective-permute-done.7.peer_ref
  23.0 1.6 %weights.1 = (bf16[192,1024]{1,0:T(8,128)(2,1)}, bf16[192,1024]{1,0:T(8,128)(2,1)}, bf16[192,1024]{1,0:T(8,128)(2,1)}) custom-call(bf16[144,1024]{1,0:T(8,128)(2,1)S(1)} %get-tuple-element.34.keep_ref, bf16[144,576]{1,0:T(8,128)(2,1)S(1)} %get-tuple-element.35.hid_ref, bf16[144,1600]{1,0:T(8,128)(2,1)S(1)} %collective-permute-done.7.peer_ref), custom_call_target="tpu_custom_call" | custom-call | flops 339738624 | bytes 1179648 | tf_op jit(solution)/shard_map/weights/pallas_call | solution.py:264
  24.6 1.0 %collective-permute-done.8.o3 = bf16[16,2432]{1,0:T(8,128)(2,1)S(1)} collective-permute-done((bf16[16,2432]{1,0:T(8,128)(2,1)S(1)}, bf16[16,2432]{1,0:T(8,128)(2,1)S(1)}, u32[]{:S(2)}, u32[]{:S(2)}) %collective-permute-start.8) | collective-permute-done | bytes 77856 | tf_op jit(solution)/shard_map/ppermute | solution.py:278
  25.5 0.5 %collective-permute-done.9.o2 = bf16[16,2432]{1,0:T(8,128)(2,1)S(1)} collective-permute-done((bf16[16,2432]{1,0:T(8,128)(2,1)S(1)}, bf16[16,2432]{1,0:T(8,128)(2,1)S(1)}, u32[]{:S(2)}, u32[]{:S(2)}) %collective-permute-start.9) | collective-permute-done | bytes 77856 | tf_op jit(solution)/shard_map/ppermute | solution.py:278
  26.0 0.7 %collective-permute-done.10.o1 = bf16[16,2432]{1,0:T(8,128)(2,1)S(1)} collective-permute-done((bf16[16,2432]{1,0:T(8,128)(2,1)S(1)}, bf16[16,2432]{1,0:T(8,128)(2,1)S(1)}, u32[]{:S(2)}, u32[]{:S(2)}) %collective-permute-start.10) | collective-permute-done | bytes 77856 | tf_op jit(solution)/shard_map/ppermute | solution.py:278
  26.8 0.0 copy-start
  26.8 2.2 %collective-permute-start.11 = (bf16[8,2432]{1,0:T(8,128)(2,1)S(1)}, bf16[8,2432]{1,0:T(8,128)(2,1)S(1)}, u32[]{:S(2)}, u32[]{:S(2)}) collective-permute-start(bf16[8,2432]{1,0:T(8,128)(2,1)S(1)} %add_convert_fusion), channel_id=1, source_target_pairs={{0,8},{2,10},{4,12},{6,14},{8,0},{10,2},{12,4},{14,6},{1,9},{3,11}... | collective-permute-start | bytes 116744 | tf_op jit(solution)/shard_map/ppermute | solution.py:278
  29.0 2.9 %collective-permute-done.11.rest_0_ = bf16[8,2432]{1,0:T(8,128)(2,1)S(1)} collective-permute-done((bf16[8,2432]{1,0:T(8,128)(2,1)S(1)}, bf16[8,2432]{1,0:T(8,128)(2,1)S(1)}, u32[]{:S(2)}, u32[]{:S(2)}) %collective-permute-start.11) | collective-permute-done | bytes 38944 | tf_op jit(solution)/shard_map/ppermute | solution.py:278
  31.9 0.0 copy-done
  31.9 1.3 %finish.1 = (bf16[128,2048]{1,0:T(8,128)(2,1)}, f32[8,128]{1,0:T(8,128)}) custom-call(s32[8,128]{1,0:T(8,128)S(1)} %bitcast.18, bf16[16,2432]{1,0:T(8,128)(2,1)S(1)} %get-tuple-element.44.o0, bf16[16,2432]{1,0:T(8,128)(2,1)S(1)} %collective-permute-done.10.o1, bf16[16,2432]{1,0:T(8,128)(2,1)S(1)} %collective-permute-done.9.o2, ...), custom_call_target="tpu_custom_call" | custom-call | flops 50331648 | bytes 524288 | tf_op jit(solution)/shard_map/finish/pallas_call | solution.py:264
  (1 shorter events, 0.0 us)
Async XLA Ops:
  2.2 7.6 %collective-permute-start = (bf16[16,2432]{1,0:T(8,128)(2,1)S(1)}, bf16[16,2432]{1,0:T(8,128)(2,1)S(1)}, u32[]{:S(2)}, u32[]{:S(2)}) collective-permute-start(bf16[16,2432]{1,0:T(8,128)(2,1)S(1)} %get-tuple-element.30), channel_id=1, source_target_pairs={{0,8},{2,10},{4,12},{6,14},{8,0},{10,2},{12,4},{14,6},{1,9},{3,11}... | collective-permute-start | bytes 233480 | tf_op jit(solution)/shard_map/ppermute | solution.py:278
  6.3 6.9 %collective-permute-start.5 = (bf16[16,2432]{1,0:T(8,128)(2,1)S(1)}, bf16[16,2432]{1,0:T(8,128)(2,1)S(1)}, u32[]{:S(2)}, u32[]{:S(2)}) collective-permute-start(bf16[16,2432]{1,0:T(8,128)(2,1)S(1)} %get-tuple-element.29.refs_0_), channel_id=1, source_target_pairs={{0,6},{2,4},{4,2},{6,0},{8,14},{10,12},{12,10},{14,8},{1,7},{3,5},... | collective-permute-start | bytes 233480 | tf_op jit(solution)/shard_map/ppermute | solution.py:278
  8.8 5.2 %collective-permute-start.3 = (bf16[16,2432]{1,0:T(8,128)(2,1)S(1)}, bf16[16,2432]{1,0:T(8,128)(2,1)S(1)}, u32[]{:S(2)}, u32[]{:S(2)}) collective-permute-start(bf16[16,2432]{1,0:T(8,128)(2,1)S(1)} %get-tuple-element.29.refs_0_), channel_id=1, source_target_pairs={{0,4},{2,6},{4,0},{6,2},{8,12},{10,14},{12,8},{14,10},{1,5},{3,7},... | collective-permute-start | bytes 233480 | tf_op jit(solution)/shard_map/ppermute | solution.py:278
  9.2 5.7 %collective-permute-start.1 = (bf16[16,2432]{1,0:T(8,128)(2,1)S(1)}, bf16[16,2432]{1,0:T(8,128)(2,1)S(1)}, u32[]{:S(2)}, u32[]{:S(2)}) collective-permute-start(bf16[16,2432]{1,0:T(8,128)(2,1)S(1)} %get-tuple-element.29.refs_0_), channel_id=1, source_target_pairs={{0,2},{2,0},{4,6},{6,4},{8,10},{10,8},{12,14},{14,12},{1,3},{3,1},... | collective-permute-start | bytes 233480 | tf_op jit(solution)/shard_map/ppermute | solution.py:278
  9.8 6.7 %collective-permute-start.6 = (bf16[16,2432]{1,0:T(8,128)(2,1)S(1)}, bf16[16,2432]{1,0:T(8,128)(2,1)S(1)}, u32[]{:S(2)}, u32[]{:S(2)}) collective-permute-start(bf16[16,2432]{1,0:T(8,128)(2,1)S(1)} %collective-permute-done.refs_1_), channel_id=1, source_target_pairs={{0,6},{2,4},{4,2},{6,0},{8,14},{10,12},{12,10},{14,8},{1,7},{3,5},... | collective-permute-start | bytes 233480 | tf_op jit(solution)/shard_map/ppermute | solution.py:278
  12.3 4.4 %collective-permute-start.4 = (bf16[16,2432]{1,0:T(8,128)(2,1)S(1)}, bf16[16,2432]{1,0:T(8,128)(2,1)S(1)}, u32[]{:S(2)}, u32[]{:S(2)}) collective-permute-start(bf16[16,2432]{1,0:T(8,128)(2,1)S(1)} %collective-permute-done.refs_1_), channel_id=1, source_target_pairs={{0,4},{2,6},{4,0},{6,2},{8,12},{10,14},{12,8},{14,10},{1,5},{3,7},... | collective-permute-start | bytes 233480 | tf_op jit(solution)/shard_map/ppermute | solution.py:278
  13.2 4.4 %collective-permute-start.2 = (bf16[16,2432]{1,0:T(8,128)(2,1)S(1)}, bf16[16,2432]{1,0:T(8,128)(2,1)S(1)}, u32[]{:S(2)}, u32[]{:S(2)}) collective-permute-start(bf16[16,2432]{1,0:T(8,128)(2,1)S(1)} %collective-permute-done.refs_1_), channel_id=1, source_target_pairs={{0,2},{2,0},{4,6},{6,4},{8,10},{10,8},{12,14},{14,12},{1,3},{3,1},... | collective-permute-start | bytes 233480 | tf_op jit(solution)/shard_map/ppermute | solution.py:278
  19.3 3.6 %collective-permute-start.7 = (bf16[144,1600]{1,0:T(8,128)(2,1)S(1)}, bf16[144,1600]{1,0:T(8,128)(2,1)S(1)}, u32[]{:S(2)}, u32[]{:S(2)}) collective-permute-start(bf16[144,1600]{1,0:T(8,128)(2,1)S(1)} %get-tuple-element.36), channel_id=1, source_target_pairs={{0,1},{1,0},{2,3},{3,2},{4,5},{5,4},{6,7},{7,6},{8,9},{9,8},{10,11... | collective-permute-start | bytes 1382408 | tf_op jit(solution)/shard_map/ppermute | solution.py:339
  19.4 6.1 %collective-permute-start.8 = (bf16[16,2432]{1,0:T(8,128)(2,1)S(1)}, bf16[16,2432]{1,0:T(8,128)(2,1)S(1)}, u32[]{:S(2)}, u32[]{:S(2)}) collective-permute-start(bf16[16,2432]{1,0:T(8,128)(2,1)S(1)} %get-tuple-element.40), channel_id=1, source_target_pairs={{0,6},{2,4},{4,2},{6,0},{8,14},{10,12},{12,10},{14,8},{1,7},{3,5},... | collective-permute-start | bytes 233480 | tf_op jit(solution)/shard_map/ppermute | solution.py:278
  20.6 5.4 %collective-permute-start.9 = (bf16[16,2432]{1,0:T(8,128)(2,1)S(1)}, bf16[16,2432]{1,0:T(8,128)(2,1)S(1)}, u32[]{:S(2)}, u32[]{:S(2)}) collective-permute-start(bf16[16,2432]{1,0:T(8,128)(2,1)S(1)} %get-tuple-element.41), channel_id=1, source_target_pairs={{0,4},{2,6},{4,0},{6,2},{8,12},{10,14},{12,8},{14,10},{1,5},{3,7},... | collective-permute-start | bytes 233480 | tf_op jit(solution)/shard_map/ppermute | solution.py:278
  21.7 5.1 %collective-permute-start.10 = (bf16[16,2432]{1,0:T(8,128)(2,1)S(1)}, bf16[16,2432]{1,0:T(8,128)(2,1)S(1)}, u32[]{:S(2)}, u32[]{:S(2)}) collective-permute-start(bf16[16,2432]{1,0:T(8,128)(2,1)S(1)} %get-tuple-element.42), channel_id=1, source_target_pairs={{0,2},{2,0},{4,6},{6,4},{8,10},{10,8},{12,14},{14,12},{1,3},{3,1},... | collective-permute-start | bytes 233480 | tf_op jit(solution)/shard_map/ppermute | solution.py:278
  26.8 5.2 %copy-start = (s32[128,8]{0,1:T(8,128)S(1)}, s32[128,8]{0,1:T(8,128)}, u32[]{:S(2)}) copy-start(s32[128,8]{0,1:T(8,128)} %param.9) | copy-start | bytes 12292
  26.8 5.1 %collective-permute-start.11 = (bf16[8,2432]{1,0:T(8,128)(2,1)S(1)}, bf16[8,2432]{1,0:T(8,128)(2,1)S(1)}, u32[]{:S(2)}, u32[]{:S(2)}) collective-permute-start(bf16[8,2432]{1,0:T(8,128)(2,1)S(1)} %add_convert_fusion), channel_id=1, source_target_pairs={{0,8},{2,10},{4,12},{6,14},{8,0},{10,2},{12,4},{14,6},{1,9},{3,11}... | collective-permute-start | bytes 116744 | tf_op jit(solution)/shard_map/ppermute | solution.py:278

commit v4 on v2

--- a/solution.py
+++ b/solution.py
@@ -32,12 +32,12 @@
         table = jnp.concatenate([table, jnp.zeros((pad, toks), F32)], axis=0)
     before = (iota((toks, toks), 0) < iota((toks, toks), 1)).astype(BF16)
     rank = dot(table.astype(BF16), before, (1, 0))
-    rank = jnp.where(table > 0, rank, -1.0)
-    return [rank[i : i + 1] for i in range(count)]
+    return jnp.where(table > 0, rank, -1.0)
 
 
 def pack_kernel(picks_hbm, gates_hbm, tok_hbm, grad_hbm, *refs):
-    outs, (picks_ref, gates_ref, tok_ref, grad_ref, sems) = refs[:-5], refs[-5:]
+    outs, rank_ref = refs[:-6], refs[-6]
+    picks_ref, gates_ref, tok_ref, grad_ref, sems = refs[-5:]
     loads = [
         pltpu.make_async_copy(src, dst, sems.at[i])
         for i, (src, dst) in enumerate(
@@ -55,7 +55,9 @@
     features = tok_ref.shape[1]
     fold = features // MAIN
     experts = [quad ^ k for k in range(window)]
-    ranks = places(picks, experts)
+    table = places(picks, experts)
+    rank_ref[...] = table
+    ranks = [table[k : k + 1] for k in range(window)]
     toks = picks.shape[1]
     seat = iota((MAIN, toks), 0).astype(F32)
     mains = [(r == seat).astype(F32) for r in ranks]
@@ -214,13 +216,13 @@
         out[...] = total.astype(BF16)
 
 
-def finish_kernel(picks_ref, o0, o1, o2, o3, *rest):
-    far, (grad_ref, comb_ref) = rest[:-2], rest[-2:]
+def finish_kernel(picks_ref, rank_ref, o0, o1, o2, o3, *rest):
+    far, (grad_hbm, comb_ref, grad_ref, sems) = rest[:-4], rest[-4:]
     window = 1 + len(far)
     quad = lax.axis_index("expert") // SPLIT
     picks = picks_ref[...]
     experts = [quad ^ k for k in range(window)]
-    ranks = places(picks, experts)
+    ranks = [rank_ref[k : k + 1, :] for k in range(window)]
     features = grad_ref.shape[1]
     fold = features // MAIN
     toks = picks.shape[1]
@@ -230,6 +232,7 @@
     blocks = [(0, o[:MAIN, :].astype(F32)) for o in (o0, o1, o2, o3)]
     blocks += [(1 + k, f[...].astype(F32)) for k, f in enumerate(far)]
     row = iota((MAIN, toks), 0)
+    stores = []
     for c in range(MAIN):
         cols = slice(c * fold, (c + 1) * fold)
         left, right = [], []
@@ -239,6 +242,13 @@
         left = jnp.concatenate(left, axis=0).astype(BF16)
         right = jnp.concatenate(right, axis=0).astype(BF16)
         grad_ref[:, cols] = dot(left, right, (0, 0)).astype(BF16)
+        if c % 2:
+            both = slice((c - 1) * fold, (c + 1) * fold)
+            store = pltpu.make_async_copy(
+                grad_ref.at[:, both], grad_hbm.at[:, both], sems.at[c // 2]
+            )
+            store.start()
+            stores.append(store)
     terms = [jnp.zeros((1, toks), F32) for _ in range(window)]
     for k, v in blocks:
         note = v[:, features + fold :]
@@ -248,6 +258,8 @@
     for k in range(window):
         comb = comb + jnp.where(picks == experts[k], terms[k], 0.0)
     comb_ref[...] = comb
+    for store in stores:
+        store.wait()
 
 
 VM = pl.BlockSpec(memory_space=pltpu.VMEM)
@@ -255,7 +267,7 @@
 ANY = pl.BlockSpec(memory_space=pl.ANY)
 
 
-def call(kernel, outs, name, args, flops, nbytes, room, specs=None, scratch=()):
+def call(kernel, outs, name, args, flops, nbytes, room, specs=None, scratch=(), out_specs=None):
     specs = specs or [VM] * len(args)
     args = [
         pltpu.with_memory_space_constraint(a, pltpu.HBM) if s is HBM else a
@@ -265,7 +277,7 @@
         kernel,
         out_shape=[jax.ShapeDtypeStruct(s, t) for s, t in outs],
         in_specs=specs,
-        out_specs=[VM] * len(outs),
+        out_specs=out_specs or [VM] * len(outs),
         scratch_shapes=list(scratch),
         compiler_params=pltpu.CompilerParams(vmem_limit_bytes=min(VMEM_LIMIT, room * MIB)),
         cost_estimate=pl.CostEstimate(flops=flops, bytes_accessed=nbytes, transcendentals=0),
@@ -290,9 +302,9 @@
     wg, wu, wd = gate_weight[0].T, up_weight[0].T, down_weight[0]
     groups = members // GROUP
 
-    packed = call(
+    *packed, ranks = call(
         pack_kernel,
-        [((2 * MAIN, width), BF16)] * window,
+        [((2 * MAIN, width), BF16)] * window + [((-(-window // 8) * 8, toks), F32)],
         "pack",
         (picks, gates_t, tokens, out_grad),
         2 * (MAIN + 1) * window * toks * features * 2,
@@ -336,6 +348,8 @@
         10 + 6 * groups,
     )
     back = [messages[0]] + [swap_by(messages[j], j) for j in range(1, SPLIT)]
+    send, first = lax.optimization_barrier((send, back[-1]))
+    back[-1] = first
     peer = lax.ppermute(send, "dp", [(0, 1), (1, 0)])
     gate_grad, up_grad, down_grad = call(
         weights_kernel,
@@ -346,21 +360,23 @@
         6 * half * hidden,
         6 + 2 * groups,
     )
-    *back, gate_grad, up_grad, down_grad = lax.optimization_barrier(
-        (*back, gate_grad, up_grad, down_grad)
-    )
-    total = sum(b[MAIN:].astype(F32) for b in back).astype(BF16)
+    total = sum(b[MAIN:].astype(F32) for b in back[::-1]).astype(BF16)
     homes = [
         swap_by(total[k * MAIN : (k + 1) * MAIN], SPLIT * (k + 1)) for k in range(window - 1)
     ]
+    gate_grad, up_grad, down_grad, *homes = lax.optimization_barrier(
+        (gate_grad, up_grad, down_grad, *homes)
+    )
     in_grad, combine = call(
         finish_kernel,
         [((toks, features), BF16), ((choices.shape[1], toks), F32)],
         "finish",
-        (picks, *back, *homes),
+        (picks, ranks, *back, *homes),
         2 * toks * features * 16 * (SPLIT + window),
         2 * toks * features,
         6 + window,
+        scratch=[pltpu.VMEM((toks, features), BF16), pltpu.SemaphoreType.DMA((MAIN // 2,))],
+        out_specs=[HBM, VM],
     )
     return (
         in_grad,

time: 33.5 us -> 33.8 us (level)
  Pallas kernels: 7.77 us -> 8.16 us
    pallas_call x5, Pallas kernels: 7.77 us -> 8.16 us  [call(): pl.pallas_call(kernel, out_shape=[jax.ShapeDtypeStruct(s, t) for s, t in...]
  transfers between devices with their start and end apart: 12 -> 12, of which waited for: 7 -> 8; matrix products, arithmetic and copies ran while one was open for 0% -> 0% of each run, Pallas kernels for 10% -> 10%
where the time goes in v4:
time: 33.8 us; the launch traced here: 33.6 us
  starting transfers between devices  18.3 us (54%)
  Pallas kernels  8.16 us (24%)
  waiting for transfers between devices  6.41 us (19%)
  between operations  0.68 us (2%)
    ppermute x11, starting transfers between devices, swap_by(): return lax.ppermute(block, 'expert', [(i, i ^ mask) for i in range(count)])  18.3 us
    pallas_call x5, Pallas kernels, call(): pl.pallas_call(kernel, out_shape=[jax.ShapeDtypeStruct(s, t) for s, t in...  8.16 us
    ppermute x11, waiting for transfers between devices, swap_by(): return lax.ppermute(block, 'expert', [(i, i ^ mask) for i in range(count)])  6.4 us
  transfers between devices with their start and end apart: 12, of which 8 were waited for; matrix products, arithmetic and copies ran while one was open for 0% of the time, Pallas kernels for 10%

profile of v4, /device:TPU:0, one launch (start us, length us, event | category | flops | bytes accessed | tf_op | source)
XLA Modules:
  0.0 33.6 jit_solution(13168097523667910565)
XLA Ops:
  0.6 1.5 %pack.1 = (bf16[16,2432]{1,0:T(8,128)(2,1)S(1)}, bf16[16,2432]{1,0:T(8,128)(2,1)S(1)}, f32[8,128]{1,0:T(8,128)S(1)}) custom-call(s32[8,128]{1,0:T(8,128)} %bitcast.17, bf16[8,128]{1,0:T(8,128)(2,1)} %bitcast.22, bf16[128,2048]{1,0:T(8,128)(2,1)} %tok_hbm.1, bf16[128,2048]{1,0:T(8,128)(2,1)} %grad_hbm.1), custom_call_target="tpu_custom_call" | custom-call | flops 18874368 | bytes 1048576 | tf_op jit(solution)/shard_map/pack/pallas_call | solution.py:276
  2.2 4.1 %collective-permute-start = (bf16[16,2432]{1,0:T(8,128)(2,1)S(1)}, bf16[16,2432]{1,0:T(8,128)(2,1)S(1)}, u32[]{:S(2)}, u32[]{:S(2)}) collective-permute-start(bf16[16,2432]{1,0:T(8,128)(2,1)S(1)} %get-tuple-element.31), channel_id=1, source_target_pairs={{0,8},{2,10},{4,12},{6,14},{8,0},{10,2},{12,4},{14,6},{1,9},{3,11}... | collective-permute-start | bytes 233480 | tf_op jit(solution)/shard_map/ppermute | solution.py:290
  6.3 2.5 %collective-permute-start.5 = (bf16[16,2432]{1,0:T(8,128)(2,1)S(1)}, bf16[16,2432]{1,0:T(8,128)(2,1)S(1)}, u32[]{:S(2)}, u32[]{:S(2)}) collective-permute-start(bf16[16,2432]{1,0:T(8,128)(2,1)S(1)} %get-tuple-element.30.refs_0_), channel_id=1, source_target_pairs={{0,6},{2,4},{4,2},{6,0},{8,14},{10,12},{12,10},{14,8},{1,7},{3,5},... | collective-permute-start | bytes 233480 | tf_op jit(solution)/shard_map/ppermute | solution.py:290
  8.8 0.4 %collective-permute-start.3 = (bf16[16,2432]{1,0:T(8,128)(2,1)S(1)}, bf16[16,2432]{1,0:T(8,128)(2,1)S(1)}, u32[]{:S(2)}, u32[]{:S(2)}) collective-permute-start(bf16[16,2432]{1,0:T(8,128)(2,1)S(1)} %get-tuple-element.30.refs_0_), channel_id=1, source_target_pairs={{0,4},{2,6},{4,0},{6,2},{8,12},{10,14},{12,8},{14,10},{1,5},{3,7},... | collective-permute-start | bytes 233480 | tf_op jit(solution)/shard_map/ppermute | solution.py:290
  9.2 0.5 %collective-permute-start.1 = (bf16[16,2432]{1,0:T(8,128)(2,1)S(1)}, bf16[16,2432]{1,0:T(8,128)(2,1)S(1)}, u32[]{:S(2)}, u32[]{:S(2)}) collective-permute-start(bf16[16,2432]{1,0:T(8,128)(2,1)S(1)} %get-tuple-element.30.refs_0_), channel_id=1, source_target_pairs={{0,2},{2,0},{4,6},{6,4},{8,10},{10,8},{12,14},{14,12},{1,3},{3,1},... | collective-permute-start | bytes 233480 | tf_op jit(solution)/shard_map/ppermute | solution.py:290
  9.8 0.0 collective-permute-done.refs_1_
  9.8 2.5 %collective-permute-start.6 = (bf16[16,2432]{1,0:T(8,128)(2,1)S(1)}, bf16[16,2432]{1,0:T(8,128)(2,1)S(1)}, u32[]{:S(2)}, u32[]{:S(2)}) collective-permute-start(bf16[16,2432]{1,0:T(8,128)(2,1)S(1)} %collective-permute-done.refs_1_), channel_id=1, source_target_pairs={{0,6},{2,4},{4,2},{6,0},{8,14},{10,12},{12,10},{14,8},{1,7},{3,5},... | collective-permute-start | bytes 233480 | tf_op jit(solution)/shard_map/ppermute | solution.py:290
  12.3 0.8 %collective-permute-start.4 = (bf16[16,2432]{1,0:T(8,128)(2,1)S(1)}, bf16[16,2432]{1,0:T(8,128)(2,1)S(1)}, u32[]{:S(2)}, u32[]{:S(2)}) collective-permute-start(bf16[16,2432]{1,0:T(8,128)(2,1)S(1)} %collective-permute-done.refs_1_), channel_id=1, source_target_pairs={{0,4},{2,6},{4,0},{6,2},{8,12},{10,14},{12,8},{14,10},{1,5},{3,7},... | collective-permute-start | bytes 233480 | tf_op jit(solution)/shard_map/ppermute | solution.py:290
  13.2 0.0 collective-permute-done.5.refs_2_.refs_6_
  13.2 0.7 %collective-permute-start.2 = (bf16[16,2432]{1,0:T(8,128)(2,1)S(1)}, bf16[16,2432]{1,0:T(8,128)(2,1)S(1)}, u32[]{:S(2)}, u32[]{:S(2)}) collective-permute-start(bf16[16,2432]{1,0:T(8,128)(2,1)S(1)} %collective-permute-done.refs_1_), channel_id=1, source_target_pairs={{0,2},{2,0},{4,6},{6,4},{8,10},{10,8},{12,14},{14,12},{1,3},{3,1},... | collective-permute-start | bytes 233480 | tf_op jit(solution)/shard_map/ppermute | solution.py:290
  13.9 0.1 collective-permute-done.3.refs_1_.refs_4_
  14.0 0.9 %collective-permute-done.1.refs_0_.refs_2_ = bf16[16,2432]{1,0:T(8,128)(2,1)S(1)} collective-permute-done((bf16[16,2432]{1,0:T(8,128)(2,1)S(1)}, bf16[16,2432]{1,0:T(8,128)(2,1)S(1)}, u32[]{:S(2)}, u32[]{:S(2)}) %collective-permute-start.1) | collective-permute-done | bytes 77856 | tf_op jit(solution)/shard_map/ppermute | solution.py:290
  14.9 1.6 %fetch.1 = (bf16[192,2048]{1,0:T(8,128)(2,1)S(1)}, bf16[192,2048]{1,0:T(8,128)(2,1)S(1)}, bf16[192,2048]{1,0:T(8,128)(2,1)S(1)}) custom-call(bf16[192,2048]{1,0:T(8,128)(2,1)} %bitcast.19, bf16[192,2048]{1,0:T(8,128)(2,1)} %bitcast.20, bf16[192,2048]{1,0:T(8,128)(2,1)} %bitcast.21, bf16[16,2432]{1,0:T(8,128)(2,1)S(1)} %collective-permute-done.1.refs_0_.refs_2_, ...), custom_call_target="tpu_custom_call" | custom-call | bytes 2359296 | tf_op jit(solution)/shard_map/fetch/pallas_call | solution.py:276
  16.5 0.0 collective-permute-done.6.refs_7_
  16.5 0.2 collective-permute-done.4.refs_5_
  16.7 0.8 %collective-permute-done.2.refs_3_ = bf16[16,2432]{1,0:T(8,128)(2,1)S(1)} collective-permute-done((bf16[16,2432]{1,0:T(8,128)(2,1)S(1)}, bf16[16,2432]{1,0:T(8,128)(2,1)S(1)}, u32[]{:S(2)}, u32[]{:S(2)}) %collective-permute-start.2) | collective-permute-done | bytes 77856 | tf_op jit(solution)/shard_map/ppermute | solution.py:290
  17.6 1.8 %expert.1 = (bf16[16,2432]{1,0:T(8,128)(2,1)S(1)}, bf16[16,2432]{1,0:T(8,128)(2,1)S(1)}, bf16[16,2432]{1,0:T(8,128)(2,1)S(1)}, bf16[16,2432]{1,0:T(8,128)(2,1)S(...) custom-call(bf16[16,2432]{1,0:T(8,128)(2,1)S(1)} %get-tuple-element.30.refs_0_, ...), custom_call_target="tpu_custom_call" | custom-call | flops 566231040 | bytes 2359296 | tf_op jit(solution)/shard_map/expert/pallas_call | solution.py:276
  19.3 1.2 %collective-permute-start.9 = (bf16[16,2432]{1,0:T(8,128)(2,1)S(1)}, bf16[16,2432]{1,0:T(8,128)(2,1)S(1)}, u32[]{:S(2)}, u32[]{:S(2)}) collective-permute-start(bf16[16,2432]{1,0:T(8,128)(2,1)S(1)} %get-tuple-element.39), channel_id=1, source_target_pairs={{0,6},{2,4},{4,2},{6,0},{8,14},{10,12},{12,10},{14,8},{1,7},{3,5},... | collective-permute-start | bytes 233480 | tf_op jit(solution)/shard_map/ppermute | solution.py:290
  20.5 1.5 %collective-permute-start.7 = (bf16[16,2432]{1,0:T(8,128)(2,1)S(1)}, bf16[16,2432]{1,0:T(8,128)(2,1)S(1)}, u32[]{:S(2)}, u32[]{:S(2)}) collective-permute-start(bf16[16,2432]{1,0:T(8,128)(2,1)S(1)} %get-tuple-element.36), channel_id=1, source_target_pairs={{0,2},{2,0},{4,6},{6,4},{8,10},{10,8},{12,14},{14,12},{1,3},{3,1},... | collective-permute-start | bytes 233480 | tf_op jit(solution)/shard_map/ppermute | solution.py:290
  22.1 0.8 %collective-permute-start.8 = (bf16[16,2432]{1,0:T(8,128)(2,1)S(1)}, bf16[16,2432]{1,0:T(8,128)(2,1)S(1)}, u32[]{:S(2)}, u32[]{:S(2)}) collective-permute-start(bf16[16,2432]{1,0:T(8,128)(2,1)S(1)} %get-tuple-element.37), channel_id=1, source_target_pairs={{0,4},{2,6},{4,0},{6,2},{8,12},{10,14},{12,8},{14,10},{1,5},{3,7},... | collective-permute-start | bytes 233480 | tf_op jit(solution)/shard_map/ppermute | solution.py:290
  22.9 1.9 %collective-permute-done.9.o3 = bf16[16,2432]{1,0:T(8,128)(2,1)S(1)} collective-permute-done((bf16[16,2432]{1,0:T(8,128)(2,1)S(1)}, bf16[16,2432]{1,0:T(8,128)(2,1)S(1)}, u32[]{:S(2)}, u32[]{:S(2)}) %collective-permute-start.9) | collective-permute-done | bytes 77856 | tf_op jit(solution)/shard_map/ppermute | solution.py:290
  24.8 0.0 collective-permute-start.10
  24.8 0.8 %collective-permute-done.7.o1 = bf16[16,2432]{1,0:T(8,128)(2,1)S(1)} collective-permute-done((bf16[16,2432]{1,0:T(8,128)(2,1)S(1)}, bf16[16,2432]{1,0:T(8,128)(2,1)S(1)}, u32[]{:S(2)}, u32[]{:S(2)}) %collective-permute-start.7) | collective-permute-done | bytes 77856 | tf_op jit(solution)/shard_map/ppermute | solution.py:290
  25.5 0.9 %collective-permute-done.8.o2 = bf16[16,2432]{1,0:T(8,128)(2,1)S(1)} collective-permute-done((bf16[16,2432]{1,0:T(8,128)(2,1)S(1)}, bf16[16,2432]{1,0:T(8,128)(2,1)S(1)}, u32[]{:S(2)}, u32[]{:S(2)}) %collective-permute-start.8) | collective-permute-done | bytes 77856 | tf_op jit(solution)/shard_map/ppermute | solution.py:290
  26.5 3.0 %collective-permute-start.11 = (bf16[8,2432]{1,0:T(8,128)(2,1)S(1)}, bf16[8,2432]{1,0:T(8,128)(2,1)S(1)}, u32[]{:S(2)}, u32[]{:S(2)}) collective-permute-start(bf16[8,2432]{1,0:T(8,128)(2,1)S(1)} %add_convert_fusion), channel_id=1, source_target_pairs={{0,8},{2,10},{4,12},{6,14},{8,0},{10,2},{12,4},{14,6},{1,9},{3,11}... | collective-permute-start | bytes 116744 | tf_op jit(solution)/shard_map/ppermute | solution.py:290
  29.5 0.0 collective-permute-done.10.peer_ref
  29.5 1.6 %weights.1 = (bf16[192,1024]{1,0:T(8,128)(2,1)}, bf16[192,1024]{1,0:T(8,128)(2,1)}, bf16[192,1024]{1,0:T(8,128)(2,1)}) custom-call(bf16[144,1024]{1,0:T(8,128)(2,1)S(1)} %get-tuple-element.41.keep_ref, bf16[144,576]{1,0:T(8,128)(2,1)S(1)} %get-tuple-element.42.hid_ref, bf16[144,1600]{1,0:T(8,128)(2,1)S(1)} %collective-permute-done.10.peer_ref), custom_call_target="tpu_custom_call" | custom-call | flops 339738624 | bytes 1179648 | tf_op jit(solution)/shard_map/weights/pallas_call | solution.py:276
  31.1 0.0 copy-start
  31.1 0.8 %collective-permute-done.11.rest_0_ = bf16[8,2432]{1,0:T(8,128)(2,1)S(1)} collective-permute-done((bf16[8,2432]{1,0:T(8,128)(2,1)S(1)}, bf16[8,2432]{1,0:T(8,128)(2,1)S(1)}, u32[]{:S(2)}, u32[]{:S(2)}) %collective-permute-start.11) | collective-permute-done | bytes 38944 | tf_op jit(solution)/shard_map/ppermute | solution.py:290
  31.9 0.0 copy-done
  31.9 1.7 %finish.1 = (bf16[128,2048]{1,0:T(8,128)(2,1)}, f32[8,128]{1,0:T(8,128)}) custom-call(s32[8,128]{1,0:T(8,128)S(1)} %bitcast.18, f32[8,128]{1,0:T(8,128)S(1)} %get-tuple-element.29.rank_ref, bf16[16,2432]{1,0:T(8,128)(2,1)S(1)} %get-tuple-element.35.o0, bf16[16,2432]{1,0:T(8,128)(2,1)S(1)} %collective-permute-done.7.o1, ...), custom_call_target="tpu_custom_call" | custom-call | flops 50331648 | bytes 524288 | tf_op jit(solution)/shard_map/finish/pallas_call | solution.py:276
  (1 shorter events, 0.0 us)
Async XLA Ops:
  2.2 7.6 %collective-permute-start = (bf16[16,2432]{1,0:T(8,128)(2,1)S(1)}, bf16[16,2432]{1,0:T(8,128)(2,1)S(1)}, u32[]{:S(2)}, u32[]{:S(2)}) collective-permute-start(bf16[16,2432]{1,0:T(8,128)(2,1)S(1)} %get-tuple-element.31), channel_id=1, source_target_pairs={{0,8},{2,10},{4,12},{6,14},{8,0},{10,2},{12,4},{14,6},{1,9},{3,11}... | collective-permute-start | bytes 233480 | tf_op jit(solution)/shard_map/ppermute | solution.py:290
  6.3 6.9 %collective-permute-start.5 = (bf16[16,2432]{1,0:T(8,128)(2,1)S(1)}, bf16[16,2432]{1,0:T(8,128)(2,1)S(1)}, u32[]{:S(2)}, u32[]{:S(2)}) collective-permute-start(bf16[16,2432]{1,0:T(8,128)(2,1)S(1)} %get-tuple-element.30.refs_0_), channel_id=1, source_target_pairs={{0,6},{2,4},{4,2},{6,0},{8,14},{10,12},{12,10},{14,8},{1,7},{3,5},... | collective-permute-start | bytes 233480 | tf_op jit(solution)/shard_map/ppermute | solution.py:290
  8.8 5.2 %collective-permute-start.3 = (bf16[16,2432]{1,0:T(8,128)(2,1)S(1)}, bf16[16,2432]{1,0:T(8,128)(2,1)S(1)}, u32[]{:S(2)}, u32[]{:S(2)}) collective-permute-start(bf16[16,2432]{1,0:T(8,128)(2,1)S(1)} %get-tuple-element.30.refs_0_), channel_id=1, source_target_pairs={{0,4},{2,6},{4,0},{6,2},{8,12},{10,14},{12,8},{14,10},{1,5},{3,7},... | collective-permute-start | bytes 233480 | tf_op jit(solution)/shard_map/ppermute | solution.py:290
  9.2 5.7 %collective-permute-start.1 = (bf16[16,2432]{1,0:T(8,128)(2,1)S(1)}, bf16[16,2432]{1,0:T(8,128)(2,1)S(1)}, u32[]{:S(2)}, u32[]{:S(2)}) collective-permute-start(bf16[16,2432]{1,0:T(8,128)(2,1)S(1)} %get-tuple-element.30.refs_0_), channel_id=1, source_target_pairs={{0,2},{2,0},{4,6},{6,4},{8,10},{10,8},{12,14},{14,12},{1,3},{3,1},... | collective-permute-start | bytes 233480 | tf_op jit(solution)/shard_map/ppermute | solution.py:290
  9.8 6.7 %collective-permute-start.6 = (bf16[16,2432]{1,0:T(8,128)(2,1)S(1)}, bf16[16,2432]{1,0:T(8,128)(2,1)S(1)}, u32[]{:S(2)}, u32[]{:S(2)}) collective-permute-start(bf16[16,2432]{1,0:T(8,128)(2,1)S(1)} %collective-permute-done.refs_1_), channel_id=1, source_target_pairs={{0,6},{2,4},{4,2},{6,0},{8,14},{10,12},{12,10},{14,8},{1,7},{3,5},... | collective-permute-start | bytes 233480 | tf_op jit(solution)/shard_map/ppermute | solution.py:290
  12.3 4.4 %collective-permute-start.4 = (bf16[16,2432]{1,0:T(8,128)(2,1)S(1)}, bf16[16,2432]{1,0:T(8,128)(2,1)S(1)}, u32[]{:S(2)}, u32[]{:S(2)}) collective-permute-start(bf16[16,2432]{1,0:T(8,128)(2,1)S(1)} %collective-permute-done.refs_1_), channel_id=1, source_target_pairs={{0,4},{2,6},{4,0},{6,2},{8,12},{10,14},{12,8},{14,10},{1,5},{3,7},... | collective-permute-start | bytes 233480 | tf_op jit(solution)/shard_map/ppermute | solution.py:290
  13.2 4.4 %collective-permute-start.2 = (bf16[16,2432]{1,0:T(8,128)(2,1)S(1)}, bf16[16,2432]{1,0:T(8,128)(2,1)S(1)}, u32[]{:S(2)}, u32[]{:S(2)}) collective-permute-start(bf16[16,2432]{1,0:T(8,128)(2,1)S(1)} %collective-permute-done.refs_1_), channel_id=1, source_target_pairs={{0,2},{2,0},{4,6},{6,4},{8,10},{10,8},{12,14},{14,12},{1,3},{3,1},... | collective-permute-start | bytes 233480 | tf_op jit(solution)/shard_map/ppermute | solution.py:290
  19.3 5.4 %collective-permute-start.9 = (bf16[16,2432]{1,0:T(8,128)(2,1)S(1)}, bf16[16,2432]{1,0:T(8,128)(2,1)S(1)}, u32[]{:S(2)}, u32[]{:S(2)}) collective-permute-start(bf16[16,2432]{1,0:T(8,128)(2,1)S(1)} %get-tuple-element.39), channel_id=1, source_target_pairs={{0,6},{2,4},{4,2},{6,0},{8,14},{10,12},{12,10},{14,8},{1,7},{3,5},... | collective-permute-start | bytes 233480 | tf_op jit(solution)/shard_map/ppermute | solution.py:290
  20.5 5.0 %collective-permute-start.7 = (bf16[16,2432]{1,0:T(8,128)(2,1)S(1)}, bf16[16,2432]{1,0:T(8,128)(2,1)S(1)}, u32[]{:S(2)}, u32[]{:S(2)}) collective-permute-start(bf16[16,2432]{1,0:T(8,128)(2,1)S(1)} %get-tuple-element.36), channel_id=1, source_target_pairs={{0,2},{2,0},{4,6},{6,4},{8,10},{10,8},{12,14},{14,12},{1,3},{3,1},... | collective-permute-start | bytes 233480 | tf_op jit(solution)/shard_map/ppermute | solution.py:290
  22.1 4.4 %collective-permute-start.8 = (bf16[16,2432]{1,0:T(8,128)(2,1)S(1)}, bf16[16,2432]{1,0:T(8,128)(2,1)S(1)}, u32[]{:S(2)}, u32[]{:S(2)}) collective-permute-start(bf16[16,2432]{1,0:T(8,128)(2,1)S(1)} %get-tuple-element.37), channel_id=1, source_target_pairs={{0,4},{2,6},{4,0},{6,2},{8,12},{10,14},{12,8},{14,10},{1,5},{3,7},... | collective-permute-start | bytes 233480 | tf_op jit(solution)/shard_map/ppermute | solution.py:290
  24.8 4.8 %collective-permute-start.10 = (bf16[144,1600]{1,0:T(8,128)(2,1)S(1)}, bf16[144,1600]{1,0:T(8,128)(2,1)S(1)}, u32[]{:S(2)}, u32[]{:S(2)}) collective-permute-start(bf16[144,1600]{1,0:T(8,128)(2,1)S(1)} %get-tuple-element.43), channel_id=1, source_target_pairs={{0,1},{1,0},{2,3},{3,2},{4,5},{5,4},{6,7},{7,6},{8,9},{9,8},{10,11... | collective-permute-start | bytes 1382408 | tf_op jit(solution)/shard_map/ppermute | solution.py:353
  26.5 5.4 %collective-permute-start.11 = (bf16[8,2432]{1,0:T(8,128)(2,1)S(1)}, bf16[8,2432]{1,0:T(8,128)(2,1)S(1)}, u32[]{:S(2)}, u32[]{:S(2)}) collective-permute-start(bf16[8,2432]{1,0:T(8,128)(2,1)S(1)} %add_convert_fusion), channel_id=1, source_target_pairs={{0,8},{2,10},{4,12},{6,14},{8,0},{10,2},{12,4},{14,6},{1,9},{3,11}... | collective-permute-start | bytes 116744 | tf_op jit(solution)/shard_map/ppermute | solution.py:290
  31.1 0.8 %copy-start = (s32[128,8]{0,1:T(8,128)S(1)}, s32[128,8]{0,1:T(8,128)}, u32[]{:S(2)}) copy-start(s32[128,8]{0,1:T(8,128)} %param.9) | copy-start | bytes 12292

commit v5 on v4

--- a/solution.py
+++ b/solution.py
@@ -91,19 +91,22 @@
 
 
 def fetch_kernel(gate_hbm, up_hbm, down_hbm, *refs):
-    outs, sems = refs[-4:-1], refs[-1]
+    gate_ref, up_ref, across_ref, down_ref, sems = refs[-5:]
+    held = (gate_ref, up_ref, down_ref)
     loads = [
         pltpu.make_async_copy(src, dst, sems.at[i])
-        for i, (src, dst) in enumerate(zip((gate_hbm, up_hbm, down_hbm), outs))
+        for i, (src, dst) in enumerate(zip((gate_hbm, up_hbm, down_hbm), held))
     ]
     for load in loads:
         load.start()
-    for load in loads:
+    hidden = gate_ref.shape[0]
+    for i, (load, ref) in enumerate(zip(loads, held)):
         load.wait()
+        across_ref[:, i * hidden : (i + 1) * hidden] = ref[...].T
 
 
 def expert_kernel(*refs):
-    wg_ref, wu_ref, wd_ref, m0, m1, m2, m3, keep_ref, hid_ref, send_ref = refs[-10:]
+    wg_ref, wu_ref, across_ref, m0, m1, m2, m3, keep_ref, hid_ref, send_ref = refs[-10:]
     zs, ms = refs[:-10], (m0, m1, m2, m3)
     features = wg_ref.shape[1]
     hidden = wg_ref.shape[0]
@@ -134,9 +137,8 @@
         flat = dot(swap.astype(BF16), bent, (1, 0)).astype(BF16)
         ninth = jnp.concatenate([flat[c * pair : (c + 1) * pair] for c in range(MAIN)], axis=1)
         rows = jnp.concatenate(main + [ninth], axis=0)
-        pre_gate = dot(rows, wg_ref[...], (1, 1))
-        pre_up = dot(rows, wu_ref[...], (1, 1))
-        back = dot(rows, wd_ref[...], (1, 1))
+        pre = dot(rows, across_ref[...], (1, 0))
+        pre_gate, pre_up, back = (pre[:, i * hidden : (i + 1) * hidden] for i in range(3))
         pieces = GROUP + 1
         upper = lambda v: v.reshape(pieces, 2, MAIN, hidden)[:, 0].reshape(pieces * MAIN, hidden)
         lower = lambda v: v.reshape(pieces, 2, MAIN, hidden)[:, 1].reshape(pieces * MAIN, hidden)
@@ -217,7 +219,7 @@
 
 
 def finish_kernel(picks_ref, rank_ref, o0, o1, o2, o3, *rest):
-    far, (grad_hbm, comb_ref, grad_ref, sems) = rest[:-4], rest[-4:]
+    far, (grad_ref, comb_ref) = rest[:-2], rest[-2:]
     window = 1 + len(far)
     quad = lax.axis_index("expert") // SPLIT
     picks = picks_ref[...]
@@ -232,7 +234,6 @@
     blocks = [(0, o[:MAIN, :].astype(F32)) for o in (o0, o1, o2, o3)]
     blocks += [(1 + k, f[...].astype(F32)) for k, f in enumerate(far)]
     row = iota((MAIN, toks), 0)
-    stores = []
     for c in range(MAIN):
         cols = slice(c * fold, (c + 1) * fold)
         left, right = [], []
@@ -242,13 +243,6 @@
         left = jnp.concatenate(left, axis=0).astype(BF16)
         right = jnp.concatenate(right, axis=0).astype(BF16)
         grad_ref[:, cols] = dot(left, right, (0, 0)).astype(BF16)
-        if c % 2:
-            both = slice((c - 1) * fold, (c + 1) * fold)
-            store = pltpu.make_async_copy(
-                grad_ref.at[:, both], grad_hbm.at[:, both], sems.at[c // 2]
-            )
-            store.start()
-            stores.append(store)
     terms = [jnp.zeros((1, toks), F32) for _ in range(window)]
     for k, v in blocks:
         note = v[:, features + fold :]
@@ -258,8 +252,6 @@
     for k in range(window):
         comb = comb + jnp.where(picks == experts[k], terms[k], 0.0)
     comb_ref[...] = comb
-    for store in stores:
-        store.wait()
 
 
 VM = pl.BlockSpec(memory_space=pltpu.VMEM)
@@ -267,7 +259,7 @@
 ANY = pl.BlockSpec(memory_space=pl.ANY)
 
 
-def call(kernel, outs, name, args, flops, nbytes, room, specs=None, scratch=(), out_specs=None):
+def call(kernel, outs, name, args, flops, nbytes, room, specs=None, scratch=()):
     specs = specs or [VM] * len(args)
     args = [
         pltpu.with_memory_space_constraint(a, pltpu.HBM) if s is HBM else a
@@ -277,7 +269,7 @@
         kernel,
         out_shape=[jax.ShapeDtypeStruct(s, t) for s, t in outs],
         in_specs=specs,
-        out_specs=out_specs or [VM] * len(outs),
+        out_specs=[VM] * len(outs),
         scratch_shapes=list(scratch),
         compiler_params=pltpu.CompilerParams(vmem_limit_bytes=min(VMEM_LIMIT, room * MIB)),
         cost_estimate=pl.CostEstimate(flops=flops, bytes_accessed=nbytes, transcendentals=0),
@@ -319,14 +311,14 @@
     near = [own] + [swap_by(own, j) for j in range(1, SPLIT)]
     held = call(
         fetch_kernel,
-        [(w.shape, BF16) for w in (wg, wu, wd)],
+        [(wg.shape, BF16), (wu.shape, BF16), ((features, 3 * hidden), BF16)],
         "fetch",
         (wg, wu, wd, *near[1:]),
         0,
         6 * features * hidden,
-        4,
+        12,
         [HBM] * 3 + [ANY] * (SPLIT - 1),
-        [pltpu.SemaphoreType.DMA((3,))],
+        [pltpu.VMEM(wd.shape, BF16), pltpu.SemaphoreType.DMA((3,))],
     )
     from_far = arrived[0] if window == 2 else jnp.concatenate(arrived, axis=0)
     far = [from_far] + [swap_by(from_far, j) for j in range(1, SPLIT)]
@@ -375,8 +367,6 @@
         2 * toks * features * 16 * (SPLIT + window),
         2 * toks * features,
         6 + window,
-        scratch=[pltpu.VMEM((toks, features), BF16), pltpu.SemaphoreType.DMA((MAIN // 2,))],
-        out_specs=[HBM, VM],
     )
     return (
         in_grad,

time: 33.8 us -> 32.9 us (0.973)
  waiting for transfers between devices: 6.41 us -> 6.06 us
    ppermute x11, waiting for transfers between devices: 6.4 us -> 6.06 us  [swap_by(): return lax.ppermute(block, 'expert', [(i, i ^ mask) for i in range(count)])]
  transfers between devices with their start and end apart: 12 -> 12, of which waited for: 8 -> 7; matrix products, arithmetic and copies ran while one was open for 0% -> 0% of each run, Pallas kernels for 10% -> 12%
where the time goes in v5:
time: 32.9 us; the launch traced here: 32.7 us
  starting transfers between devices  18 us (55%)
  Pallas kernels  7.88 us (24%)
  waiting for transfers between devices  6.06 us (18%)
  between operations  0.69 us (2%)
    ppermute x11, starting transfers between devices, swap_by(): return lax.ppermute(block, 'expert', [(i, i ^ mask) for i in range(count)])  18 us
    pallas_call x5, Pallas kernels, call(): pl.pallas_call(kernel, out_shape=[jax.ShapeDtypeStruct(s, t) for s, t in...  7.88 us
    ppermute x11, waiting for transfers between devices, swap_by(): return lax.ppermute(block, 'expert', [(i, i ^ mask) for i in range(count)])  6.06 us
  transfers between devices with their start and end apart: 12, of which 7 were waited for; matrix products, arithmetic and copies ran while one was open for 0% of the time, Pallas kernels for 12%

profile of v5, /device:TPU:0, one launch (start us, length us, event | category | flops | bytes accessed | tf_op | source)
XLA Modules:
  0.0 32.7 jit_solution(17260229111600716597)
XLA Ops:
  0.6 1.5 %pack.1 = (bf16[16,2432]{1,0:T(8,128)(2,1)S(1)}, bf16[16,2432]{1,0:T(8,128)(2,1)S(1)}, f32[8,128]{1,0:T(8,128)S(1)}) custom-call(s32[8,128]{1,0:T(8,128)} %bitcast.17, bf16[8,128]{1,0:T(8,128)(2,1)} %bitcast.22, bf16[128,2048]{1,0:T(8,128)(2,1)} %tok_hbm.1, bf16[128,2048]{1,0:T(8,128)(2,1)} %grad_hbm.1), custom_call_target="tpu_custom_call" | custom-call | flops 18874368 | bytes 1048576 | tf_op jit(solution)/shard_map/pack/pallas_call | solution.py:268
  2.2 4.1 %collective-permute-start = (bf16[16,2432]{1,0:T(8,128)(2,1)S(1)}, bf16[16,2432]{1,0:T(8,128)(2,1)S(1)}, u32[]{:S(2)}, u32[]{:S(2)}) collective-permute-start(bf16[16,2432]{1,0:T(8,128)(2,1)S(1)} %get-tuple-element.31), channel_id=1, source_target_pairs={{0,8},{2,10},{4,12},{6,14},{8,0},{10,2},{12,4},{14,6},{1,9},{3,11}... | collective-permute-start | bytes 233480 | tf_op jit(solution)/shard_map/ppermute | solution.py:282
  6.3 2.5 %collective-permute-start.5 = (bf16[16,2432]{1,0:T(8,128)(2,1)S(1)}, bf16[16,2432]{1,0:T(8,128)(2,1)S(1)}, u32[]{:S(2)}, u32[]{:S(2)}) collective-permute-start(bf16[16,2432]{1,0:T(8,128)(2,1)S(1)} %get-tuple-element.30.refs_0_), channel_id=1, source_target_pairs={{0,6},{2,4},{4,2},{6,0},{8,14},{10,12},{12,10},{14,8},{1,7},{3,5},... | collective-permute-start | bytes 233480 | tf_op jit(solution)/shard_map/ppermute | solution.py:282
  8.8 0.4 %collective-permute-start.3 = (bf16[16,2432]{1,0:T(8,128)(2,1)S(1)}, bf16[16,2432]{1,0:T(8,128)(2,1)S(1)}, u32[]{:S(2)}, u32[]{:S(2)}) collective-permute-start(bf16[16,2432]{1,0:T(8,128)(2,1)S(1)} %get-tuple-element.30.refs_0_), channel_id=1, source_target_pairs={{0,4},{2,6},{4,0},{6,2},{8,12},{10,14},{12,8},{14,10},{1,5},{3,7},... | collective-permute-start | bytes 233480 | tf_op jit(solution)/shard_map/ppermute | solution.py:282
  9.2 0.5 %collective-permute-start.1 = (bf16[16,2432]{1,0:T(8,128)(2,1)S(1)}, bf16[16,2432]{1,0:T(8,128)(2,1)S(1)}, u32[]{:S(2)}, u32[]{:S(2)}) collective-permute-start(bf16[16,2432]{1,0:T(8,128)(2,1)S(1)} %get-tuple-element.30.refs_0_), channel_id=1, source_target_pairs={{0,2},{2,0},{4,6},{6,4},{8,10},{10,8},{12,14},{14,12},{1,3},{3,1},... | collective-permute-start | bytes 233480 | tf_op jit(solution)/shard_map/ppermute | solution.py:282
  9.8 0.0 collective-permute-done.refs_1_
  9.8 2.5 %collective-permute-start.6 = (bf16[16,2432]{1,0:T(8,128)(2,1)S(1)}, bf16[16,2432]{1,0:T(8,128)(2,1)S(1)}, u32[]{:S(2)}, u32[]{:S(2)}) collective-permute-start(bf16[16,2432]{1,0:T(8,128)(2,1)S(1)} %collective-permute-done.refs_1_), channel_id=1, source_target_pairs={{0,6},{2,4},{4,2},{6,0},{8,14},{10,12},{12,10},{14,8},{1,7},{3,5},... | collective-permute-start | bytes 233480 | tf_op jit(solution)/shard_map/ppermute | solution.py:282
  12.3 0.8 %collective-permute-start.4 = (bf16[16,2432]{1,0:T(8,128)(2,1)S(1)}, bf16[16,2432]{1,0:T(8,128)(2,1)S(1)}, u32[]{:S(2)}, u32[]{:S(2)}) collective-permute-start(bf16[16,2432]{1,0:T(8,128)(2,1)S(1)} %collective-permute-done.refs_1_), channel_id=1, source_target_pairs={{0,4},{2,6},{4,0},{6,2},{8,12},{10,14},{12,8},{14,10},{1,5},{3,7},... | collective-permute-start | bytes 233480 | tf_op jit(solution)/shard_map/ppermute | solution.py:282
  13.2 0.0 collective-permute-done.5.refs_2_.refs_6_
  13.2 0.7 %collective-permute-start.2 = (bf16[16,2432]{1,0:T(8,128)(2,1)S(1)}, bf16[16,2432]{1,0:T(8,128)(2,1)S(1)}, u32[]{:S(2)}, u32[]{:S(2)}) collective-permute-start(bf16[16,2432]{1,0:T(8,128)(2,1)S(1)} %collective-permute-done.refs_1_), channel_id=1, source_target_pairs={{0,2},{2,0},{4,6},{6,4},{8,10},{10,8},{12,14},{14,12},{1,3},{3,1},... | collective-permute-start | bytes 233480 | tf_op jit(solution)/shard_map/ppermute | solution.py:282
  13.9 0.1 collective-permute-done.3.refs_1_.refs_4_
  14.0 0.9 %collective-permute-done.1.refs_0_.refs_2_ = bf16[16,2432]{1,0:T(8,128)(2,1)S(1)} collective-permute-done((bf16[16,2432]{1,0:T(8,128)(2,1)S(1)}, bf16[16,2432]{1,0:T(8,128)(2,1)S(1)}, u32[]{:S(2)}, u32[]{:S(2)}) %collective-permute-start.1) | collective-permute-done | bytes 77856 | tf_op jit(solution)/shard_map/ppermute | solution.py:282
  14.9 2.4 %fetch.1 = (bf16[192,2048]{1,0:T(8,128)(2,1)S(1)}, bf16[192,2048]{1,0:T(8,128)(2,1)S(1)}, bf16[2048,576]{1,0:T(8,128)(2,1)S(1)}) custom-call(bf16[192,2048]{1,0:T(8,128)(2,1)} %bitcast.19, bf16[192,2048]{1,0:T(8,128)(2,1)} %bitcast.20, bf16[192,2048]{1,0:T(8,128)(2,1)} %bitcast.21, bf16[16,2432]{1,0:T(8,128)(2,1)S(1)} %collective-permute-done.1.refs_0_.refs_2_, ...), custom_call_target="tpu_custom_call" | custom-call | bytes 2359296 | tf_op jit(solution)/shard_map/fetch/pallas_call | solution.py:268
  17.3 0.0 collective-permute-done.6.refs_7_
  17.4 0.0 collective-permute-done.4.refs_5_
  17.4 0.2 collective-permute-done.2.refs_3_
  17.6 0.0 copy-start
  17.6 1.2 %expert.1 = (bf16[16,2432]{1,0:T(8,128)(2,1)S(1)}, bf16[16,2432]{1,0:T(8,128)(2,1)S(1)}, bf16[16,2432]{1,0:T(8,128)(2,1)S(1)}, bf16[16,2432]{1,0:T(8,128)(2,1)S(...) custom-call(bf16[16,2432]{1,0:T(8,128)(2,1)S(1)} %get-tuple-element.30.refs_0_, ...), custom_call_target="tpu_custom_call" | custom-call | flops 566231040 | bytes 2359296 | tf_op jit(solution)/shard_map/expert/pallas_call | solution.py:268
  18.8 1.2 %collective-permute-start.9 = (bf16[16,2432]{1,0:T(8,128)(2,1)S(1)}, bf16[16,2432]{1,0:T(8,128)(2,1)S(1)}, u32[]{:S(2)}, u32[]{:S(2)}) collective-permute-start(bf16[16,2432]{1,0:T(8,128)(2,1)S(1)} %get-tuple-element.39), channel_id=1, source_target_pairs={{0,6},{2,4},{4,2},{6,0},{8,14},{10,12},{12,10},{14,8},{1,7},{3,5},... | collective-permute-start | bytes 233480 | tf_op jit(solution)/shard_map/ppermute | solution.py:282
  20.0 1.8 %collective-permute-start.7 = (bf16[16,2432]{1,0:T(8,128)(2,1)S(1)}, bf16[16,2432]{1,0:T(8,128)(2,1)S(1)}, u32[]{:S(2)}, u32[]{:S(2)}) collective-permute-start(bf16[16,2432]{1,0:T(8,128)(2,1)S(1)} %get-tuple-element.36), channel_id=1, source_target_pairs={{0,2},{2,0},{4,6},{6,4},{8,10},{10,8},{12,14},{14,12},{1,3},{3,1},... | collective-permute-start | bytes 233480 | tf_op jit(solution)/shard_map/ppermute | solution.py:282
  21.8 0.5 %collective-permute-start.8 = (bf16[16,2432]{1,0:T(8,128)(2,1)S(1)}, bf16[16,2432]{1,0:T(8,128)(2,1)S(1)}, u32[]{:S(2)}, u32[]{:S(2)}) collective-permute-start(bf16[16,2432]{1,0:T(8,128)(2,1)S(1)} %get-tuple-element.37), channel_id=1, source_target_pairs={{0,4},{2,6},{4,0},{6,2},{8,12},{10,14},{12,8},{14,10},{1,5},{3,7},... | collective-permute-start | bytes 233480 | tf_op jit(solution)/shard_map/ppermute | solution.py:282
  22.3 1.9 %collective-permute-done.9.o3 = bf16[16,2432]{1,0:T(8,128)(2,1)S(1)} collective-permute-done((bf16[16,2432]{1,0:T(8,128)(2,1)S(1)}, bf16[16,2432]{1,0:T(8,128)(2,1)S(1)}, u32[]{:S(2)}, u32[]{:S(2)}) %collective-permute-start.9) | collective-permute-done | bytes 77856 | tf_op jit(solution)/shard_map/ppermute | solution.py:282
  24.2 0.0 collective-permute-start.10
  24.2 0.8 %collective-permute-done.7.o1 = bf16[16,2432]{1,0:T(8,128)(2,1)S(1)} collective-permute-done((bf16[16,2432]{1,0:T(8,128)(2,1)S(1)}, bf16[16,2432]{1,0:T(8,128)(2,1)S(1)}, u32[]{:S(2)}, u32[]{:S(2)}) %collective-permute-start.7) | collective-permute-done | bytes 77856 | tf_op jit(solution)/shard_map/ppermute | solution.py:282
  25.0 1.2 %collective-permute-done.8.o2 = bf16[16,2432]{1,0:T(8,128)(2,1)S(1)} collective-permute-done((bf16[16,2432]{1,0:T(8,128)(2,1)S(1)}, bf16[16,2432]{1,0:T(8,128)(2,1)S(1)}, u32[]{:S(2)}, u32[]{:S(2)}) %collective-permute-start.8) | collective-permute-done | bytes 77856 | tf_op jit(solution)/shard_map/ppermute | solution.py:282
  26.2 2.8 %collective-permute-start.11 = (bf16[8,2432]{1,0:T(8,128)(2,1)S(1)}, bf16[8,2432]{1,0:T(8,128)(2,1)S(1)}, u32[]{:S(2)}, u32[]{:S(2)}) collective-permute-start(bf16[8,2432]{1,0:T(8,128)(2,1)S(1)} %add_convert_fusion), channel_id=1, source_target_pairs={{0,8},{2,10},{4,12},{6,14},{8,0},{10,2},{12,4},{14,6},{1,9},{3,11}... | collective-permute-start | bytes 116744 | tf_op jit(solution)/shard_map/ppermute | solution.py:282
  29.0 0.0 collective-permute-done.10.peer_ref
  29.0 1.6 %weights.1 = (bf16[192,1024]{1,0:T(8,128)(2,1)}, bf16[192,1024]{1,0:T(8,128)(2,1)}, bf16[192,1024]{1,0:T(8,128)(2,1)}) custom-call(bf16[144,1024]{1,0:T(8,128)(2,1)S(1)} %get-tuple-element.41.keep_ref, bf16[144,576]{1,0:T(8,128)(2,1)S(1)} %get-tuple-element.42.hid_ref, bf16[144,1600]{1,0:T(8,128)(2,1)S(1)} %collective-permute-done.10.peer_ref), custom_call_target="tpu_custom_call" | custom-call | flops 339738624 | bytes 1179648 | tf_op jit(solution)/shard_map/weights/pallas_call | solution.py:268
  30.6 1.0 %collective-permute-done.11.rest_0_ = bf16[8,2432]{1,0:T(8,128)(2,1)S(1)} collective-permute-done((bf16[8,2432]{1,0:T(8,128)(2,1)S(1)}, bf16[8,2432]{1,0:T(8,128)(2,1)S(1)}, u32[]{:S(2)}, u32[]{:S(2)}) %collective-permute-start.11) | collective-permute-done | bytes 38944 | tf_op jit(solution)/shard_map/ppermute | solution.py:282
  31.5 0.0 copy-done
  31.5 1.1 %finish.1 = (bf16[128,2048]{1,0:T(8,128)(2,1)}, f32[8,128]{1,0:T(8,128)}) custom-call(s32[8,128]{1,0:T(8,128)S(1)} %bitcast.18, f32[8,128]{1,0:T(8,128)S(1)} %get-tuple-element.29.rank_ref, bf16[16,2432]{1,0:T(8,128)(2,1)S(1)} %get-tuple-element.35.o0, bf16[16,2432]{1,0:T(8,128)(2,1)S(1)} %collective-permute-done.7.o1, ...), custom_call_target="tpu_custom_call" | custom-call | flops 50331648 | bytes 524288 | tf_op jit(solution)/shard_map/finish/pallas_call | solution.py:268
  (1 shorter events, 0.0 us)
Async XLA Ops:
  2.2 7.6 %collective-permute-start = (bf16[16,2432]{1,0:T(8,128)(2,1)S(1)}, bf16[16,2432]{1,0:T(8,128)(2,1)S(1)}, u32[]{:S(2)}, u32[]{:S(2)}) collective-permute-start(bf16[16,2432]{1,0:T(8,128)(2,1)S(1)} %get-tuple-element.31), channel_id=1, source_target_pairs={{0,8},{2,10},{4,12},{6,14},{8,0},{10,2},{12,4},{14,6},{1,9},{3,11}... | collective-permute-start | bytes 233480 | tf_op jit(solution)/shard_map/ppermute | solution.py:282
  6.3 6.9 %collective-permute-start.5 = (bf16[16,2432]{1,0:T(8,128)(2,1)S(1)}, bf16[16,2432]{1,0:T(8,128)(2,1)S(1)}, u32[]{:S(2)}, u32[]{:S(2)}) collective-permute-start(bf16[16,2432]{1,0:T(8,128)(2,1)S(1)} %get-tuple-element.30.refs_0_), channel_id=1, source_target_pairs={{0,6},{2,4},{4,2},{6,0},{8,14},{10,12},{12,10},{14,8},{1,7},{3,5},... | collective-permute-start | bytes 233480 | tf_op jit(solution)/shard_map/ppermute | solution.py:282
  8.8 5.2 %collective-permute-start.3 = (bf16[16,2432]{1,0:T(8,128)(2,1)S(1)}, bf16[16,2432]{1,0:T(8,128)(2,1)S(1)}, u32[]{:S(2)}, u32[]{:S(2)}) collective-permute-start(bf16[16,2432]{1,0:T(8,128)(2,1)S(1)} %get-tuple-element.30.refs_0_), channel_id=1, source_target_pairs={{0,4},{2,6},{4,0},{6,2},{8,12},{10,14},{12,8},{14,10},{1,5},{3,7},... | collective-permute-start | bytes 233480 | tf_op jit(solution)/shard_map/ppermute | solution.py:282
  9.2 5.7 %collective-permute-start.1 = (bf16[16,2432]{1,0:T(8,128)(2,1)S(1)}, bf16[16,2432]{1,0:T(8,128)(2,1)S(1)}, u32[]{:S(2)}, u32[]{:S(2)}) collective-permute-start(bf16[16,2432]{1,0:T(8,128)(2,1)S(1)} %get-tuple-element.30.refs_0_), channel_id=1, source_target_pairs={{0,2},{2,0},{4,6},{6,4},{8,10},{10,8},{12,14},{14,12},{1,3},{3,1},... | collective-permute-start | bytes 233480 | tf_op jit(solution)/shard_map/ppermute | solution.py:282
  9.8 7.5 %collective-permute-start.6 = (bf16[16,2432]{1,0:T(8,128)(2,1)S(1)}, bf16[16,2432]{1,0:T(8,128)(2,1)S(1)}, u32[]{:S(2)}, u32[]{:S(2)}) collective-permute-start(bf16[16,2432]{1,0:T(8,128)(2,1)S(1)} %collective-permute-done.refs_1_), channel_id=1, source_target_pairs={{0,6},{2,4},{4,2},{6,0},{8,14},{10,12},{12,10},{14,8},{1,7},{3,5},... | collective-permute-start | bytes 233480 | tf_op jit(solution)/shard_map/ppermute | solution.py:282
  12.3 5.0 %collective-permute-start.4 = (bf16[16,2432]{1,0:T(8,128)(2,1)S(1)}, bf16[16,2432]{1,0:T(8,128)(2,1)S(1)}, u32[]{:S(2)}, u32[]{:S(2)}) collective-permute-start(bf16[16,2432]{1,0:T(8,128)(2,1)S(1)} %collective-permute-done.refs_1_), channel_id=1, source_target_pairs={{0,4},{2,6},{4,0},{6,2},{8,12},{10,14},{12,8},{14,10},{1,5},{3,7},... | collective-permute-start | bytes 233480 | tf_op jit(solution)/shard_map/ppermute | solution.py:282
  13.2 4.4 %collective-permute-start.2 = (bf16[16,2432]{1,0:T(8,128)(2,1)S(1)}, bf16[16,2432]{1,0:T(8,128)(2,1)S(1)}, u32[]{:S(2)}, u32[]{:S(2)}) collective-permute-start(bf16[16,2432]{1,0:T(8,128)(2,1)S(1)} %collective-permute-done.refs_1_), channel_id=1, source_target_pairs={{0,2},{2,0},{4,6},{6,4},{8,10},{10,8},{12,14},{14,12},{1,3},{3,1},... | collective-permute-start | bytes 233480 | tf_op jit(solution)/shard_map/ppermute | solution.py:282
  17.6 14.0 %copy-start = (s32[128,8]{0,1:T(8,128)S(1)}, s32[128,8]{0,1:T(8,128)}, u32[]{:S(2)}) copy-start(s32[128,8]{0,1:T(8,128)} %param.9) | copy-start | bytes 12292
  18.8 5.4 %collective-permute-start.9 = (bf16[16,2432]{1,0:T(8,128)(2,1)S(1)}, bf16[16,2432]{1,0:T(8,128)(2,1)S(1)}, u32[]{:S(2)}, u32[]{:S(2)}) collective-permute-start(bf16[16,2432]{1,0:T(8,128)(2,1)S(1)} %get-tuple-element.39), channel_id=1, source_target_pairs={{0,6},{2,4},{4,2},{6,0},{8,14},{10,12},{12,10},{14,8},{1,7},{3,5},... | collective-permute-start | bytes 233480 | tf_op jit(solution)/shard_map/ppermute | solution.py:282
  20.0 5.0 %collective-permute-start.7 = (bf16[16,2432]{1,0:T(8,128)(2,1)S(1)}, bf16[16,2432]{1,0:T(8,128)(2,1)S(1)}, u32[]{:S(2)}, u32[]{:S(2)}) collective-permute-start(bf16[16,2432]{1,0:T(8,128)(2,1)S(1)} %get-tuple-element.36), channel_id=1, source_target_pairs={{0,2},{2,0},{4,6},{6,4},{8,10},{10,8},{12,14},{14,12},{1,3},{3,1},... | collective-permute-start | bytes 233480 | tf_op jit(solution)/shard_map/ppermute | solution.py:282
  21.8 4.4 %collective-permute-start.8 = (bf16[16,2432]{1,0:T(8,128)(2,1)S(1)}, bf16[16,2432]{1,0:T(8,128)(2,1)S(1)}, u32[]{:S(2)}, u32[]{:S(2)}) collective-permute-start(bf16[16,2432]{1,0:T(8,128)(2,1)S(1)} %get-tuple-element.37), channel_id=1, source_target_pairs={{0,4},{2,6},{4,0},{6,2},{8,12},{10,14},{12,8},{14,10},{1,5},{3,7},... | collective-permute-start | bytes 233480 | tf_op jit(solution)/shard_map/ppermute | solution.py:282
  24.2 4.8 %collective-permute-start.10 = (bf16[144,1600]{1,0:T(8,128)(2,1)S(1)}, bf16[144,1600]{1,0:T(8,128)(2,1)S(1)}, u32[]{:S(2)}, u32[]{:S(2)}) collective-permute-start(bf16[144,1600]{1,0:T(8,128)(2,1)S(1)} %get-tuple-element.43), channel_id=1, source_target_pairs={{0,1},{1,0},{2,3},{3,2},{4,5},{5,4},{6,7},{7,6},{8,9},{9,8},{10,11... | collective-permute-start | bytes 1382408 | tf_op jit(solution)/shard_map/ppermute | solution.py:345
  26.2 5.3 %collective-permute-start.11 = (bf16[8,2432]{1,0:T(8,128)(2,1)S(1)}, bf16[8,2432]{1,0:T(8,128)(2,1)S(1)}, u32[]{:S(2)}, u32[]{:S(2)}) collective-permute-start(bf16[8,2432]{1,0:T(8,128)(2,1)S(1)} %add_convert_fusion), channel_id=1, source_target_pairs={{0,8},{2,10},{4,12},{6,14},{8,0},{10,2},{12,4},{14,6},{1,9},{3,11}... | collective-permute-start | bytes 116744 | tf_op jit(solution)/shard_map/ppermute | solution.py:282

commit v6 on v5

--- a/solution.py
+++ b/solution.py
@@ -8,6 +8,7 @@
 SPLIT = 4
 MAIN = 8
 TILE = 128
+PIECES = 4
 GROUP = 8
 MIB = 1024 * 1024
 VMEM_LIMIT = 60 * MIB
@@ -38,17 +39,15 @@
 def pack_kernel(picks_hbm, gates_hbm, tok_hbm, grad_hbm, *refs):
     outs, rank_ref = refs[:-6], refs[-6]
     picks_ref, gates_ref, tok_ref, grad_ref, sems = refs[-5:]
-    loads = [
-        pltpu.make_async_copy(src, dst, sems.at[i])
-        for i, (src, dst) in enumerate(
-            [(picks_hbm, picks_ref), (gates_hbm, gates_ref), (tok_hbm, tok_ref), (grad_hbm, grad_ref)]
-        )
+    moves = [
+        (picks_hbm, picks_ref), (gates_hbm, gates_ref), (tok_hbm, tok_ref), (grad_hbm, grad_ref)
     ]
+    loads = [pltpu.make_async_copy(src, dst, sems.at[i]) for i, (src, dst) in enumerate(moves)]
     for load in loads:
         load.start()
     window = len(outs)
-    loads[0].wait()
-    loads[1].wait()
+    for load in loads[:2]:
+        load.wait()
     quad = lax.axis_index("expert") // SPLIT
     picks = picks_ref[...]
     gates = gates_ref[...].astype(F32)
@@ -219,7 +218,7 @@
 
 
 def finish_kernel(picks_ref, rank_ref, o0, o1, o2, o3, *rest):
-    far, (grad_ref, comb_ref) = rest[:-2], rest[-2:]
+    far, (grad_hbm, comb_hbm, grad_ref, comb_ref, sems) = rest[:-5], rest[-5:]
     window = 1 + len(far)
     quad = lax.axis_index("expert") // SPLIT
     picks = picks_ref[...]
@@ -233,7 +232,19 @@
     lasts = [(r == float(MAIN)).astype(F32) for r in ranks]
     blocks = [(0, o[:MAIN, :].astype(F32)) for o in (o0, o1, o2, o3)]
     blocks += [(1 + k, f[...].astype(F32)) for k, f in enumerate(far)]
+    terms = [jnp.zeros((1, toks), F32) for _ in range(window)]
+    for k, v in blocks:
+        note = v[:, features + fold :]
+        terms[k] = terms[k] + jnp.sum(mains[k] * note[:, 0:1], axis=0, keepdims=True)
+        terms[k] = terms[k] + lasts[k] * note[0:1, 1:2]
+    comb = jnp.zeros(picks.shape, F32)
+    for k in range(window):
+        comb = comb + jnp.where(picks == experts[k], terms[k], 0.0)
+    comb_ref[...] = comb
+    stores = [pltpu.make_async_copy(comb_ref, comb_hbm, sems.at[PIECES])]
+    stores[0].start()
     row = iota((MAIN, toks), 0)
+    each = MAIN // PIECES
     for c in range(MAIN):
         cols = slice(c * fold, (c + 1) * fold)
         left, right = [], []
@@ -243,15 +254,15 @@
         left = jnp.concatenate(left, axis=0).astype(BF16)
         right = jnp.concatenate(right, axis=0).astype(BF16)
         grad_ref[:, cols] = dot(left, right, (0, 0)).astype(BF16)
-    terms = [jnp.zeros((1, toks), F32) for _ in range(window)]
-    for k, v in blocks:
-        note = v[:, features + fold :]
-        terms[k] = terms[k] + jnp.sum(mains[k] * note[:, 0:1], axis=0, keepdims=True)
-        terms[k] = terms[k] + lasts[k] * note[0:1, 1:2]
-    comb = jnp.zeros(picks.shape, F32)
-    for k in range(window):
-        comb = comb + jnp.where(picks == experts[k], terms[k], 0.0)
-    comb_ref[...] = comb
+        if c % each == each - 1:
+            done = slice((c + 1 - each) * fold, (c + 1) * fold)
+            store = pltpu.make_async_copy(
+                grad_ref.at[:, done], grad_hbm.at[:, done], sems.at[c // each]
+            )
+            store.start()
+            stores.append(store)
+    for store in stores:
+        store.wait()
 
 
 VM = pl.BlockSpec(memory_space=pltpu.VMEM)
@@ -259,7 +270,7 @@
 ANY = pl.BlockSpec(memory_space=pl.ANY)
 
 
-def call(kernel, outs, name, args, flops, nbytes, room, specs=None, scratch=()):
+def call(kernel, outs, name, args, flops, nbytes, room, specs=None, scratch=(), out_specs=None):
     specs = specs or [VM] * len(args)
     args = [
         pltpu.with_memory_space_constraint(a, pltpu.HBM) if s is HBM else a
@@ -269,7 +280,7 @@
         kernel,
         out_shape=[jax.ShapeDtypeStruct(s, t) for s, t in outs],
         in_specs=specs,
-        out_specs=[VM] * len(outs),
+        out_specs=out_specs or [VM] * len(outs),
         scratch_shapes=list(scratch),
         compiler_params=pltpu.CompilerParams(vmem_limit_bytes=min(VMEM_LIMIT, room * MIB)),
         cost_estimate=pl.CostEstimate(flops=flops, bytes_accessed=nbytes, transcendentals=0),
@@ -313,11 +324,11 @@
         fetch_kernel,
         [(wg.shape, BF16), (wu.shape, BF16), ((features, 3 * hidden), BF16)],
         "fetch",
-        (wg, wu, wd, *near[1:]),
+        (wg, wu, wd, near[-1]),
         0,
         6 * features * hidden,
         12,
-        [HBM] * 3 + [ANY] * (SPLIT - 1),
+        [HBM] * 3 + [ANY],
         [pltpu.VMEM(wd.shape, BF16), pltpu.SemaphoreType.DMA((3,))],
     )
     from_far = arrived[0] if window == 2 else jnp.concatenate(arrived, axis=0)
@@ -367,6 +378,12 @@
         2 * toks * features * 16 * (SPLIT + window),
         2 * toks * features,
         6 + window,
+        scratch=[
+            pltpu.VMEM((toks, features), BF16),
+            pltpu.VMEM((choices.shape[1], toks), F32),
+            pltpu.SemaphoreType.DMA((PIECES + 1,)),
+        ],
+        out_specs=[HBM, HBM],
     )
     return (
         in_grad,

time: 32.9 us -> 32.6 us (level)
  waiting for transfers between devices: 6.06 us -> 5.58 us
    ppermute x11, waiting for transfers between devices: 6.06 us -> 5.58 us  [swap_by(): return lax.ppermute(block, 'expert', [(i, i ^ mask) for i in range(count)])]
  transfers between devices with their start and end apart: 12 -> 12, of which waited for: 7 -> 6; matrix products, arithmetic and copies ran while one was open for 0% -> 0% of each run, Pallas kernels for 12% -> 12%
where the time goes in v6:
time: 32.6 us; the launch traced here: 32.4 us
  starting transfers between devices  18.3 us (56%)
  Pallas kernels  7.81 us (24%)
  waiting for transfers between devices  5.58 us (17%)
  between operations  0.69 us (2%)
    ppermute x11, starting transfers between devices, swap_by(): return lax.ppermute(block, 'expert', [(i, i ^ mask) for i in range(count)])  18.3 us
    pallas_call x5, Pallas kernels, call(): pl.pallas_call(kernel, out_shape=[jax.ShapeDtypeStruct(s, t) for s, t in...  7.81 us
    ppermute x11, waiting for transfers between devices, swap_by(): return lax.ppermute(block, 'expert', [(i, i ^ mask) for i in range(count)])  5.58 us
  transfers between devices with their start and end apart: 12, of which 6 were waited for; matrix products, arithmetic and copies ran while one was open for 0% of the time, Pallas kernels for 12%

profile of v6, /device:TPU:0, one launch (start us, length us, event | category | flops | bytes accessed | tf_op | source)
XLA Modules:
  0.0 32.4 jit_solution(7777520363900897025)
XLA Ops:
  0.6 1.5 %pack.1 = (bf16[16,2432]{1,0:T(8,128)(2,1)S(1)}, bf16[16,2432]{1,0:T(8,128)(2,1)S(1)}, f32[8,128]{1,0:T(8,128)S(1)}) custom-call(s32[8,128]{1,0:T(8,128)} %bitcast.17, bf16[8,128]{1,0:T(8,128)(2,1)} %bitcast.22, bf16[128,2048]{1,0:T(8,128)(2,1)} %tok_hbm.1, bf16[128,2048]{1,0:T(8,128)(2,1)} %grad_hbm.1), custom_call_target="tpu_custom_call" | custom-call | flops 18874368 | bytes 1048576 | tf_op jit(solution)/shard_map/pack/pallas_call | solution.py:279
  2.2 4.1 %collective-permute-start = (bf16[16,2432]{1,0:T(8,128)(2,1)S(1)}, bf16[16,2432]{1,0:T(8,128)(2,1)S(1)}, u32[]{:S(2)}, u32[]{:S(2)}) collective-permute-start(bf16[16,2432]{1,0:T(8,128)(2,1)S(1)} %get-tuple-element.31), channel_id=1, source_target_pairs={{0,8},{2,10},{4,12},{6,14},{8,0},{10,2},{12,4},{14,6},{1,9},{3,11}... | collective-permute-start | bytes 233480 | tf_op jit(solution)/shard_map/ppermute | solution.py:293
  6.3 2.5 %collective-permute-start.5 = (bf16[16,2432]{1,0:T(8,128)(2,1)S(1)}, bf16[16,2432]{1,0:T(8,128)(2,1)S(1)}, u32[]{:S(2)}, u32[]{:S(2)}) collective-permute-start(bf16[16,2432]{1,0:T(8,128)(2,1)S(1)} %get-tuple-element.30.refs_0_), channel_id=1, source_target_pairs={{0,6},{2,4},{4,2},{6,0},{8,14},{10,12},{12,10},{14,8},{1,7},{3,5},... | collective-permute-start | bytes 233480 | tf_op jit(solution)/shard_map/ppermute | solution.py:293
  8.8 0.4 %collective-permute-start.3 = (bf16[16,2432]{1,0:T(8,128)(2,1)S(1)}, bf16[16,2432]{1,0:T(8,128)(2,1)S(1)}, u32[]{:S(2)}, u32[]{:S(2)}) collective-permute-start(bf16[16,2432]{1,0:T(8,128)(2,1)S(1)} %get-tuple-element.30.refs_0_), channel_id=1, source_target_pairs={{0,4},{2,6},{4,0},{6,2},{8,12},{10,14},{12,8},{14,10},{1,5},{3,7},... | collective-permute-start | bytes 233480 | tf_op jit(solution)/shard_map/ppermute | solution.py:293
  9.2 0.5 %collective-permute-start.1 = (bf16[16,2432]{1,0:T(8,128)(2,1)S(1)}, bf16[16,2432]{1,0:T(8,128)(2,1)S(1)}, u32[]{:S(2)}, u32[]{:S(2)}) collective-permute-start(bf16[16,2432]{1,0:T(8,128)(2,1)S(1)} %get-tuple-element.30.refs_0_), channel_id=1, source_target_pairs={{0,2},{2,0},{4,6},{6,4},{8,10},{10,8},{12,14},{14,12},{1,3},{3,1},... | collective-permute-start | bytes 233480 | tf_op jit(solution)/shard_map/ppermute | solution.py:293
  9.8 0.0 collective-permute-done.refs_1_
  9.8 2.5 %collective-permute-start.6 = (bf16[16,2432]{1,0:T(8,128)(2,1)S(1)}, bf16[16,2432]{1,0:T(8,128)(2,1)S(1)}, u32[]{:S(2)}, u32[]{:S(2)}) collective-permute-start(bf16[16,2432]{1,0:T(8,128)(2,1)S(1)} %collective-permute-done.refs_1_), channel_id=1, source_target_pairs={{0,6},{2,4},{4,2},{6,0},{8,14},{10,12},{12,10},{14,8},{1,7},{3,5},... | collective-permute-start | bytes 233480 | tf_op jit(solution)/shard_map/ppermute | solution.py:293
  12.3 0.8 %collective-permute-start.4 = (bf16[16,2432]{1,0:T(8,128)(2,1)S(1)}, bf16[16,2432]{1,0:T(8,128)(2,1)S(1)}, u32[]{:S(2)}, u32[]{:S(2)}) collective-permute-start(bf16[16,2432]{1,0:T(8,128)(2,1)S(1)} %collective-permute-done.refs_1_), channel_id=1, source_target_pairs={{0,4},{2,6},{4,0},{6,2},{8,12},{10,14},{12,8},{14,10},{1,5},{3,7},... | collective-permute-start | bytes 233480 | tf_op jit(solution)/shard_map/ppermute | solution.py:293
  13.2 0.0 collective-permute-done.5.refs_0_.refs_6_
  13.2 0.7 %collective-permute-start.2 = (bf16[16,2432]{1,0:T(8,128)(2,1)S(1)}, bf16[16,2432]{1,0:T(8,128)(2,1)S(1)}, u32[]{:S(2)}, u32[]{:S(2)}) collective-permute-start(bf16[16,2432]{1,0:T(8,128)(2,1)S(1)} %collective-permute-done.refs_1_), channel_id=1, source_target_pairs={{0,2},{2,0},{4,6},{6,4},{8,10},{10,8},{12,14},{14,12},{1,3},{3,1},... | collective-permute-start | bytes 233480 | tf_op jit(solution)/shard_map/ppermute | solution.py:293
  13.9 2.4 %fetch.1 = (bf16[192,2048]{1,0:T(8,128)(2,1)S(1)}, bf16[192,2048]{1,0:T(8,128)(2,1)S(1)}, bf16[2048,576]{1,0:T(8,128)(2,1)S(1)}) custom-call(bf16[192,2048]{1,0:T(8,128)(2,1)} %bitcast.19, bf16[192,2048]{1,0:T(8,128)(2,1)} %bitcast.20, bf16[192,2048]{1,0:T(8,128)(2,1)} %bitcast.21, bf16[16,2432]{1,0:T(8,128)(2,1)S(1)} %collective-permute-done.5.refs_0_.refs_6_), custom_call_target="tpu_custom_call" | custom-call | bytes 2359296 | tf_op jit(solution)/shard_map/fetch/pallas_call | solution.py:279
  16.4 0.0 collective-permute-done.3.refs_4_
  16.4 0.0 collective-permute-done.1.refs_2_
  16.4 0.0 collective-permute-done.6.refs_7_
  16.4 0.3 collective-permute-done.4.refs_5_
  16.7 0.8 %collective-permute-done.2.refs_3_ = bf16[16,2432]{1,0:T(8,128)(2,1)S(1)} collective-permute-done((bf16[16,2432]{1,0:T(8,128)(2,1)S(1)}, bf16[16,2432]{1,0:T(8,128)(2,1)S(1)}, u32[]{:S(2)}, u32[]{:S(2)}) %collective-permute-start.2) | collective-permute-done | bytes 77856 | tf_op jit(solution)/shard_map/ppermute | solution.py:293
  17.6 0.0 copy-start
  17.6 1.2 %expert.1 = (bf16[16,2432]{1,0:T(8,128)(2,1)S(1)}, bf16[16,2432]{1,0:T(8,128)(2,1)S(1)}, bf16[16,2432]{1,0:T(8,128)(2,1)S(1)}, bf16[16,2432]{1,0:T(8,128)(2,1)S(...) custom-call(bf16[16,2432]{1,0:T(8,128)(2,1)S(1)} %get-tuple-element.30.refs_0_, ...), custom_call_target="tpu_custom_call" | custom-call | flops 566231040 | bytes 2359296 | tf_op jit(solution)/shard_map/expert/pallas_call | solution.py:279
  18.8 1.2 %collective-permute-start.9 = (bf16[16,2432]{1,0:T(8,128)(2,1)S(1)}, bf16[16,2432]{1,0:T(8,128)(2,1)S(1)}, u32[]{:S(2)}, u32[]{:S(2)}) collective-permute-start(bf16[16,2432]{1,0:T(8,128)(2,1)S(1)} %get-tuple-element.39), channel_id=1, source_target_pairs={{0,6},{2,4},{4,2},{6,0},{8,14},{10,12},{12,10},{14,8},{1,7},{3,5},... | collective-permute-start | bytes 233480 | tf_op jit(solution)/shard_map/ppermute | solution.py:293
  20.0 1.5 %collective-permute-start.7 = (bf16[16,2432]{1,0:T(8,128)(2,1)S(1)}, bf16[16,2432]{1,0:T(8,128)(2,1)S(1)}, u32[]{:S(2)}, u32[]{:S(2)}) collective-permute-start(bf16[16,2432]{1,0:T(8,128)(2,1)S(1)} %get-tuple-element.36), channel_id=1, source_target_pairs={{0,2},{2,0},{4,6},{6,4},{8,10},{10,8},{12,14},{14,12},{1,3},{3,1},... | collective-permute-start | bytes 233480 | tf_op jit(solution)/shard_map/ppermute | solution.py:293
  21.5 0.8 %collective-permute-start.8 = (bf16[16,2432]{1,0:T(8,128)(2,1)S(1)}, bf16[16,2432]{1,0:T(8,128)(2,1)S(1)}, u32[]{:S(2)}, u32[]{:S(2)}) collective-permute-start(bf16[16,2432]{1,0:T(8,128)(2,1)S(1)} %get-tuple-element.37), channel_id=1, source_target_pairs={{0,4},{2,6},{4,0},{6,2},{8,12},{10,14},{12,8},{14,10},{1,5},{3,7},... | collective-permute-start | bytes 233480 | tf_op jit(solution)/shard_map/ppermute | solution.py:293
  22.3 1.9 %collective-permute-done.9.o3 = bf16[16,2432]{1,0:T(8,128)(2,1)S(1)} collective-permute-done((bf16[16,2432]{1,0:T(8,128)(2,1)S(1)}, bf16[16,2432]{1,0:T(8,128)(2,1)S(1)}, u32[]{:S(2)}, u32[]{:S(2)}) %collective-permute-start.9) | collective-permute-done | bytes 77856 | tf_op jit(solution)/shard_map/ppermute | solution.py:293
  24.2 0.0 collective-permute-start.10
  24.2 0.8 %collective-permute-done.7.o1 = bf16[16,2432]{1,0:T(8,128)(2,1)S(1)} collective-permute-done((bf16[16,2432]{1,0:T(8,128)(2,1)S(1)}, bf16[16,2432]{1,0:T(8,128)(2,1)S(1)}, u32[]{:S(2)}, u32[]{:S(2)}) %collective-permute-start.7) | collective-permute-done | bytes 77856 | tf_op jit(solution)/shard_map/ppermute | solution.py:293
  25.0 0.9 %collective-permute-done.8.o2 = bf16[16,2432]{1,0:T(8,128)(2,1)S(1)} collective-permute-done((bf16[16,2432]{1,0:T(8,128)(2,1)S(1)}, bf16[16,2432]{1,0:T(8,128)(2,1)S(1)}, u32[]{:S(2)}, u32[]{:S(2)}) %collective-permute-start.8) | collective-permute-done | bytes 77856 | tf_op jit(solution)/shard_map/ppermute | solution.py:293
  25.9 3.1 %collective-permute-start.11 = (bf16[8,2432]{1,0:T(8,128)(2,1)S(1)}, bf16[8,2432]{1,0:T(8,128)(2,1)S(1)}, u32[]{:S(2)}, u32[]{:S(2)}) collective-permute-start(bf16[8,2432]{1,0:T(8,128)(2,1)S(1)} %add_convert_fusion), channel_id=1, source_target_pairs={{0,8},{2,10},{4,12},{6,14},{8,0},{10,2},{12,4},{14,6},{1,9},{3,11}... | collective-permute-start | bytes 116744 | tf_op jit(solution)/shard_map/ppermute | solution.py:293
  29.0 0.0 collective-permute-done.10.peer_ref
  29.0 1.6 %weights.1 = (bf16[192,1024]{1,0:T(8,128)(2,1)}, bf16[192,1024]{1,0:T(8,128)(2,1)}, bf16[192,1024]{1,0:T(8,128)(2,1)}) custom-call(bf16[144,1024]{1,0:T(8,128)(2,1)S(1)} %get-tuple-element.41.keep_ref, bf16[144,576]{1,0:T(8,128)(2,1)S(1)} %get-tuple-element.42.hid_ref, bf16[144,1600]{1,0:T(8,128)(2,1)S(1)} %collective-permute-done.10.peer_ref), custom_call_target="tpu_custom_call" | custom-call | flops 339738624 | bytes 1179648 | tf_op jit(solution)/shard_map/weights/pallas_call | solution.py:279
  30.5 0.8 %collective-permute-done.11.rest_0_ = bf16[8,2432]{1,0:T(8,128)(2,1)S(1)} collective-permute-done((bf16[8,2432]{1,0:T(8,128)(2,1)S(1)}, bf16[8,2432]{1,0:T(8,128)(2,1)S(1)}, u32[]{:S(2)}, u32[]{:S(2)}) %collective-permute-start.11) | collective-permute-done | bytes 38944 | tf_op jit(solution)/shard_map/ppermute | solution.py:293
  31.3 0.0 copy-done
  31.3 1.1 %finish.1 = (bf16[128,2048]{1,0:T(8,128)(2,1)}, f32[8,128]{1,0:T(8,128)}) custom-call(s32[8,128]{1,0:T(8,128)S(1)} %bitcast.18, f32[8,128]{1,0:T(8,128)S(1)} %get-tuple-element.29.rank_ref, bf16[16,2432]{1,0:T(8,128)(2,1)S(1)} %get-tuple-element.35.o0, bf16[16,2432]{1,0:T(8,128)(2,1)S(1)} %collective-permute-done.7.o1, ...), custom_call_target="tpu_custom_call" | custom-call | flops 50331648 | bytes 524288 | tf_op jit(solution)/shard_map/finish/pallas_call | solution.py:279
  (1 shorter events, 0.0 us)
Async XLA Ops:
  2.2 7.6 %collective-permute-start = (bf16[16,2432]{1,0:T(8,128)(2,1)S(1)}, bf16[16,2432]{1,0:T(8,128)(2,1)S(1)}, u32[]{:S(2)}, u32[]{:S(2)}) collective-permute-start(bf16[16,2432]{1,0:T(8,128)(2,1)S(1)} %get-tuple-element.31), channel_id=1, source_target_pairs={{0,8},{2,10},{4,12},{6,14},{8,0},{10,2},{12,4},{14,6},{1,9},{3,11}... | collective-permute-start | bytes 233480 | tf_op jit(solution)/shard_map/ppermute | solution.py:293
  6.3 6.9 %collective-permute-start.5 = (bf16[16,2432]{1,0:T(8,128)(2,1)S(1)}, bf16[16,2432]{1,0:T(8,128)(2,1)S(1)}, u32[]{:S(2)}, u32[]{:S(2)}) collective-permute-start(bf16[16,2432]{1,0:T(8,128)(2,1)S(1)} %get-tuple-element.30.refs_0_), channel_id=1, source_target_pairs={{0,6},{2,4},{4,2},{6,0},{8,14},{10,12},{12,10},{14,8},{1,7},{3,5},... | collective-permute-start | bytes 233480 | tf_op jit(solution)/shard_map/ppermute | solution.py:293
  8.8 7.6 %collective-permute-start.3 = (bf16[16,2432]{1,0:T(8,128)(2,1)S(1)}, bf16[16,2432]{1,0:T(8,128)(2,1)S(1)}, u32[]{:S(2)}, u32[]{:S(2)}) collective-permute-start(bf16[16,2432]{1,0:T(8,128)(2,1)S(1)} %get-tuple-element.30.refs_0_), channel_id=1, source_target_pairs={{0,4},{2,6},{4,0},{6,2},{8,12},{10,14},{12,8},{14,10},{1,5},{3,7},... | collective-permute-start | bytes 233480 | tf_op jit(solution)/shard_map/ppermute | solution.py:293
  9.2 7.2 %collective-permute-start.1 = (bf16[16,2432]{1,0:T(8,128)(2,1)S(1)}, bf16[16,2432]{1,0:T(8,128)(2,1)S(1)}, u32[]{:S(2)}, u32[]{:S(2)}) collective-permute-start(bf16[16,2432]{1,0:T(8,128)(2,1)S(1)} %get-tuple-element.30.refs_0_), channel_id=1, source_target_pairs={{0,2},{2,0},{4,6},{6,4},{8,10},{10,8},{12,14},{14,12},{1,3},{3,1},... | collective-permute-start | bytes 233480 | tf_op jit(solution)/shard_map/ppermute | solution.py:293
  9.8 6.6 %collective-permute-start.6 = (bf16[16,2432]{1,0:T(8,128)(2,1)S(1)}, bf16[16,2432]{1,0:T(8,128)(2,1)S(1)}, u32[]{:S(2)}, u32[]{:S(2)}) collective-permute-start(bf16[16,2432]{1,0:T(8,128)(2,1)S(1)} %collective-permute-done.refs_1_), channel_id=1, source_target_pairs={{0,6},{2,4},{4,2},{6,0},{8,14},{10,12},{12,10},{14,8},{1,7},{3,5},... | collective-permute-start | bytes 233480 | tf_op jit(solution)/shard_map/ppermute | solution.py:293
  12.3 4.4 %collective-permute-start.4 = (bf16[16,2432]{1,0:T(8,128)(2,1)S(1)}, bf16[16,2432]{1,0:T(8,128)(2,1)S(1)}, u32[]{:S(2)}, u32[]{:S(2)}) collective-permute-start(bf16[16,2432]{1,0:T(8,128)(2,1)S(1)} %collective-permute-done.refs_1_), channel_id=1, source_target_pairs={{0,4},{2,6},{4,0},{6,2},{8,12},{10,14},{12,8},{14,10},{1,5},{3,7},... | collective-permute-start | bytes 233480 | tf_op jit(solution)/shard_map/ppermute | solution.py:293
  13.2 4.4 %collective-permute-start.2 = (bf16[16,2432]{1,0:T(8,128)(2,1)S(1)}, bf16[16,2432]{1,0:T(8,128)(2,1)S(1)}, u32[]{:S(2)}, u32[]{:S(2)}) collective-permute-start(bf16[16,2432]{1,0:T(8,128)(2,1)S(1)} %collective-permute-done.refs_1_), channel_id=1, source_target_pairs={{0,2},{2,0},{4,6},{6,4},{8,10},{10,8},{12,14},{14,12},{1,3},{3,1},... | collective-permute-start | bytes 233480 | tf_op jit(solution)/shard_map/ppermute | solution.py:293
  17.6 13.8 %copy-start = (s32[128,8]{0,1:T(8,128)S(1)}, s32[128,8]{0,1:T(8,128)}, u32[]{:S(2)}) copy-start(s32[128,8]{0,1:T(8,128)} %param.9) | copy-start | bytes 12292
  18.8 5.4 %collective-permute-start.9 = (bf16[16,2432]{1,0:T(8,128)(2,1)S(1)}, bf16[16,2432]{1,0:T(8,128)(2,1)S(1)}, u32[]{:S(2)}, u32[]{:S(2)}) collective-permute-start(bf16[16,2432]{1,0:T(8,128)(2,1)S(1)} %get-tuple-element.39), channel_id=1, source_target_pairs={{0,6},{2,4},{4,2},{6,0},{8,14},{10,12},{12,10},{14,8},{1,7},{3,5},... | collective-permute-start | bytes 233480 | tf_op jit(solution)/shard_map/ppermute | solution.py:293
  20.0 5.0 %collective-permute-start.7 = (bf16[16,2432]{1,0:T(8,128)(2,1)S(1)}, bf16[16,2432]{1,0:T(8,128)(2,1)S(1)}, u32[]{:S(2)}, u32[]{:S(2)}) collective-permute-start(bf16[16,2432]{1,0:T(8,128)(2,1)S(1)} %get-tuple-element.36), channel_id=1, source_target_pairs={{0,2},{2,0},{4,6},{6,4},{8,10},{10,8},{12,14},{14,12},{1,3},{3,1},... | collective-permute-start | bytes 233480 | tf_op jit(solution)/shard_map/ppermute | solution.py:293
  21.5 4.4 %collective-permute-start.8 = (bf16[16,2432]{1,0:T(8,128)(2,1)S(1)}, bf16[16,2432]{1,0:T(8,128)(2,1)S(1)}, u32[]{:S(2)}, u32[]{:S(2)}) collective-permute-start(bf16[16,2432]{1,0:T(8,128)(2,1)S(1)} %get-tuple-element.37), channel_id=1, source_target_pairs={{0,4},{2,6},{4,0},{6,2},{8,12},{10,14},{12,8},{14,10},{1,5},{3,7},... | collective-permute-start | bytes 233480 | tf_op jit(solution)/shard_map/ppermute | solution.py:293
  24.2 4.8 %collective-permute-start.10 = (bf16[144,1600]{1,0:T(8,128)(2,1)S(1)}, bf16[144,1600]{1,0:T(8,128)(2,1)S(1)}, u32[]{:S(2)}, u32[]{:S(2)}) collective-permute-start(bf16[144,1600]{1,0:T(8,128)(2,1)S(1)} %get-tuple-element.43), channel_id=1, source_target_pairs={{0,1},{1,0},{2,3},{3,2},{4,5},{5,4},{6,7},{7,6},{8,9},{9,8},{10,11... | collective-permute-start | bytes 1382408 | tf_op jit(solution)/shard_map/ppermute | solution.py:356
  25.9 5.4 %collective-permute-start.11 = (bf16[8,2432]{1,0:T(8,128)(2,1)S(1)}, bf16[8,2432]{1,0:T(8,128)(2,1)S(1)}, u32[]{:S(2)}, u32[]{:S(2)}) collective-permute-start(bf16[8,2432]{1,0:T(8,128)(2,1)S(1)} %add_convert_fusion), channel_id=1, source_target_pairs={{0,8},{2,10},{4,12},{6,14},{8,0},{10,2},{12,4},{14,6},{1,9},{3,11}... | collective-permute-start | bytes 116744 | tf_op jit(solution)/shard_map/ppermute | solution.py:293

commit v7 on v6

--- a/solution.py
+++ b/solution.py
@@ -1,3 +1,5 @@
+import functools
+
 import jax
 import jax.numpy as jnp
 from jax import lax
@@ -104,9 +106,9 @@
         across_ref[:, i * hidden : (i + 1) * hidden] = ref[...].T
 
 
-def expert_kernel(*refs):
-    wg_ref, wu_ref, across_ref, m0, m1, m2, m3, keep_ref, hid_ref, send_ref = refs[-10:]
-    zs, ms = refs[:-10], (m0, m1, m2, m3)
+def expert_kernel(inputs, *refs):
+    wg_ref, wu_ref, across_ref = refs[inputs : inputs + 3]
+    zs, ms, (keep_ref, hid_ref, send_ref) = refs[:inputs], refs[inputs + 3 : -3], refs[-3:]
     features = wg_ref.shape[1]
     hidden = wg_ref.shape[0]
     fold = features // MAIN
@@ -121,7 +123,6 @@
     def work(g):
         if groups == 1:
             src = slice(0, rows_in)
-            dst = slice(0, per * MAIN)
             all_rows = slice(0, (GROUP + 1) * pair)
         else:
             src = pl.ds(pl.multiple_of(g * rows_in, rows_in), rows_in)
@@ -177,13 +178,14 @@
                     jnp.where(lane == 1, combine[at : at + 1], 0.0),
                 )
             )
-        for j, m in enumerate(ms):
-            span = slice(j * per * MAIN, (j + 1) * per * MAIN)
+        for i, m in enumerate(ms):
+            if groups == 1:
+                dst = slice(0, m.shape[0])
+            at, size = (i, m.shape[0] // MAIN) if groups == 1 else (i * per, per)
+            span = slice(at * MAIN, (at + size) * MAIN)
             m[dst, :features] = part[span].astype(BF16)
             m[dst, features : features + fold] = folded[span].astype(BF16)
-            m[dst, features + fold :] = jnp.concatenate(
-                notes[j * per : (j + 1) * per], axis=0
-            ).astype(BF16)
+            m[dst, features + fold :] = jnp.concatenate(notes[at : at + size], axis=0).astype(BF16)
         none = jnp.zeros((pieces, MAIN, hidden), F32)
 
         def lay(v, place):
@@ -340,9 +342,12 @@
         zs = [jnp.concatenate(pair, axis=0) for pair in pairs]
 
     all_rows = groups * (GROUP + 1) * 2 * MAIN
+    kinds = [((MAIN, width), BF16)] * (GROUP - 2) + [((2 * MAIN, width), BF16)]
+    if groups > 1:
+        kinds = [((window * MAIN, width), BF16)] * SPLIT
     *messages, keep, hid, send = call(
-        expert_kernel,
-        [((window * MAIN, width), BF16)] * SPLIT
+        functools.partial(expert_kernel, len(zs)),
+        kinds
         + [((all_rows, half), BF16), ((all_rows, 3 * hidden), BF16), ((all_rows, half + 3 * hidden), BF16)],
         "expert",
         (*zs, *held),
@@ -350,10 +355,18 @@
         6 * features * hidden,
         10 + 6 * groups,
     )
-    back = [messages[0]] + [swap_by(messages[j], j) for j in range(1, SPLIT)]
+    if groups == 1:
+        home, away = messages[:-1:2], messages[1:-1:2]
+    else:
+        home, away = [m[:MAIN] for m in messages[:-1]], [m[MAIN:] for m in messages[:-1]]
+    both = swap_by(messages[-1], SPLIT - 1)
+    back = [away[0]] + [swap_by(away[j], j) for j in range(1, SPLIT - 1)] + [both]
+    home = [home[0]] + [swap_by(home[j], j) for j in range(1, SPLIT - 1)]
     send, first = lax.optimization_barrier((send, back[-1]))
     back[-1] = first
     peer = lax.ppermute(send, "dp", [(0, 1), (1, 0)])
+    peer, *rest = lax.optimization_barrier((peer, *home[:0:-1]))
+    home = home[:1] + rest[::-1]
     gate_grad, up_grad, down_grad = call(
         weights_kernel,
         [((hidden, half), BF16)] * 3,
@@ -363,7 +376,8 @@
         6 * half * hidden,
         6 + 2 * groups,
     )
-    total = sum(b[MAIN:].astype(F32) for b in back[::-1]).astype(BF16)
+    *parts, both = back
+    total = sum([b.astype(F32) for b in parts[::-1]], both[MAIN:].astype(F32)).astype(BF16)
     homes = [
         swap_by(total[k * MAIN : (k + 1) * MAIN], SPLIT * (k + 1)) for k in range(window - 1)
     ]
@@ -374,7 +388,7 @@
         finish_kernel,
         [((toks, features), BF16), ((choices.shape[1], toks), F32)],
         "finish",
-        (picks, ranks, *back, *homes),
+        (picks, ranks, *home, both, *homes),
         2 * toks * features * 16 * (SPLIT + window),
         2 * toks * features,
         6 + window,

time: 32.6 us -> 32.1 us (0.985)
  waiting for transfers between devices: 5.58 us -> 3.66 us
  starting transfers between devices: 18.3 us -> 19.7 us
    ppermute x11 -> x13, waiting for transfers between devices: 5.58 us -> 3.66 us  [swap_by(): return lax.ppermute(block, 'expert', [(i, i ^ mask) for i in range(count)])]
    ppermute x11 -> x13, starting transfers between devices: 18.3 us -> 19.7 us  [swap_by(): return lax.ppermute(block, 'expert', [(i, i ^ mask) for i in range(count)])]
  transfers between devices with their start and end apart: 12 -> 14, of which waited for: 6 -> 6; matrix products, arithmetic and copies ran while one was open for 0% -> 0% of each run, Pallas kernels for 12% -> 13%
where the time goes in v7:
time: 32.1 us; the launch traced here: 31.9 us
  starting transfers between devices  19.7 us (61%)
  Pallas kernels  7.81 us (24%)
  waiting for transfers between devices  3.66 us (11%)
  between operations  0.7 us (2%)
    ppermute x13, starting transfers between devices, swap_by(): return lax.ppermute(block, 'expert', [(i, i ^ mask) for i in range(count)])  19.7 us
    pallas_call x5, Pallas kernels, call(): pl.pallas_call(kernel, out_shape=[jax.ShapeDtypeStruct(s, t) for s, t in...  7.81 us
    ppermute x13, waiting for transfers between devices, swap_by(): return lax.ppermute(block, 'expert', [(i, i ^ mask) for i in range(count)])  3.66 us
  transfers between devices with their start and end apart: 14, of which 6 were waited for; matrix products, arithmetic and copies ran while one was open for 0% of the time, Pallas kernels for 13%

profile of v7, /device:TPU:0, one launch (start us, length us, event | category | flops | bytes accessed | tf_op | source)
XLA Modules:
  0.0 31.9 jit_solution(18186245409263229063)
XLA Ops:
  0.6 1.5 %pack.1 = (bf16[16,2432]{1,0:T(8,128)(2,1)S(1)}, bf16[16,2432]{1,0:T(8,128)(2,1)S(1)}, f32[8,128]{1,0:T(8,128)S(1)}) custom-call(s32[8,128]{1,0:T(8,128)} %bitcast.17, bf16[8,128]{1,0:T(8,128)(2,1)} %bitcast.22, bf16[128,2048]{1,0:T(8,128)(2,1)} %tok_hbm.1, bf16[128,2048]{1,0:T(8,128)(2,1)} %grad_hbm.1), custom_call_target="tpu_custom_call" | custom-call | flops 18874368 | bytes 1048576 | tf_op jit(solution)/shard_map/pack/pallas_call | solution.py:281
  2.2 4.1 %collective-permute-start = (bf16[16,2432]{1,0:T(8,128)(2,1)S(1)}, bf16[16,2432]{1,0:T(8,128)(2,1)S(1)}, u32[]{:S(2)}, u32[]{:S(2)}) collective-permute-start(bf16[16,2432]{1,0:T(8,128)(2,1)S(1)} %get-tuple-element.37), channel_id=1, source_target_pairs={{0,8},{2,10},{4,12},{6,14},{8,0},{10,2},{12,4},{14,6},{1,9},{3,11}... | collective-permute-start | bytes 233480 | tf_op jit(solution)/shard_map/ppermute | solution.py:295
  6.3 2.5 %collective-permute-start.5 = (bf16[16,2432]{1,0:T(8,128)(2,1)S(1)}, bf16[16,2432]{1,0:T(8,128)(2,1)S(1)}, u32[]{:S(2)}, u32[]{:S(2)}) collective-permute-start(bf16[16,2432]{1,0:T(8,128)(2,1)S(1)} %get-tuple-element.36.refs_0_), channel_id=1, source_target_pairs={{0,6},{2,4},{4,2},{6,0},{8,14},{10,12},{12,10},{14,8},{1,7},{3,5},... | collective-permute-start | bytes 233480 | tf_op jit(solution)/shard_map/ppermute | solution.py:295
  8.8 0.4 %collective-permute-start.3 = (bf16[16,2432]{1,0:T(8,128)(2,1)S(1)}, bf16[16,2432]{1,0:T(8,128)(2,1)S(1)}, u32[]{:S(2)}, u32[]{:S(2)}) collective-permute-start(bf16[16,2432]{1,0:T(8,128)(2,1)S(1)} %get-tuple-element.36.refs_0_), channel_id=1, source_target_pairs={{0,4},{2,6},{4,0},{6,2},{8,12},{10,14},{12,8},{14,10},{1,5},{3,7},... | collective-permute-start | bytes 233480 | tf_op jit(solution)/shard_map/ppermute | solution.py:295
  9.2 0.5 %collective-permute-start.1 = (bf16[16,2432]{1,0:T(8,128)(2,1)S(1)}, bf16[16,2432]{1,0:T(8,128)(2,1)S(1)}, u32[]{:S(2)}, u32[]{:S(2)}) collective-permute-start(bf16[16,2432]{1,0:T(8,128)(2,1)S(1)} %get-tuple-element.36.refs_0_), channel_id=1, source_target_pairs={{0,2},{2,0},{4,6},{6,4},{8,10},{10,8},{12,14},{14,12},{1,3},{3,1},... | collective-permute-start | bytes 233480 | tf_op jit(solution)/shard_map/ppermute | solution.py:295
  9.8 0.0 collective-permute-done.refs_1_
  9.8 2.5 %collective-permute-start.6 = (bf16[16,2432]{1,0:T(8,128)(2,1)S(1)}, bf16[16,2432]{1,0:T(8,128)(2,1)S(1)}, u32[]{:S(2)}, u32[]{:S(2)}) collective-permute-start(bf16[16,2432]{1,0:T(8,128)(2,1)S(1)} %collective-permute-done.refs_1_), channel_id=1, source_target_pairs={{0,6},{2,4},{4,2},{6,0},{8,14},{10,12},{12,10},{14,8},{1,7},{3,5},... | collective-permute-start | bytes 233480 | tf_op jit(solution)/shard_map/ppermute | solution.py:295
  12.3 0.8 %collective-permute-start.4 = (bf16[16,2432]{1,0:T(8,128)(2,1)S(1)}, bf16[16,2432]{1,0:T(8,128)(2,1)S(1)}, u32[]{:S(2)}, u32[]{:S(2)}) collective-permute-start(bf16[16,2432]{1,0:T(8,128)(2,1)S(1)} %collective-permute-done.refs_1_), channel_id=1, source_target_pairs={{0,4},{2,6},{4,0},{6,2},{8,12},{10,14},{12,8},{14,10},{1,5},{3,7},... | collective-permute-start | bytes 233480 | tf_op jit(solution)/shard_map/ppermute | solution.py:295
  13.2 0.0 collective-permute-done.5.refs_0_.refs_6_
  13.2 0.7 %collective-permute-start.2 = (bf16[16,2432]{1,0:T(8,128)(2,1)S(1)}, bf16[16,2432]{1,0:T(8,128)(2,1)S(1)}, u32[]{:S(2)}, u32[]{:S(2)}) collective-permute-start(bf16[16,2432]{1,0:T(8,128)(2,1)S(1)} %collective-permute-done.refs_1_), channel_id=1, source_target_pairs={{0,2},{2,0},{4,6},{6,4},{8,10},{10,8},{12,14},{14,12},{1,3},{3,1},... | collective-permute-start | bytes 233480 | tf_op jit(solution)/shard_map/ppermute | solution.py:295
  13.9 2.4 %fetch.1 = (bf16[192,2048]{1,0:T(8,128)(2,1)S(1)}, bf16[192,2048]{1,0:T(8,128)(2,1)S(1)}, bf16[2048,576]{1,0:T(8,128)(2,1)S(1)}) custom-call(bf16[192,2048]{1,0:T(8,128)(2,1)} %bitcast.19, bf16[192,2048]{1,0:T(8,128)(2,1)} %bitcast.20, bf16[192,2048]{1,0:T(8,128)(2,1)} %bitcast.21, bf16[16,2432]{1,0:T(8,128)(2,1)S(1)} %collective-permute-done.5.refs_0_.refs_6_), custom_call_target="tpu_custom_call" | custom-call | bytes 2359296 | tf_op jit(solution)/shard_map/fetch/pallas_call | solution.py:281
  16.4 0.0 collective-permute-done.3.refs_4_
  16.4 0.0 collective-permute-done.1.refs_2_
  16.4 0.0 collective-permute-done.6.refs_7_
  16.4 0.3 %collective-permute-done.4.refs_5_ = bf16[16,2432]{1,0:T(8,128)(2,1)S(1)} collective-permute-done((bf16[16,2432]{1,0:T(8,128)(2,1)S(1)}, bf16[16,2432]{1,0:T(8,128)(2,1)S(1)}, u32[]{:S(2)}, u32[]{:S(2)}) %collective-permute-start.4) | collective-permute-done | bytes 77856 | tf_op jit(solution)/shard_map/ppermute | solution.py:295
  16.7 0.8 %collective-permute-done.2.refs_3_ = bf16[16,2432]{1,0:T(8,128)(2,1)S(1)} collective-permute-done((bf16[16,2432]{1,0:T(8,128)(2,1)S(1)}, bf16[16,2432]{1,0:T(8,128)(2,1)S(1)}, u32[]{:S(2)}, u32[]{:S(2)}) %collective-permute-start.2) | collective-permute-done | bytes 77856 | tf_op jit(solution)/shard_map/ppermute | solution.py:295
  17.6 0.0 copy-start
  17.6 1.2 %expert.1 = (bf16[8,2432]{1,0:T(8,128)(2,1)S(1)}, bf16[8,2432]{1,0:T(8,128)(2,1)S(1)}, bf16[8,2432]{1,0:T(8,128)(2,1)S(1)}, bf16[8,2432]{1,0:T(8,128)(2,1)S(1)},...) custom-call(bf16[16,2432]{1,0:T(8,128)(2,1)S(1)} %get-tuple-element., ...), custom_call_target="tpu_custom_call" | custom-call | flops 566231040 | bytes 2359296 | tf_op jit(solution)/shard_map/expert/pallas_call | solution.py:281
  18.8 1.2 %collective-permute-start.7 = (bf16[16,2432]{1,0:T(8,128)(2,1)S(1)}, bf16[16,2432]{1,0:T(8,128)(2,1)S(1)}, u32[]{:S(2)}, u32[]{:S(2)}) collective-permute-start(bf16[16,2432]{1,0:T(8,128)(2,1)S(1)} %get-tuple-element.43), channel_id=1, source_target_pairs={{0,6},{2,4},{4,2},{6,0},{8,14},{10,12},{12,10},{14,8},{1,7},{3,5},... | collective-permute-start | bytes 233480 | tf_op jit(solution)/shard_map/ppermute | solution.py:295
  20.0 1.1 %collective-permute-start.11 = (bf16[8,2432]{1,0:T(8,128)(2,1)S(1)}, bf16[8,2432]{1,0:T(8,128)(2,1)S(1)}, u32[]{:S(2)}, u32[]{:S(2)}) collective-permute-start(bf16[8,2432]{1,0:T(8,128)(2,1)S(1)} %get-tuple-element.56), channel_id=1, source_target_pairs={{0,4},{2,6},{4,0},{6,2},{8,12},{10,14},{12,8},{14,10},{1,5},{3,7},... | collective-permute-start | bytes 116744 | tf_op jit(solution)/shard_map/ppermute | solution.py:295
  21.1 1.3 %collective-permute-start.12 = (bf16[8,2432]{1,0:T(8,128)(2,1)S(1)}, bf16[8,2432]{1,0:T(8,128)(2,1)S(1)}, u32[]{:S(2)}, u32[]{:S(2)}) collective-permute-start(bf16[8,2432]{1,0:T(8,128)(2,1)S(1)} %get-tuple-element.57), channel_id=1, source_target_pairs={{0,2},{2,0},{4,6},{6,4},{8,10},{10,8},{12,14},{14,12},{1,3},{3,1},... | collective-permute-start | bytes 116744 | tf_op jit(solution)/shard_map/ppermute | solution.py:295
  22.3 1.2 %collective-permute-start.9 = (bf16[8,2432]{1,0:T(8,128)(2,1)S(1)}, bf16[8,2432]{1,0:T(8,128)(2,1)S(1)}, u32[]{:S(2)}, u32[]{:S(2)}) collective-permute-start(bf16[8,2432]{1,0:T(8,128)(2,1)S(1)} %get-tuple-element.45), channel_id=1, source_target_pairs={{0,4},{2,6},{4,0},{6,2},{8,12},{10,14},{12,8},{14,10},{1,5},{3,7},... | collective-permute-start | bytes 116744 | tf_op jit(solution)/shard_map/ppermute | solution.py:295
  23.5 0.5 %collective-permute-start.10 = (bf16[8,2432]{1,0:T(8,128)(2,1)S(1)}, bf16[8,2432]{1,0:T(8,128)(2,1)S(1)}, u32[]{:S(2)}, u32[]{:S(2)}) collective-permute-start(bf16[8,2432]{1,0:T(8,128)(2,1)S(1)} %get-tuple-element.46), channel_id=1, source_target_pairs={{0,2},{2,0},{4,6},{6,4},{8,10},{10,8},{12,14},{14,12},{1,3},{3,1},... | collective-permute-start | bytes 116744 | tf_op jit(solution)/shard_map/ppermute | solution.py:295
  24.0 0.1 collective-permute-done.7.o3
  24.1 0.0 collective-permute-start.8
  24.1 0.1 collective-permute-done.11
  24.3 0.8 %collective-permute-done.12 = bf16[8,2432]{1,0:T(8,128)(2,1)S(1)} collective-permute-done((bf16[8,2432]{1,0:T(8,128)(2,1)S(1)}, bf16[8,2432]{1,0:T(8,128)(2,1)S(1)}, u32[]{:S(2)}, u32[]{:S(2)}) %collective-permute-start.12) | collective-permute-done | bytes 38944 | tf_op jit(solution)/shard_map/ppermute | solution.py:295
  25.1 2.7 %collective-permute-start.13 = (bf16[8,2432]{1,0:T(8,128)(2,1)S(1)}, bf16[8,2432]{1,0:T(8,128)(2,1)S(1)}, u32[]{:S(2)}, u32[]{:S(2)}) collective-permute-start(bf16[8,2432]{1,0:T(8,128)(2,1)S(1)} %add_convert_fusion), channel_id=1, source_target_pairs={{0,8},{2,10},{4,12},{6,14},{8,0},{10,2},{12,4},{14,6},{1,9},{3,11}... | collective-permute-start | bytes 116744 | tf_op jit(solution)/shard_map/ppermute | solution.py:295
  27.8 0.0 collective-permute-done.9.o2
  27.8 0.0 collective-permute-done.10.o1
  27.8 0.0 collective-permute-done.8.peer_ref
  27.8 1.6 %weights.1 = (bf16[192,1024]{1,0:T(8,128)(2,1)}, bf16[192,1024]{1,0:T(8,128)(2,1)}, bf16[192,1024]{1,0:T(8,128)(2,1)}) custom-call(bf16[144,1024]{1,0:T(8,128)(2,1)S(1)} %get-tuple-element.50.keep_ref, bf16[144,576]{1,0:T(8,128)(2,1)S(1)} %get-tuple-element.51.hid_ref, bf16[144,1600]{1,0:T(8,128)(2,1)S(1)} %collective-permute-done.8.peer_ref), custom_call_target="tpu_custom_call" | custom-call | flops 339738624 | bytes 1179648 | tf_op jit(solution)/shard_map/weights/pallas_call | solution.py:281
  29.3 1.5 %collective-permute-done.13.rest_0_ = bf16[8,2432]{1,0:T(8,128)(2,1)S(1)} collective-permute-done((bf16[8,2432]{1,0:T(8,128)(2,1)S(1)}, bf16[8,2432]{1,0:T(8,128)(2,1)S(1)}, u32[]{:S(2)}, u32[]{:S(2)}) %collective-permute-start.13) | collective-permute-done | bytes 38944 | tf_op jit(solution)/shard_map/ppermute | solution.py:295
  30.8 0.0 copy-done
  30.8 1.1 %finish.1 = (bf16[128,2048]{1,0:T(8,128)(2,1)}, f32[8,128]{1,0:T(8,128)}) custom-call(s32[8,128]{1,0:T(8,128)S(1)} %bitcast.18, f32[8,128]{1,0:T(8,128)S(1)} %get-tuple-element.35.rank_ref, bf16[8,2432]{1,0:T(8,128)(2,1)S(1)} %get-tuple-element.41.o0, bf16[8,2432]{1,0:T(8,128)(2,1)S(1)} %collective-permute-done.10.o1, ...), custom_call_target="tpu_custom_call" | custom-call | flops 50331648 | bytes 524288 | tf_op jit(solution)/shard_map/finish/pallas_call | solution.py:281
  (1 shorter events, 0.0 us)
Async XLA Ops:
  2.2 7.6 %collective-permute-start = (bf16[16,2432]{1,0:T(8,128)(2,1)S(1)}, bf16[16,2432]{1,0:T(8,128)(2,1)S(1)}, u32[]{:S(2)}, u32[]{:S(2)}) collective-permute-start(bf16[16,2432]{1,0:T(8,128)(2,1)S(1)} %get-tuple-element.37), channel_id=1, source_target_pairs={{0,8},{2,10},{4,12},{6,14},{8,0},{10,2},{12,4},{14,6},{1,9},{3,11}... | collective-permute-start | bytes 233480 | tf_op jit(solution)/shard_map/ppermute | solution.py:295
  6.3 6.9 %collective-permute-start.5 = (bf16[16,2432]{1,0:T(8,128)(2,1)S(1)}, bf16[16,2432]{1,0:T(8,128)(2,1)S(1)}, u32[]{:S(2)}, u32[]{:S(2)}) collective-permute-start(bf16[16,2432]{1,0:T(8,128)(2,1)S(1)} %get-tuple-element.36.refs_0_), channel_id=1, source_target_pairs={{0,6},{2,4},{4,2},{6,0},{8,14},{10,12},{12,10},{14,8},{1,7},{3,5},... | collective-permute-start | bytes 233480 | tf_op jit(solution)/shard_map/ppermute | solution.py:295
  8.8 7.6 %collective-permute-start.3 = (bf16[16,2432]{1,0:T(8,128)(2,1)S(1)}, bf16[16,2432]{1,0:T(8,128)(2,1)S(1)}, u32[]{:S(2)}, u32[]{:S(2)}) collective-permute-start(bf16[16,2432]{1,0:T(8,128)(2,1)S(1)} %get-tuple-element.36.refs_0_), channel_id=1, source_target_pairs={{0,4},{2,6},{4,0},{6,2},{8,12},{10,14},{12,8},{14,10},{1,5},{3,7},... | collective-permute-start | bytes 233480 | tf_op jit(solution)/shard_map/ppermute | solution.py:295
  9.2 7.2 %collective-permute-start.1 = (bf16[16,2432]{1,0:T(8,128)(2,1)S(1)}, bf16[16,2432]{1,0:T(8,128)(2,1)S(1)}, u32[]{:S(2)}, u32[]{:S(2)}) collective-permute-start(bf16[16,2432]{1,0:T(8,128)(2,1)S(1)} %get-tuple-element.36.refs_0_), channel_id=1, source_target_pairs={{0,2},{2,0},{4,6},{6,4},{8,10},{10,8},{12,14},{14,12},{1,3},{3,1},... | collective-permute-start | bytes 233480 | tf_op jit(solution)/shard_map/ppermute | solution.py:295
  9.8 6.6 %collective-permute-start.6 = (bf16[16,2432]{1,0:T(8,128)(2,1)S(1)}, bf16[16,2432]{1,0:T(8,128)(2,1)S(1)}, u32[]{:S(2)}, u32[]{:S(2)}) collective-permute-start(bf16[16,2432]{1,0:T(8,128)(2,1)S(1)} %collective-permute-done.refs_1_), channel_id=1, source_target_pairs={{0,6},{2,4},{4,2},{6,0},{8,14},{10,12},{12,10},{14,8},{1,7},{3,5},... | collective-permute-start | bytes 233480 | tf_op jit(solution)/shard_map/ppermute | solution.py:295
  12.3 4.4 %collective-permute-start.4 = (bf16[16,2432]{1,0:T(8,128)(2,1)S(1)}, bf16[16,2432]{1,0:T(8,128)(2,1)S(1)}, u32[]{:S(2)}, u32[]{:S(2)}) collective-permute-start(bf16[16,2432]{1,0:T(8,128)(2,1)S(1)} %collective-permute-done.refs_1_), channel_id=1, source_target_pairs={{0,4},{2,6},{4,0},{6,2},{8,12},{10,14},{12,8},{14,10},{1,5},{3,7},... | collective-permute-start | bytes 233480 | tf_op jit(solution)/shard_map/ppermute | solution.py:295
  13.2 4.4 %collective-permute-start.2 = (bf16[16,2432]{1,0:T(8,128)(2,1)S(1)}, bf16[16,2432]{1,0:T(8,128)(2,1)S(1)}, u32[]{:S(2)}, u32[]{:S(2)}) collective-permute-start(bf16[16,2432]{1,0:T(8,128)(2,1)S(1)} %collective-permute-done.refs_1_), channel_id=1, source_target_pairs={{0,2},{2,0},{4,6},{6,4},{8,10},{10,8},{12,14},{14,12},{1,3},{3,1},... | collective-permute-start | bytes 233480 | tf_op jit(solution)/shard_map/ppermute | solution.py:295
  17.6 13.2 %copy-start = (s32[128,8]{0,1:T(8,128)S(1)}, s32[128,8]{0,1:T(8,128)}, u32[]{:S(2)}) copy-start(s32[128,8]{0,1:T(8,128)} %param.9) | copy-start | bytes 12292
  18.8 5.4 %collective-permute-start.7 = (bf16[16,2432]{1,0:T(8,128)(2,1)S(1)}, bf16[16,2432]{1,0:T(8,128)(2,1)S(1)}, u32[]{:S(2)}, u32[]{:S(2)}) collective-permute-start(bf16[16,2432]{1,0:T(8,128)(2,1)S(1)} %get-tuple-element.43), channel_id=1, source_target_pairs={{0,6},{2,4},{4,2},{6,0},{8,14},{10,12},{12,10},{14,8},{1,7},{3,5},... | collective-permute-start | bytes 233480 | tf_op jit(solution)/shard_map/ppermute | solution.py:295
  20.0 4.3 %collective-permute-start.11 = (bf16[8,2432]{1,0:T(8,128)(2,1)S(1)}, bf16[8,2432]{1,0:T(8,128)(2,1)S(1)}, u32[]{:S(2)}, u32[]{:S(2)}) collective-permute-start(bf16[8,2432]{1,0:T(8,128)(2,1)S(1)} %get-tuple-element.56), channel_id=1, source_target_pairs={{0,4},{2,6},{4,0},{6,2},{8,12},{10,14},{12,8},{14,10},{1,5},{3,7},... | collective-permute-start | bytes 116744 | tf_op jit(solution)/shard_map/ppermute | solution.py:295
  21.1 4.0 %collective-permute-start.12 = (bf16[8,2432]{1,0:T(8,128)(2,1)S(1)}, bf16[8,2432]{1,0:T(8,128)(2,1)S(1)}, u32[]{:S(2)}, u32[]{:S(2)}) collective-permute-start(bf16[8,2432]{1,0:T(8,128)(2,1)S(1)} %get-tuple-element.57), channel_id=1, source_target_pairs={{0,2},{2,0},{4,6},{6,4},{8,10},{10,8},{12,14},{14,12},{1,3},{3,1},... | collective-permute-start | bytes 116744 | tf_op jit(solution)/shard_map/ppermute | solution.py:295
  22.3 5.4 %collective-permute-start.9 = (bf16[8,2432]{1,0:T(8,128)(2,1)S(1)}, bf16[8,2432]{1,0:T(8,128)(2,1)S(1)}, u32[]{:S(2)}, u32[]{:S(2)}) collective-permute-start(bf16[8,2432]{1,0:T(8,128)(2,1)S(1)} %get-tuple-element.45), channel_id=1, source_target_pairs={{0,4},{2,6},{4,0},{6,2},{8,12},{10,14},{12,8},{14,10},{1,5},{3,7},... | collective-permute-start | bytes 116744 | tf_op jit(solution)/shard_map/ppermute | solution.py:295
  23.5 4.3 %collective-permute-start.10 = (bf16[8,2432]{1,0:T(8,128)(2,1)S(1)}, bf16[8,2432]{1,0:T(8,128)(2,1)S(1)}, u32[]{:S(2)}, u32[]{:S(2)}) collective-permute-start(bf16[8,2432]{1,0:T(8,128)(2,1)S(1)} %get-tuple-element.46), channel_id=1, source_target_pairs={{0,2},{2,0},{4,6},{6,4},{8,10},{10,8},{12,14},{14,12},{1,3},{3,1},... | collective-permute-start | bytes 116744 | tf_op jit(solution)/shard_map/ppermute | solution.py:295
  24.1 3.6 %collective-permute-start.8 = (bf16[144,1600]{1,0:T(8,128)(2,1)S(1)}, bf16[144,1600]{1,0:T(8,128)(2,1)S(1)}, u32[]{:S(2)}, u32[]{:S(2)}) collective-permute-start(bf16[144,1600]{1,0:T(8,128)(2,1)S(1)} %get-tuple-element.44), channel_id=1, source_target_pairs={{0,1},{1,0},{2,3},{3,2},{4,5},{5,4},{6,7},{7,6},{8,9},{9,8},{10,11... | collective-permute-start | bytes 1382408 | tf_op jit(solution)/shard_map/ppermute | solution.py:367
  25.1 5.7 %collective-permute-start.13 = (bf16[8,2432]{1,0:T(8,128)(2,1)S(1)}, bf16[8,2432]{1,0:T(8,128)(2,1)S(1)}, u32[]{:S(2)}, u32[]{:S(2)}) collective-permute-start(bf16[8,2432]{1,0:T(8,128)(2,1)S(1)} %add_convert_fusion), channel_id=1, source_target_pairs={{0,8},{2,10},{4,12},{6,14},{8,0},{10,2},{12,4},{14,6},{1,9},{3,11}... | collective-permute-start | bytes 116744 | tf_op jit(solution)/shard_map/ppermute | solution.py:295

commit v8 on v7

--- a/solution.py
+++ b/solution.py
@@ -326,7 +326,7 @@
         fetch_kernel,
         [(wg.shape, BF16), (wu.shape, BF16), ((features, 3 * hidden), BF16)],
         "fetch",
-        (wg, wu, wd, near[-1]),
+        (wg, wu, wd, near[1]),
         0,
         6 * features * hidden,
         12,

time: 32.1 us -> 31.6 us (0.984)
  starting transfers between devices: 19.7 us -> 19.1 us
    ppermute x13, starting transfers between devices: 19.7 us -> 19.1 us  [swap_by(): return lax.ppermute(block, 'expert', [(i, i ^ mask) for i in range(count)])]
where the time goes in v8:
time: 31.6 us; the launch traced here: 31.4 us
  starting transfers between devices  19.1 us (60%)
  Pallas kernels  7.82 us (25%)
  waiting for transfers between devices  3.81 us (12%)
  between operations  0.69 us (2%)
    ppermute x13, starting transfers between devices, swap_by(): return lax.ppermute(block, 'expert', [(i, i ^ mask) for i in range(count)])  19.1 us
    pallas_call x5, Pallas kernels, call(): pl.pallas_call(kernel, out_shape=[jax.ShapeDtypeStruct(s, t) for s, t in...  7.82 us
    ppermute x13, waiting for transfers between devices, swap_by(): return lax.ppermute(block, 'expert', [(i, i ^ mask) for i in range(count)])  3.81 us
  transfers between devices with their start and end apart: 14, of which 6 were waited for; matrix products, arithmetic and copies ran while one was open for 0% of the time, Pallas kernels for 13%

profile of v8, /device:TPU:0, one launch (start us, length us, event | category | flops | bytes accessed | tf_op | source)
XLA Modules:
  0.0 31.4 jit_solution(6356929785811474277)
XLA Ops:
  0.6 1.5 %pack.1 = (bf16[16,2432]{1,0:T(8,128)(2,1)S(1)}, bf16[16,2432]{1,0:T(8,128)(2,1)S(1)}, f32[8,128]{1,0:T(8,128)S(1)}) custom-call(s32[8,128]{1,0:T(8,128)} %bitcast.17, bf16[8,128]{1,0:T(8,128)(2,1)} %bitcast.22, bf16[128,2048]{1,0:T(8,128)(2,1)} %tok_hbm.1, bf16[128,2048]{1,0:T(8,128)(2,1)} %grad_hbm.1), custom_call_target="tpu_custom_call" | custom-call | flops 18874368 | bytes 1048576 | tf_op jit(solution)/shard_map/pack/pallas_call | solution.py:281
  2.2 4.1 %collective-permute-start = (bf16[16,2432]{1,0:T(8,128)(2,1)S(1)}, bf16[16,2432]{1,0:T(8,128)(2,1)S(1)}, u32[]{:S(2)}, u32[]{:S(2)}) collective-permute-start(bf16[16,2432]{1,0:T(8,128)(2,1)S(1)} %get-tuple-element.37), channel_id=1, source_target_pairs={{0,8},{2,10},{4,12},{6,14},{8,0},{10,2},{12,4},{14,6},{1,9},{3,11}... | collective-permute-start | bytes 233480 | tf_op jit(solution)/shard_map/ppermute | solution.py:295
  6.3 1.5 %collective-permute-start.1 = (bf16[16,2432]{1,0:T(8,128)(2,1)S(1)}, bf16[16,2432]{1,0:T(8,128)(2,1)S(1)}, u32[]{:S(2)}, u32[]{:S(2)}) collective-permute-start(bf16[16,2432]{1,0:T(8,128)(2,1)S(1)} %get-tuple-element.36.refs_0_), channel_id=1, source_target_pairs={{0,2},{2,0},{4,6},{6,4},{8,10},{10,8},{12,14},{14,12},{1,3},{3,1},... | collective-permute-start | bytes 233480 | tf_op jit(solution)/shard_map/ppermute | solution.py:295
  7.8 1.6 %collective-permute-start.5 = (bf16[16,2432]{1,0:T(8,128)(2,1)S(1)}, bf16[16,2432]{1,0:T(8,128)(2,1)S(1)}, u32[]{:S(2)}, u32[]{:S(2)}) collective-permute-start(bf16[16,2432]{1,0:T(8,128)(2,1)S(1)} %get-tuple-element.36.refs_0_), channel_id=1, source_target_pairs={{0,6},{2,4},{4,2},{6,0},{8,14},{10,12},{12,10},{14,8},{1,7},{3,5},... | collective-permute-start | bytes 233480 | tf_op jit(solution)/shard_map/ppermute | solution.py:295
  9.3 0.4 %collective-permute-start.3 = (bf16[16,2432]{1,0:T(8,128)(2,1)S(1)}, bf16[16,2432]{1,0:T(8,128)(2,1)S(1)}, u32[]{:S(2)}, u32[]{:S(2)}) collective-permute-start(bf16[16,2432]{1,0:T(8,128)(2,1)S(1)} %get-tuple-element.36.refs_0_), channel_id=1, source_target_pairs={{0,4},{2,6},{4,0},{6,2},{8,12},{10,14},{12,8},{14,10},{1,5},{3,7},... | collective-permute-start | bytes 233480 | tf_op jit(solution)/shard_map/ppermute | solution.py:295
  9.8 0.3 collective-permute-done.refs_1_
  10.1 2.2 %collective-permute-start.6 = (bf16[16,2432]{1,0:T(8,128)(2,1)S(1)}, bf16[16,2432]{1,0:T(8,128)(2,1)S(1)}, u32[]{:S(2)}, u32[]{:S(2)}) collective-permute-start(bf16[16,2432]{1,0:T(8,128)(2,1)S(1)} %collective-permute-done.refs_1_), channel_id=1, source_target_pairs={{0,6},{2,4},{4,2},{6,0},{8,14},{10,12},{12,10},{14,8},{1,7},{3,5},... | collective-permute-start | bytes 233480 | tf_op jit(solution)/shard_map/ppermute | solution.py:295
  12.3 1.1 %collective-permute-start.4 = (bf16[16,2432]{1,0:T(8,128)(2,1)S(1)}, bf16[16,2432]{1,0:T(8,128)(2,1)S(1)}, u32[]{:S(2)}, u32[]{:S(2)}) collective-permute-start(bf16[16,2432]{1,0:T(8,128)(2,1)S(1)} %collective-permute-done.refs_1_), channel_id=1, source_target_pairs={{0,4},{2,6},{4,0},{6,2},{8,12},{10,14},{12,8},{14,10},{1,5},{3,7},... | collective-permute-start | bytes 233480 | tf_op jit(solution)/shard_map/ppermute | solution.py:295
  13.4 0.0 collective-permute-done.1.refs_0_.refs_2_
  13.4 0.1 collective-permute-start.2
  13.6 2.4 %fetch.1 = (bf16[192,2048]{1,0:T(8,128)(2,1)S(1)}, bf16[192,2048]{1,0:T(8,128)(2,1)S(1)}, bf16[2048,576]{1,0:T(8,128)(2,1)S(1)}) custom-call(bf16[192,2048]{1,0:T(8,128)(2,1)} %bitcast.19, bf16[192,2048]{1,0:T(8,128)(2,1)} %bitcast.20, bf16[192,2048]{1,0:T(8,128)(2,1)} %bitcast.21, bf16[16,2432]{1,0:T(8,128)(2,1)S(1)} %collective-permute-done.1.refs_0_.refs_2_), custom_call_target="tpu_custom_call" | custom-call | bytes 2359296 | tf_op jit(solution)/shard_map/fetch/pallas_call | solution.py:281
  16.0 0.0 collective-permute-done.5.refs_6_
  16.0 0.0 collective-permute-done.3.refs_4_
  16.0 0.8 %collective-permute-done.6.refs_7_ = bf16[16,2432]{1,0:T(8,128)(2,1)S(1)} collective-permute-done((bf16[16,2432]{1,0:T(8,128)(2,1)S(1)}, bf16[16,2432]{1,0:T(8,128)(2,1)S(1)}, u32[]{:S(2)}, u32[]{:S(2)}) %collective-permute-start.6) | collective-permute-done | bytes 77856 | tf_op jit(solution)/shard_map/ppermute | solution.py:295
  16.8 0.0 collective-permute-done.4.refs_5_
  16.8 1.0 %collective-permute-done.2.refs_3_ = bf16[16,2432]{1,0:T(8,128)(2,1)S(1)} collective-permute-done((bf16[16,2432]{1,0:T(8,128)(2,1)S(1)}, bf16[16,2432]{1,0:T(8,128)(2,1)S(1)}, u32[]{:S(2)}, u32[]{:S(2)}) %collective-permute-start.2) | collective-permute-done | bytes 77856 | tf_op jit(solution)/shard_map/ppermute | solution.py:295
  17.8 0.0 copy-start
  17.8 1.2 %expert.1 = (bf16[8,2432]{1,0:T(8,128)(2,1)S(1)}, bf16[8,2432]{1,0:T(8,128)(2,1)S(1)}, bf16[8,2432]{1,0:T(8,128)(2,1)S(1)}, bf16[8,2432]{1,0:T(8,128)(2,1)S(1)},...) custom-call(bf16[16,2432]{1,0:T(8,128)(2,1)S(1)} %get-tuple-element., ...), custom_call_target="tpu_custom_call" | custom-call | flops 566231040 | bytes 2359296 | tf_op jit(solution)/shard_map/expert/pallas_call | solution.py:281
  19.0 1.1 %collective-permute-start.7 = (bf16[16,2432]{1,0:T(8,128)(2,1)S(1)}, bf16[16,2432]{1,0:T(8,128)(2,1)S(1)}, u32[]{:S(2)}, u32[]{:S(2)}) collective-permute-start(bf16[16,2432]{1,0:T(8,128)(2,1)S(1)} %get-tuple-element.43), channel_id=1, source_target_pairs={{0,6},{2,4},{4,2},{6,0},{8,14},{10,12},{12,10},{14,8},{1,7},{3,5},... | collective-permute-start | bytes 233480 | tf_op jit(solution)/shard_map/ppermute | solution.py:295
  20.1 0.9 %collective-permute-start.11 = (bf16[8,2432]{1,0:T(8,128)(2,1)S(1)}, bf16[8,2432]{1,0:T(8,128)(2,1)S(1)}, u32[]{:S(2)}, u32[]{:S(2)}) collective-permute-start(bf16[8,2432]{1,0:T(8,128)(2,1)S(1)} %get-tuple-element.56), channel_id=1, source_target_pairs={{0,4},{2,6},{4,0},{6,2},{8,12},{10,14},{12,8},{14,10},{1,5},{3,7},... | collective-permute-start | bytes 116744 | tf_op jit(solution)/shard_map/ppermute | solution.py:295
  21.0 1.6 %collective-permute-start.12 = (bf16[8,2432]{1,0:T(8,128)(2,1)S(1)}, bf16[8,2432]{1,0:T(8,128)(2,1)S(1)}, u32[]{:S(2)}, u32[]{:S(2)}) collective-permute-start(bf16[8,2432]{1,0:T(8,128)(2,1)S(1)} %get-tuple-element.57), channel_id=1, source_target_pairs={{0,2},{2,0},{4,6},{6,4},{8,10},{10,8},{12,14},{14,12},{1,3},{3,1},... | collective-permute-start | bytes 116744 | tf_op jit(solution)/shard_map/ppermute | solution.py:295
  22.6 1.0 %collective-permute-start.9 = (bf16[8,2432]{1,0:T(8,128)(2,1)S(1)}, bf16[8,2432]{1,0:T(8,128)(2,1)S(1)}, u32[]{:S(2)}, u32[]{:S(2)}) collective-permute-start(bf16[8,2432]{1,0:T(8,128)(2,1)S(1)} %get-tuple-element.45), channel_id=1, source_target_pairs={{0,4},{2,6},{4,0},{6,2},{8,12},{10,14},{12,8},{14,10},{1,5},{3,7},... | collective-permute-start | bytes 116744 | tf_op jit(solution)/shard_map/ppermute | solution.py:295
  23.6 0.6 %collective-permute-start.10 = (bf16[8,2432]{1,0:T(8,128)(2,1)S(1)}, bf16[8,2432]{1,0:T(8,128)(2,1)S(1)}, u32[]{:S(2)}, u32[]{:S(2)}) collective-permute-start(bf16[8,2432]{1,0:T(8,128)(2,1)S(1)} %get-tuple-element.46), channel_id=1, source_target_pairs={{0,2},{2,0},{4,6},{6,4},{8,10},{10,8},{12,14},{14,12},{1,3},{3,1},... | collective-permute-start | bytes 116744 | tf_op jit(solution)/shard_map/ppermute | solution.py:295
  24.1 0.3 collective-permute-done.7.o3
  24.4 0.0 collective-permute-start.8
  24.4 0.0 collective-permute-done.11
  24.4 0.5 %collective-permute-done.12 = bf16[8,2432]{1,0:T(8,128)(2,1)S(1)} collective-permute-done((bf16[8,2432]{1,0:T(8,128)(2,1)S(1)}, bf16[8,2432]{1,0:T(8,128)(2,1)S(1)}, u32[]{:S(2)}, u32[]{:S(2)}) %collective-permute-start.12) | collective-permute-done | bytes 38944 | tf_op jit(solution)/shard_map/ppermute | solution.py:295
  25.0 2.9 %collective-permute-start.13 = (bf16[8,2432]{1,0:T(8,128)(2,1)S(1)}, bf16[8,2432]{1,0:T(8,128)(2,1)S(1)}, u32[]{:S(2)}, u32[]{:S(2)}) collective-permute-start(bf16[8,2432]{1,0:T(8,128)(2,1)S(1)} %add_convert_fusion), channel_id=1, source_target_pairs={{0,8},{2,10},{4,12},{6,14},{8,0},{10,2},{12,4},{14,6},{1,9},{3,11}... | collective-permute-start | bytes 116744 | tf_op jit(solution)/shard_map/ppermute | solution.py:295
  27.9 0.0 collective-permute-done.9.o2
  27.9 0.0 collective-permute-done.10.o1
  27.9 0.0 collective-permute-done.8.peer_ref
  27.9 1.6 %weights.1 = (bf16[192,1024]{1,0:T(8,128)(2,1)}, bf16[192,1024]{1,0:T(8,128)(2,1)}, bf16[192,1024]{1,0:T(8,128)(2,1)}) custom-call(bf16[144,1024]{1,0:T(8,128)(2,1)S(1)} %get-tuple-element.50.keep_ref, bf16[144,576]{1,0:T(8,128)(2,1)S(1)} %get-tuple-element.51.hid_ref, bf16[144,1600]{1,0:T(8,128)(2,1)S(1)} %collective-permute-done.8.peer_ref), custom_call_target="tpu_custom_call" | custom-call | flops 339738624 | bytes 1179648 | tf_op jit(solution)/shard_map/weights/pallas_call | solution.py:281
  29.5 0.9 %collective-permute-done.13.rest_0_ = bf16[8,2432]{1,0:T(8,128)(2,1)S(1)} collective-permute-done((bf16[8,2432]{1,0:T(8,128)(2,1)S(1)}, bf16[8,2432]{1,0:T(8,128)(2,1)S(1)}, u32[]{:S(2)}, u32[]{:S(2)}) %collective-permute-start.13) | collective-permute-done | bytes 38944 | tf_op jit(solution)/shard_map/ppermute | solution.py:295
  30.3 0.0 copy-done
  30.3 1.1 %finish.1 = (bf16[128,2048]{1,0:T(8,128)(2,1)}, f32[8,128]{1,0:T(8,128)}) custom-call(s32[8,128]{1,0:T(8,128)S(1)} %bitcast.18, f32[8,128]{1,0:T(8,128)S(1)} %get-tuple-element.35.rank_ref, bf16[8,2432]{1,0:T(8,128)(2,1)S(1)} %get-tuple-element.41.o0, bf16[8,2432]{1,0:T(8,128)(2,1)S(1)} %collective-permute-done.10.o1, ...), custom_call_target="tpu_custom_call" | custom-call | flops 50331648 | bytes 524288 | tf_op jit(solution)/shard_map/finish/pallas_call | solution.py:281
  (1 shorter events, 0.0 us)
Async XLA Ops:
  2.2 7.9 %collective-permute-start = (bf16[16,2432]{1,0:T(8,128)(2,1)S(1)}, bf16[16,2432]{1,0:T(8,128)(2,1)S(1)}, u32[]{:S(2)}, u32[]{:S(2)}) collective-permute-start(bf16[16,2432]{1,0:T(8,128)(2,1)S(1)} %get-tuple-element.37), channel_id=1, source_target_pairs={{0,8},{2,10},{4,12},{6,14},{8,0},{10,2},{12,4},{14,6},{1,9},{3,11}... | collective-permute-start | bytes 233480 | tf_op jit(solution)/shard_map/ppermute | solution.py:295
  6.3 7.1 %collective-permute-start.1 = (bf16[16,2432]{1,0:T(8,128)(2,1)S(1)}, bf16[16,2432]{1,0:T(8,128)(2,1)S(1)}, u32[]{:S(2)}, u32[]{:S(2)}) collective-permute-start(bf16[16,2432]{1,0:T(8,128)(2,1)S(1)} %get-tuple-element.36.refs_0_), channel_id=1, source_target_pairs={{0,2},{2,0},{4,6},{6,4},{8,10},{10,8},{12,14},{14,12},{1,3},{3,1},... | collective-permute-start | bytes 233480 | tf_op jit(solution)/shard_map/ppermute | solution.py:295
  7.8 8.2 %collective-permute-start.5 = (bf16[16,2432]{1,0:T(8,128)(2,1)S(1)}, bf16[16,2432]{1,0:T(8,128)(2,1)S(1)}, u32[]{:S(2)}, u32[]{:S(2)}) collective-permute-start(bf16[16,2432]{1,0:T(8,128)(2,1)S(1)} %get-tuple-element.36.refs_0_), channel_id=1, source_target_pairs={{0,6},{2,4},{4,2},{6,0},{8,14},{10,12},{12,10},{14,8},{1,7},{3,5},... | collective-permute-start | bytes 233480 | tf_op jit(solution)/shard_map/ppermute | solution.py:295
  9.3 6.7 %collective-permute-start.3 = (bf16[16,2432]{1,0:T(8,128)(2,1)S(1)}, bf16[16,2432]{1,0:T(8,128)(2,1)S(1)}, u32[]{:S(2)}, u32[]{:S(2)}) collective-permute-start(bf16[16,2432]{1,0:T(8,128)(2,1)S(1)} %get-tuple-element.36.refs_0_), channel_id=1, source_target_pairs={{0,4},{2,6},{4,0},{6,2},{8,12},{10,14},{12,8},{14,10},{1,5},{3,7},... | collective-permute-start | bytes 233480 | tf_op jit(solution)/shard_map/ppermute | solution.py:295
  10.1 6.8 %collective-permute-start.6 = (bf16[16,2432]{1,0:T(8,128)(2,1)S(1)}, bf16[16,2432]{1,0:T(8,128)(2,1)S(1)}, u32[]{:S(2)}, u32[]{:S(2)}) collective-permute-start(bf16[16,2432]{1,0:T(8,128)(2,1)S(1)} %collective-permute-done.refs_1_), channel_id=1, source_target_pairs={{0,6},{2,4},{4,2},{6,0},{8,14},{10,12},{12,10},{14,8},{1,7},{3,5},... | collective-permute-start | bytes 233480 | tf_op jit(solution)/shard_map/ppermute | solution.py:295
  12.3 4.6 %collective-permute-start.4 = (bf16[16,2432]{1,0:T(8,128)(2,1)S(1)}, bf16[16,2432]{1,0:T(8,128)(2,1)S(1)}, u32[]{:S(2)}, u32[]{:S(2)}) collective-permute-start(bf16[16,2432]{1,0:T(8,128)(2,1)S(1)} %collective-permute-done.refs_1_), channel_id=1, source_target_pairs={{0,4},{2,6},{4,0},{6,2},{8,12},{10,14},{12,8},{14,10},{1,5},{3,7},... | collective-permute-start | bytes 233480 | tf_op jit(solution)/shard_map/ppermute | solution.py:295
  13.4 4.4 %collective-permute-start.2 = (bf16[16,2432]{1,0:T(8,128)(2,1)S(1)}, bf16[16,2432]{1,0:T(8,128)(2,1)S(1)}, u32[]{:S(2)}, u32[]{:S(2)}) collective-permute-start(bf16[16,2432]{1,0:T(8,128)(2,1)S(1)} %collective-permute-done.refs_1_), channel_id=1, source_target_pairs={{0,2},{2,0},{4,6},{6,4},{8,10},{10,8},{12,14},{14,12},{1,3},{3,1},... | collective-permute-start | bytes 233480 | tf_op jit(solution)/shard_map/ppermute | solution.py:295
  17.8 12.5 %copy-start = (s32[128,8]{0,1:T(8,128)S(1)}, s32[128,8]{0,1:T(8,128)}, u32[]{:S(2)}) copy-start(s32[128,8]{0,1:T(8,128)} %param.9) | copy-start | bytes 12292
  19.0 5.4 %collective-permute-start.7 = (bf16[16,2432]{1,0:T(8,128)(2,1)S(1)}, bf16[16,2432]{1,0:T(8,128)(2,1)S(1)}, u32[]{:S(2)}, u32[]{:S(2)}) collective-permute-start(bf16[16,2432]{1,0:T(8,128)(2,1)S(1)} %get-tuple-element.43), channel_id=1, source_target_pairs={{0,6},{2,4},{4,2},{6,0},{8,14},{10,12},{12,10},{14,8},{1,7},{3,5},... | collective-permute-start | bytes 233480 | tf_op jit(solution)/shard_map/ppermute | solution.py:295
  20.1 4.3 %collective-permute-start.11 = (bf16[8,2432]{1,0:T(8,128)(2,1)S(1)}, bf16[8,2432]{1,0:T(8,128)(2,1)S(1)}, u32[]{:S(2)}, u32[]{:S(2)}) collective-permute-start(bf16[8,2432]{1,0:T(8,128)(2,1)S(1)} %get-tuple-element.56), channel_id=1, source_target_pairs={{0,4},{2,6},{4,0},{6,2},{8,12},{10,14},{12,8},{14,10},{1,5},{3,7},... | collective-permute-start | bytes 116744 | tf_op jit(solution)/shard_map/ppermute | solution.py:295
  21.0 4.0 %collective-permute-start.12 = (bf16[8,2432]{1,0:T(8,128)(2,1)S(1)}, bf16[8,2432]{1,0:T(8,128)(2,1)S(1)}, u32[]{:S(2)}, u32[]{:S(2)}) collective-permute-start(bf16[8,2432]{1,0:T(8,128)(2,1)S(1)} %get-tuple-element.57), channel_id=1, source_target_pairs={{0,2},{2,0},{4,6},{6,4},{8,10},{10,8},{12,14},{14,12},{1,3},{3,1},... | collective-permute-start | bytes 116744 | tf_op jit(solution)/shard_map/ppermute | solution.py:295
  22.6 5.3 %collective-permute-start.9 = (bf16[8,2432]{1,0:T(8,128)(2,1)S(1)}, bf16[8,2432]{1,0:T(8,128)(2,1)S(1)}, u32[]{:S(2)}, u32[]{:S(2)}) collective-permute-start(bf16[8,2432]{1,0:T(8,128)(2,1)S(1)} %get-tuple-element.45), channel_id=1, source_target_pairs={{0,4},{2,6},{4,0},{6,2},{8,12},{10,14},{12,8},{14,10},{1,5},{3,7},... | collective-permute-start | bytes 116744 | tf_op jit(solution)/shard_map/ppermute | solution.py:295
  23.6 4.3 %collective-permute-start.10 = (bf16[8,2432]{1,0:T(8,128)(2,1)S(1)}, bf16[8,2432]{1,0:T(8,128)(2,1)S(1)}, u32[]{:S(2)}, u32[]{:S(2)}) collective-permute-start(bf16[8,2432]{1,0:T(8,128)(2,1)S(1)} %get-tuple-element.46), channel_id=1, source_target_pairs={{0,2},{2,0},{4,6},{6,4},{8,10},{10,8},{12,14},{14,12},{1,3},{3,1},... | collective-permute-start | bytes 116744 | tf_op jit(solution)/shard_map/ppermute | solution.py:295
  24.4 3.5 %collective-permute-start.8 = (bf16[144,1600]{1,0:T(8,128)(2,1)S(1)}, bf16[144,1600]{1,0:T(8,128)(2,1)S(1)}, u32[]{:S(2)}, u32[]{:S(2)}) collective-permute-start(bf16[144,1600]{1,0:T(8,128)(2,1)S(1)} %get-tuple-element.44), channel_id=1, source_target_pairs={{0,1},{1,0},{2,3},{3,2},{4,5},{5,4},{6,7},{7,6},{8,9},{9,8},{10,11... | collective-permute-start | bytes 1382408 | tf_op jit(solution)/shard_map/ppermute | solution.py:367
  25.0 5.4 %collective-permute-start.13 = (bf16[8,2432]{1,0:T(8,128)(2,1)S(1)}, bf16[8,2432]{1,0:T(8,128)(2,1)S(1)}, u32[]{:S(2)}, u32[]{:S(2)}) collective-permute-start(bf16[8,2432]{1,0:T(8,128)(2,1)S(1)} %add_convert_fusion), channel_id=1, source_target_pairs={{0,8},{2,10},{4,12},{6,14},{8,0},{10,2},{12,4},{14,6},{1,9},{3,11}... | collective-permute-start | bytes 116744 | tf_op jit(solution)/shard_map/ppermute | solution.py:295

commit v9 on v8

--- a/solution.py
+++ b/solution.py
@@ -362,8 +362,8 @@
     both = swap_by(messages[-1], SPLIT - 1)
     back = [away[0]] + [swap_by(away[j], j) for j in range(1, SPLIT - 1)] + [both]
     home = [home[0]] + [swap_by(home[j], j) for j in range(1, SPLIT - 1)]
-    send, first = lax.optimization_barrier((send, back[-1]))
-    back[-1] = first
+    send, first = lax.optimization_barrier((send, back[2]))
+    back[2] = first
     peer = lax.ppermute(send, "dp", [(0, 1), (1, 0)])
     peer, *rest = lax.optimization_barrier((peer, *home[:0:-1]))
     home = home[:1] + rest[::-1]

time: 31.6 us -> 31.5 us (level)
  transfers between devices with their start and end apart: 14 -> 14, of which waited for: 6 -> 5; matrix products, arithmetic and copies ran while one was open for 0% -> 0% of each run, Pallas kernels for 13% -> 13%
where the time goes in v9:
time: 31.5 us; the launch traced here: 31.3 us
  starting transfers between devices  19.1 us (61%)
  Pallas kernels  7.81 us (25%)
  waiting for transfers between devices  3.72 us (12%)
  between operations  0.69 us (2%)
    ppermute x13, starting transfers between devices, swap_by(): return lax.ppermute(block, 'expert', [(i, i ^ mask) for i in range(count)])  19.1 us
    pallas_call x5, Pallas kernels, call(): pl.pallas_call(kernel, out_shape=[jax.ShapeDtypeStruct(s, t) for s, t in...  7.81 us
    ppermute x13, waiting for transfers between devices, swap_by(): return lax.ppermute(block, 'expert', [(i, i ^ mask) for i in range(count)])  3.71 us
  transfers between devices with their start and end apart: 14, of which 5 were waited for; matrix products, arithmetic and copies ran while one was open for 0% of the time, Pallas kernels for 13%

profile of v9, /device:TPU:0, one launch (start us, length us, event | category | flops | bytes accessed | tf_op | source)
XLA Modules:
  0.0 31.3 jit_solution(6547976776390025908)
XLA Ops:
  0.6 1.5 %pack.1 = (bf16[16,2432]{1,0:T(8,128)(2,1)S(1)}, bf16[16,2432]{1,0:T(8,128)(2,1)S(1)}, f32[8,128]{1,0:T(8,128)S(1)}) custom-call(s32[8,128]{1,0:T(8,128)} %bitcast.17, bf16[8,128]{1,0:T(8,128)(2,1)} %bitcast.22, bf16[128,2048]{1,0:T(8,128)(2,1)} %tok_hbm.1, bf16[128,2048]{1,0:T(8,128)(2,1)} %grad_hbm.1), custom_call_target="tpu_custom_call" | custom-call | flops 18874368 | bytes 1048576 | tf_op jit(solution)/shard_map/pack/pallas_call | solution.py:281
  2.2 4.1 %collective-permute-start = (bf16[16,2432]{1,0:T(8,128)(2,1)S(1)}, bf16[16,2432]{1,0:T(8,128)(2,1)S(1)}, u32[]{:S(2)}, u32[]{:S(2)}) collective-permute-start(bf16[16,2432]{1,0:T(8,128)(2,1)S(1)} %get-tuple-element.37), channel_id=1, source_target_pairs={{0,8},{2,10},{4,12},{6,14},{8,0},{10,2},{12,4},{14,6},{1,9},{3,11}... | collective-permute-start | bytes 233480 | tf_op jit(solution)/shard_map/ppermute | solution.py:295
  6.3 1.5 %collective-permute-start.1 = (bf16[16,2432]{1,0:T(8,128)(2,1)S(1)}, bf16[16,2432]{1,0:T(8,128)(2,1)S(1)}, u32[]{:S(2)}, u32[]{:S(2)}) collective-permute-start(bf16[16,2432]{1,0:T(8,128)(2,1)S(1)} %get-tuple-element.36.refs_0_), channel_id=1, source_target_pairs={{0,2},{2,0},{4,6},{6,4},{8,10},{10,8},{12,14},{14,12},{1,3},{3,1},... | collective-permute-start | bytes 233480 | tf_op jit(solution)/shard_map/ppermute | solution.py:295
  7.8 1.6 %collective-permute-start.5 = (bf16[16,2432]{1,0:T(8,128)(2,1)S(1)}, bf16[16,2432]{1,0:T(8,128)(2,1)S(1)}, u32[]{:S(2)}, u32[]{:S(2)}) collective-permute-start(bf16[16,2432]{1,0:T(8,128)(2,1)S(1)} %get-tuple-element.36.refs_0_), channel_id=1, source_target_pairs={{0,6},{2,4},{4,2},{6,0},{8,14},{10,12},{12,10},{14,8},{1,7},{3,5},... | collective-permute-start | bytes 233480 | tf_op jit(solution)/shard_map/ppermute | solution.py:295
  9.3 0.4 %collective-permute-start.3 = (bf16[16,2432]{1,0:T(8,128)(2,1)S(1)}, bf16[16,2432]{1,0:T(8,128)(2,1)S(1)}, u32[]{:S(2)}, u32[]{:S(2)}) collective-permute-start(bf16[16,2432]{1,0:T(8,128)(2,1)S(1)} %get-tuple-element.36.refs_0_), channel_id=1, source_target_pairs={{0,4},{2,6},{4,0},{6,2},{8,12},{10,14},{12,8},{14,10},{1,5},{3,7},... | collective-permute-start | bytes 233480 | tf_op jit(solution)/shard_map/ppermute | solution.py:295
  9.8 0.3 collective-permute-done.refs_1_
  10.1 2.2 %collective-permute-start.6 = (bf16[16,2432]{1,0:T(8,128)(2,1)S(1)}, bf16[16,2432]{1,0:T(8,128)(2,1)S(1)}, u32[]{:S(2)}, u32[]{:S(2)}) collective-permute-start(bf16[16,2432]{1,0:T(8,128)(2,1)S(1)} %collective-permute-done.refs_1_), channel_id=1, source_target_pairs={{0,6},{2,4},{4,2},{6,0},{8,14},{10,12},{12,10},{14,8},{1,7},{3,5},... | collective-permute-start | bytes 233480 | tf_op jit(solution)/shard_map/ppermute | solution.py:295
  12.3 1.1 %collective-permute-start.4 = (bf16[16,2432]{1,0:T(8,128)(2,1)S(1)}, bf16[16,2432]{1,0:T(8,128)(2,1)S(1)}, u32[]{:S(2)}, u32[]{:S(2)}) collective-permute-start(bf16[16,2432]{1,0:T(8,128)(2,1)S(1)} %collective-permute-done.refs_1_), channel_id=1, source_target_pairs={{0,4},{2,6},{4,0},{6,2},{8,12},{10,14},{12,8},{14,10},{1,5},{3,7},... | collective-permute-start | bytes 233480 | tf_op jit(solution)/shard_map/ppermute | solution.py:295
  13.4 0.0 collective-permute-done.1.refs_0_.refs_2_
  13.4 0.1 collective-permute-start.2
  13.6 2.4 %fetch.1 = (bf16[192,2048]{1,0:T(8,128)(2,1)S(1)}, bf16[192,2048]{1,0:T(8,128)(2,1)S(1)}, bf16[2048,576]{1,0:T(8,128)(2,1)S(1)}) custom-call(bf16[192,2048]{1,0:T(8,128)(2,1)} %bitcast.19, bf16[192,2048]{1,0:T(8,128)(2,1)} %bitcast.20, bf16[192,2048]{1,0:T(8,128)(2,1)} %bitcast.21, bf16[16,2432]{1,0:T(8,128)(2,1)S(1)} %collective-permute-done.1.refs_0_.refs_2_), custom_call_target="tpu_custom_call" | custom-call | bytes 2359296 | tf_op jit(solution)/shard_map/fetch/pallas_call | solution.py:281
  16.0 0.0 collective-permute-done.5.refs_6_
  16.0 0.0 collective-permute-done.3.refs_4_
  16.0 0.8 %collective-permute-done.6.refs_7_ = bf16[16,2432]{1,0:T(8,128)(2,1)S(1)} collective-permute-done((bf16[16,2432]{1,0:T(8,128)(2,1)S(1)}, bf16[16,2432]{1,0:T(8,128)(2,1)S(1)}, u32[]{:S(2)}, u32[]{:S(2)}) %collective-permute-start.6) | collective-permute-done | bytes 77856 | tf_op jit(solution)/shard_map/ppermute | solution.py:295
  16.8 0.0 collective-permute-done.4.refs_5_
  16.8 1.0 %collective-permute-done.2.refs_3_ = bf16[16,2432]{1,0:T(8,128)(2,1)S(1)} collective-permute-done((bf16[16,2432]{1,0:T(8,128)(2,1)S(1)}, bf16[16,2432]{1,0:T(8,128)(2,1)S(1)}, u32[]{:S(2)}, u32[]{:S(2)}) %collective-permute-start.2) | collective-permute-done | bytes 77856 | tf_op jit(solution)/shard_map/ppermute | solution.py:295
  17.8 0.0 copy-start
  17.8 1.2 %expert.1 = (bf16[8,2432]{1,0:T(8,128)(2,1)S(1)}, bf16[8,2432]{1,0:T(8,128)(2,1)S(1)}, bf16[8,2432]{1,0:T(8,128)(2,1)S(1)}, bf16[8,2432]{1,0:T(8,128)(2,1)S(1)},...) custom-call(bf16[16,2432]{1,0:T(8,128)(2,1)S(1)} %get-tuple-element., ...), custom_call_target="tpu_custom_call" | custom-call | flops 566231040 | bytes 2359296 | tf_op jit(solution)/shard_map/expert/pallas_call | solution.py:281
  19.0 1.1 %collective-permute-start.11 = (bf16[16,2432]{1,0:T(8,128)(2,1)S(1)}, bf16[16,2432]{1,0:T(8,128)(2,1)S(1)}, u32[]{:S(2)}, u32[]{:S(2)}) collective-permute-start(bf16[16,2432]{1,0:T(8,128)(2,1)S(1)} %get-tuple-element.49), channel_id=1, source_target_pairs={{0,6},{2,4},{4,2},{6,0},{8,14},{10,12},{12,10},{14,8},{1,7},{3,5},... | collective-permute-start | bytes 233480 | tf_op jit(solution)/shard_map/ppermute | solution.py:295
  20.1 0.9 %collective-permute-start.7 = (bf16[8,2432]{1,0:T(8,128)(2,1)S(1)}, bf16[8,2432]{1,0:T(8,128)(2,1)S(1)}, u32[]{:S(2)}, u32[]{:S(2)}) collective-permute-start(bf16[8,2432]{1,0:T(8,128)(2,1)S(1)} %get-tuple-element.43), channel_id=1, source_target_pairs={{0,4},{2,6},{4,0},{6,2},{8,12},{10,14},{12,8},{14,10},{1,5},{3,7},... | collective-permute-start | bytes 116744 | tf_op jit(solution)/shard_map/ppermute | solution.py:295
  21.0 1.6 %collective-permute-start.12 = (bf16[8,2432]{1,0:T(8,128)(2,1)S(1)}, bf16[8,2432]{1,0:T(8,128)(2,1)S(1)}, u32[]{:S(2)}, u32[]{:S(2)}) collective-permute-start(bf16[8,2432]{1,0:T(8,128)(2,1)S(1)} %get-tuple-element.57), channel_id=1, source_target_pairs={{0,2},{2,0},{4,6},{6,4},{8,10},{10,8},{12,14},{14,12},{1,3},{3,1},... | collective-permute-start | bytes 116744 | tf_op jit(solution)/shard_map/ppermute | solution.py:295
  22.6 1.0 %collective-permute-start.9 = (bf16[8,2432]{1,0:T(8,128)(2,1)S(1)}, bf16[8,2432]{1,0:T(8,128)(2,1)S(1)}, u32[]{:S(2)}, u32[]{:S(2)}) collective-permute-start(bf16[8,2432]{1,0:T(8,128)(2,1)S(1)} %get-tuple-element.45), channel_id=1, source_target_pairs={{0,4},{2,6},{4,0},{6,2},{8,12},{10,14},{12,8},{14,10},{1,5},{3,7},... | collective-permute-start | bytes 116744 | tf_op jit(solution)/shard_map/ppermute | solution.py:295
  23.6 0.6 %collective-permute-start.10 = (bf16[8,2432]{1,0:T(8,128)(2,1)S(1)}, bf16[8,2432]{1,0:T(8,128)(2,1)S(1)}, u32[]{:S(2)}, u32[]{:S(2)}) collective-permute-start(bf16[8,2432]{1,0:T(8,128)(2,1)S(1)} %get-tuple-element.46), channel_id=1, source_target_pairs={{0,2},{2,0},{4,6},{6,4},{8,10},{10,8},{12,14},{14,12},{1,3},{3,1},... | collective-permute-start | bytes 116744 | tf_op jit(solution)/shard_map/ppermute | solution.py:295
  24.1 0.0 collective-permute-done.7
  24.1 0.0 collective-permute-start.8
  24.1 0.8 %collective-permute-done.12 = bf16[8,2432]{1,0:T(8,128)(2,1)S(1)} collective-permute-done((bf16[8,2432]{1,0:T(8,128)(2,1)S(1)}, bf16[8,2432]{1,0:T(8,128)(2,1)S(1)}, u32[]{:S(2)}, u32[]{:S(2)}) %collective-permute-start.12) | collective-permute-done | bytes 38944 | tf_op jit(solution)/shard_map/ppermute | solution.py:295
  25.0 0.0 collective-permute-done.11.o3
  25.0 2.9 %collective-permute-start.13 = (bf16[8,2432]{1,0:T(8,128)(2,1)S(1)}, bf16[8,2432]{1,0:T(8,128)(2,1)S(1)}, u32[]{:S(2)}, u32[]{:S(2)}) collective-permute-start(bf16[8,2432]{1,0:T(8,128)(2,1)S(1)} %add_convert_fusion), channel_id=1, source_target_pairs={{0,8},{2,10},{4,12},{6,14},{8,0},{10,2},{12,4},{14,6},{1,9},{3,11}... | collective-permute-start | bytes 116744 | tf_op jit(solution)/shard_map/ppermute | solution.py:295
  27.9 0.0 collective-permute-done.9.o2
  27.9 0.0 collective-permute-done.10.o1
  27.9 0.0 collective-permute-done.8.peer_ref
  27.9 1.6 %weights.1 = (bf16[192,1024]{1,0:T(8,128)(2,1)}, bf16[192,1024]{1,0:T(8,128)(2,1)}, bf16[192,1024]{1,0:T(8,128)(2,1)}) custom-call(bf16[144,1024]{1,0:T(8,128)(2,1)S(1)} %get-tuple-element.50.keep_ref, bf16[144,576]{1,0:T(8,128)(2,1)S(1)} %get-tuple-element.51.hid_ref, bf16[144,1600]{1,0:T(8,128)(2,1)S(1)} %collective-permute-done.8.peer_ref), custom_call_target="tpu_custom_call" | custom-call | flops 339738624 | bytes 1179648 | tf_op jit(solution)/shard_map/weights/pallas_call | solution.py:281
  29.5 0.8 %collective-permute-done.13.rest_0_ = bf16[8,2432]{1,0:T(8,128)(2,1)S(1)} collective-permute-done((bf16[8,2432]{1,0:T(8,128)(2,1)S(1)}, bf16[8,2432]{1,0:T(8,128)(2,1)S(1)}, u32[]{:S(2)}, u32[]{:S(2)}) %collective-permute-start.13) | collective-permute-done | bytes 38944 | tf_op jit(solution)/shard_map/ppermute | solution.py:295
  30.3 0.0 copy-done
  30.3 1.1 %finish.1 = (bf16[128,2048]{1,0:T(8,128)(2,1)}, f32[8,128]{1,0:T(8,128)}) custom-call(s32[8,128]{1,0:T(8,128)S(1)} %bitcast.18, f32[8,128]{1,0:T(8,128)S(1)} %get-tuple-element.35.rank_ref, bf16[8,2432]{1,0:T(8,128)(2,1)S(1)} %get-tuple-element.41.o0, bf16[8,2432]{1,0:T(8,128)(2,1)S(1)} %collective-permute-done.10.o1, ...), custom_call_target="tpu_custom_call" | custom-call | flops 50331648 | bytes 524288 | tf_op jit(solution)/shard_map/finish/pallas_call | solution.py:281
  (1 shorter events, 0.0 us)
Async XLA Ops:
  2.2 7.9 %collective-permute-start = (bf16[16,2432]{1,0:T(8,128)(2,1)S(1)}, bf16[16,2432]{1,0:T(8,128)(2,1)S(1)}, u32[]{:S(2)}, u32[]{:S(2)}) collective-permute-start(bf16[16,2432]{1,0:T(8,128)(2,1)S(1)} %get-tuple-element.37), channel_id=1, source_target_pairs={{0,8},{2,10},{4,12},{6,14},{8,0},{10,2},{12,4},{14,6},{1,9},{3,11}... | collective-permute-start | bytes 233480 | tf_op jit(solution)/shard_map/ppermute | solution.py:295
  6.3 7.1 %collective-permute-start.1 = (bf16[16,2432]{1,0:T(8,128)(2,1)S(1)}, bf16[16,2432]{1,0:T(8,128)(2,1)S(1)}, u32[]{:S(2)}, u32[]{:S(2)}) collective-permute-start(bf16[16,2432]{1,0:T(8,128)(2,1)S(1)} %get-tuple-element.36.refs_0_), channel_id=1, source_target_pairs={{0,2},{2,0},{4,6},{6,4},{8,10},{10,8},{12,14},{14,12},{1,3},{3,1},... | collective-permute-start | bytes 233480 | tf_op jit(solution)/shard_map/ppermute | solution.py:295
  7.8 8.2 %collective-permute-start.5 = (bf16[16,2432]{1,0:T(8,128)(2,1)S(1)}, bf16[16,2432]{1,0:T(8,128)(2,1)S(1)}, u32[]{:S(2)}, u32[]{:S(2)}) collective-permute-start(bf16[16,2432]{1,0:T(8,128)(2,1)S(1)} %get-tuple-element.36.refs_0_), channel_id=1, source_target_pairs={{0,6},{2,4},{4,2},{6,0},{8,14},{10,12},{12,10},{14,8},{1,7},{3,5},... | collective-permute-start | bytes 233480 | tf_op jit(solution)/shard_map/ppermute | solution.py:295
  9.3 6.7 %collective-permute-start.3 = (bf16[16,2432]{1,0:T(8,128)(2,1)S(1)}, bf16[16,2432]{1,0:T(8,128)(2,1)S(1)}, u32[]{:S(2)}, u32[]{:S(2)}) collective-permute-start(bf16[16,2432]{1,0:T(8,128)(2,1)S(1)} %get-tuple-element.36.refs_0_), channel_id=1, source_target_pairs={{0,4},{2,6},{4,0},{6,2},{8,12},{10,14},{12,8},{14,10},{1,5},{3,7},... | collective-permute-start | bytes 233480 | tf_op jit(solution)/shard_map/ppermute | solution.py:295
  10.1 6.8 %collective-permute-start.6 = (bf16[16,2432]{1,0:T(8,128)(2,1)S(1)}, bf16[16,2432]{1,0:T(8,128)(2,1)S(1)}, u32[]{:S(2)}, u32[]{:S(2)}) collective-permute-start(bf16[16,2432]{1,0:T(8,128)(2,1)S(1)} %collective-permute-done.refs_1_), channel_id=1, source_target_pairs={{0,6},{2,4},{4,2},{6,0},{8,14},{10,12},{12,10},{14,8},{1,7},{3,5},... | collective-permute-start | bytes 233480 | tf_op jit(solution)/shard_map/ppermute | solution.py:295
  12.3 4.6 %collective-permute-start.4 = (bf16[16,2432]{1,0:T(8,128)(2,1)S(1)}, bf16[16,2432]{1,0:T(8,128)(2,1)S(1)}, u32[]{:S(2)}, u32[]{:S(2)}) collective-permute-start(bf16[16,2432]{1,0:T(8,128)(2,1)S(1)} %collective-permute-done.refs_1_), channel_id=1, source_target_pairs={{0,4},{2,6},{4,0},{6,2},{8,12},{10,14},{12,8},{14,10},{1,5},{3,7},... | collective-permute-start | bytes 233480 | tf_op jit(solution)/shard_map/ppermute | solution.py:295
  13.4 4.4 %collective-permute-start.2 = (bf16[16,2432]{1,0:T(8,128)(2,1)S(1)}, bf16[16,2432]{1,0:T(8,128)(2,1)S(1)}, u32[]{:S(2)}, u32[]{:S(2)}) collective-permute-start(bf16[16,2432]{1,0:T(8,128)(2,1)S(1)} %collective-permute-done.refs_1_), channel_id=1, source_target_pairs={{0,2},{2,0},{4,6},{6,4},{8,10},{10,8},{12,14},{14,12},{1,3},{3,1},... | collective-permute-start | bytes 233480 | tf_op jit(solution)/shard_map/ppermute | solution.py:295
  17.8 12.4 %copy-start = (s32[128,8]{0,1:T(8,128)S(1)}, s32[128,8]{0,1:T(8,128)}, u32[]{:S(2)}) copy-start(s32[128,8]{0,1:T(8,128)} %param.9) | copy-start | bytes 12292
  19.0 5.9 %collective-permute-start.11 = (bf16[16,2432]{1,0:T(8,128)(2,1)S(1)}, bf16[16,2432]{1,0:T(8,128)(2,1)S(1)}, u32[]{:S(2)}, u32[]{:S(2)}) collective-permute-start(bf16[16,2432]{1,0:T(8,128)(2,1)S(1)} %get-tuple-element.49), channel_id=1, source_target_pairs={{0,6},{2,4},{4,2},{6,0},{8,14},{10,12},{12,10},{14,8},{1,7},{3,5},... | collective-permute-start | bytes 233480 | tf_op jit(solution)/shard_map/ppermute | solution.py:295
  20.1 4.1 %collective-permute-start.7 = (bf16[8,2432]{1,0:T(8,128)(2,1)S(1)}, bf16[8,2432]{1,0:T(8,128)(2,1)S(1)}, u32[]{:S(2)}, u32[]{:S(2)}) collective-permute-start(bf16[8,2432]{1,0:T(8,128)(2,1)S(1)} %get-tuple-element.43), channel_id=1, source_target_pairs={{0,4},{2,6},{4,0},{6,2},{8,12},{10,14},{12,8},{14,10},{1,5},{3,7},... | collective-permute-start | bytes 116744 | tf_op jit(solution)/shard_map/ppermute | solution.py:295
  21.0 4.0 %collective-permute-start.12 = (bf16[8,2432]{1,0:T(8,128)(2,1)S(1)}, bf16[8,2432]{1,0:T(8,128)(2,1)S(1)}, u32[]{:S(2)}, u32[]{:S(2)}) collective-permute-start(bf16[8,2432]{1,0:T(8,128)(2,1)S(1)} %get-tuple-element.57), channel_id=1, source_target_pairs={{0,2},{2,0},{4,6},{6,4},{8,10},{10,8},{12,14},{14,12},{1,3},{3,1},... | collective-permute-start | bytes 116744 | tf_op jit(solution)/shard_map/ppermute | solution.py:295
  22.6 5.3 %collective-permute-start.9 = (bf16[8,2432]{1,0:T(8,128)(2,1)S(1)}, bf16[8,2432]{1,0:T(8,128)(2,1)S(1)}, u32[]{:S(2)}, u32[]{:S(2)}) collective-permute-start(bf16[8,2432]{1,0:T(8,128)(2,1)S(1)} %get-tuple-element.45), channel_id=1, source_target_pairs={{0,4},{2,6},{4,0},{6,2},{8,12},{10,14},{12,8},{14,10},{1,5},{3,7},... | collective-permute-start | bytes 116744 | tf_op jit(solution)/shard_map/ppermute | solution.py:295
  23.6 4.3 %collective-permute-start.10 = (bf16[8,2432]{1,0:T(8,128)(2,1)S(1)}, bf16[8,2432]{1,0:T(8,128)(2,1)S(1)}, u32[]{:S(2)}, u32[]{:S(2)}) collective-permute-start(bf16[8,2432]{1,0:T(8,128)(2,1)S(1)} %get-tuple-element.46), channel_id=1, source_target_pairs={{0,2},{2,0},{4,6},{6,4},{8,10},{10,8},{12,14},{14,12},{1,3},{3,1},... | collective-permute-start | bytes 116744 | tf_op jit(solution)/shard_map/ppermute | solution.py:295
  24.1 3.7 %collective-permute-start.8 = (bf16[144,1600]{1,0:T(8,128)(2,1)S(1)}, bf16[144,1600]{1,0:T(8,128)(2,1)S(1)}, u32[]{:S(2)}, u32[]{:S(2)}) collective-permute-start(bf16[144,1600]{1,0:T(8,128)(2,1)S(1)} %get-tuple-element.44), channel_id=1, source_target_pairs={{0,1},{1,0},{2,3},{3,2},{4,5},{5,4},{6,7},{7,6},{8,9},{9,8},{10,11... | collective-permute-start | bytes 1382408 | tf_op jit(solution)/shard_map/ppermute | solution.py:367
  25.0 5.3 %collective-permute-start.13 = (bf16[8,2432]{1,0:T(8,128)(2,1)S(1)}, bf16[8,2432]{1,0:T(8,128)(2,1)S(1)}, u32[]{:S(2)}, u32[]{:S(2)}) collective-permute-start(bf16[8,2432]{1,0:T(8,128)(2,1)S(1)} %add_convert_fusion), channel_id=1, source_target_pairs={{0,8},{2,10},{4,12},{6,14},{8,0},{10,2},{12,4},{14,6},{1,9},{3,11}... | collective-permute-start | bytes 116744 | tf_op jit(solution)/shard_map/ppermute | solution.py:295

commit v10 on v9

--- a/solution.py
+++ b/solution.py
@@ -326,11 +326,11 @@
         fetch_kernel,
         [(wg.shape, BF16), (wu.shape, BF16), ((features, 3 * hidden), BF16)],
         "fetch",
-        (wg, wu, wd, near[1]),
+        (wg, wu, wd, near[1], near[2]),
         0,
         6 * features * hidden,
         12,
-        [HBM] * 3 + [ANY],
+        [HBM] * 3 + [ANY] * 2,
         [pltpu.VMEM(wd.shape, BF16), pltpu.SemaphoreType.DMA((3,))],
     )
     from_far = arrived[0] if window == 2 else jnp.concatenate(arrived, axis=0)

time: 31.5 us -> 31.7 us (level)
  waiting for transfers between devices: 3.72 us -> 4.29 us
  starting transfers between devices: 19.1 us -> 18.7 us
    ppermute x13, waiting for transfers between devices: 3.71 us -> 4.28 us  [swap_by(): return lax.ppermute(block, 'expert', [(i, i ^ mask) for i in range(count)])]
    ppermute x13, starting transfers between devices: 19.1 us -> 18.7 us  [swap_by(): return lax.ppermute(block, 'expert', [(i, i ^ mask) for i in range(count)])]
where the time goes in v10:
time: 31.7 us; the launch traced here: 31.5 us
  starting transfers between devices  18.7 us (59%)
  Pallas kernels  7.82 us (25%)
  waiting for transfers between devices  4.29 us (14%)
  between operations  0.69 us (2%)
    ppermute x13, starting transfers between devices, swap_by(): return lax.ppermute(block, 'expert', [(i, i ^ mask) for i in range(count)])  18.7 us
    pallas_call x5, Pallas kernels, call(): pl.pallas_call(kernel, out_shape=[jax.ShapeDtypeStruct(s, t) for s, t in...  7.82 us
    ppermute x13, waiting for transfers between devices, swap_by(): return lax.ppermute(block, 'expert', [(i, i ^ mask) for i in range(count)])  4.28 us
  transfers between devices with their start and end apart: 14, of which 5 were waited for; matrix products, arithmetic and copies ran while one was open for 0% of the time, Pallas kernels for 13%

profile of v10, /device:TPU:0, one launch (start us, length us, event | category | flops | bytes accessed | tf_op | source)
XLA Modules:
  0.0 31.5 jit_solution(13649334008952287033)
XLA Ops:
  0.6 1.5 %pack.1 = (bf16[16,2432]{1,0:T(8,128)(2,1)S(1)}, bf16[16,2432]{1,0:T(8,128)(2,1)S(1)}, f32[8,128]{1,0:T(8,128)S(1)}) custom-call(s32[8,128]{1,0:T(8,128)} %bitcast.17, bf16[8,128]{1,0:T(8,128)(2,1)} %bitcast.22, bf16[128,2048]{1,0:T(8,128)(2,1)} %tok_hbm.1, bf16[128,2048]{1,0:T(8,128)(2,1)} %grad_hbm.1), custom_call_target="tpu_custom_call" | custom-call | flops 18874368 | bytes 1048576 | tf_op jit(solution)/shard_map/pack/pallas_call | solution.py:281
  2.2 4.1 %collective-permute-start = (bf16[16,2432]{1,0:T(8,128)(2,1)S(1)}, bf16[16,2432]{1,0:T(8,128)(2,1)S(1)}, u32[]{:S(2)}, u32[]{:S(2)}) collective-permute-start(bf16[16,2432]{1,0:T(8,128)(2,1)S(1)} %get-tuple-element.37), channel_id=1, source_target_pairs={{0,8},{2,10},{4,12},{6,14},{8,0},{10,2},{12,4},{14,6},{1,9},{3,11}... | collective-permute-start | bytes 233480 | tf_op jit(solution)/shard_map/ppermute | solution.py:295
  6.3 1.6 %collective-permute-start.3 = (bf16[16,2432]{1,0:T(8,128)(2,1)S(1)}, bf16[16,2432]{1,0:T(8,128)(2,1)S(1)}, u32[]{:S(2)}, u32[]{:S(2)}) collective-permute-start(bf16[16,2432]{1,0:T(8,128)(2,1)S(1)} %get-tuple-element.36.refs_0_), channel_id=1, source_target_pairs={{0,4},{2,6},{4,0},{6,2},{8,12},{10,14},{12,8},{14,10},{1,5},{3,7},... | collective-permute-start | bytes 233480 | tf_op jit(solution)/shard_map/ppermute | solution.py:295
  7.9 1.5 %collective-permute-start.1 = (bf16[16,2432]{1,0:T(8,128)(2,1)S(1)}, bf16[16,2432]{1,0:T(8,128)(2,1)S(1)}, u32[]{:S(2)}, u32[]{:S(2)}) collective-permute-start(bf16[16,2432]{1,0:T(8,128)(2,1)S(1)} %get-tuple-element.36.refs_0_), channel_id=1, source_target_pairs={{0,2},{2,0},{4,6},{6,4},{8,10},{10,8},{12,14},{14,12},{1,3},{3,1},... | collective-permute-start | bytes 233480 | tf_op jit(solution)/shard_map/ppermute | solution.py:295
  9.3 0.4 %collective-permute-start.5 = (bf16[16,2432]{1,0:T(8,128)(2,1)S(1)}, bf16[16,2432]{1,0:T(8,128)(2,1)S(1)}, u32[]{:S(2)}, u32[]{:S(2)}) collective-permute-start(bf16[16,2432]{1,0:T(8,128)(2,1)S(1)} %get-tuple-element.36.refs_0_), channel_id=1, source_target_pairs={{0,6},{2,4},{4,2},{6,0},{8,14},{10,12},{12,10},{14,8},{1,7},{3,5},... | collective-permute-start | bytes 233480 | tf_op jit(solution)/shard_map/ppermute | solution.py:295
  9.8 0.0 collective-permute-done.refs_1_
  9.8 2.5 %collective-permute-start.6 = (bf16[16,2432]{1,0:T(8,128)(2,1)S(1)}, bf16[16,2432]{1,0:T(8,128)(2,1)S(1)}, u32[]{:S(2)}, u32[]{:S(2)}) collective-permute-start(bf16[16,2432]{1,0:T(8,128)(2,1)S(1)} %collective-permute-done.refs_1_), channel_id=1, source_target_pairs={{0,6},{2,4},{4,2},{6,0},{8,14},{10,12},{12,10},{14,8},{1,7},{3,5},... | collective-permute-start | bytes 233480 | tf_op jit(solution)/shard_map/ppermute | solution.py:295
  12.3 0.9 %collective-permute-start.4 = (bf16[16,2432]{1,0:T(8,128)(2,1)S(1)}, bf16[16,2432]{1,0:T(8,128)(2,1)S(1)}, u32[]{:S(2)}, u32[]{:S(2)}) collective-permute-start(bf16[16,2432]{1,0:T(8,128)(2,1)S(1)} %collective-permute-done.refs_1_), channel_id=1, source_target_pairs={{0,4},{2,6},{4,0},{6,2},{8,12},{10,14},{12,8},{14,10},{1,5},{3,7},... | collective-permute-start | bytes 233480 | tf_op jit(solution)/shard_map/ppermute | solution.py:295
  13.2 0.0 collective-permute-done.3.refs_1_.refs_4_
  13.2 0.1 collective-permute-start.2
  13.3 0.9 %collective-permute-done.1.refs_0_.refs_2_ = bf16[16,2432]{1,0:T(8,128)(2,1)S(1)} collective-permute-done((bf16[16,2432]{1,0:T(8,128)(2,1)S(1)}, bf16[16,2432]{1,0:T(8,128)(2,1)S(1)}, u32[]{:S(2)}, u32[]{:S(2)}) %collective-permute-start.1) | collective-permute-done | bytes 77856 | tf_op jit(solution)/shard_map/ppermute | solution.py:295
  14.2 2.4 %fetch.1 = (bf16[192,2048]{1,0:T(8,128)(2,1)S(1)}, bf16[192,2048]{1,0:T(8,128)(2,1)S(1)}, bf16[2048,576]{1,0:T(8,128)(2,1)S(1)}) custom-call(bf16[192,2048]{1,0:T(8,128)(2,1)} %bitcast.19, bf16[192,2048]{1,0:T(8,128)(2,1)} %bitcast.20, bf16[192,2048]{1,0:T(8,128)(2,1)} %bitcast.21, bf16[16,2432]{1,0:T(8,128)(2,1)S(1)} %collective-permute-done.1.refs_0_.refs_2_, ...), custom_call_target="tpu_custom_call" | custom-call | bytes 2359296 | tf_op jit(solution)/shard_map/fetch/pallas_call | solution.py:281
  16.6 0.0 collective-permute-done.5.refs_6_
  16.7 0.0 collective-permute-done.6.refs_7_
  16.7 0.0 collective-permute-done.4.refs_5_
  16.7 0.9 %collective-permute-done.2.refs_3_ = bf16[16,2432]{1,0:T(8,128)(2,1)S(1)} collective-permute-done((bf16[16,2432]{1,0:T(8,128)(2,1)S(1)}, bf16[16,2432]{1,0:T(8,128)(2,1)S(1)}, u32[]{:S(2)}, u32[]{:S(2)}) %collective-permute-start.2) | collective-permute-done | bytes 77856 | tf_op jit(solution)/shard_map/ppermute | solution.py:295
  17.6 0.0 copy-start
  17.6 1.2 %expert.1 = (bf16[8,2432]{1,0:T(8,128)(2,1)S(1)}, bf16[8,2432]{1,0:T(8,128)(2,1)S(1)}, bf16[8,2432]{1,0:T(8,128)(2,1)S(1)}, bf16[8,2432]{1,0:T(8,128)(2,1)S(1)},...) custom-call(bf16[16,2432]{1,0:T(8,128)(2,1)S(1)} %get-tuple-element., ...), custom_call_target="tpu_custom_call" | custom-call | flops 566231040 | bytes 2359296 | tf_op jit(solution)/shard_map/expert/pallas_call | solution.py:281
  18.8 1.2 %collective-permute-start.11 = (bf16[16,2432]{1,0:T(8,128)(2,1)S(1)}, bf16[16,2432]{1,0:T(8,128)(2,1)S(1)}, u32[]{:S(2)}, u32[]{:S(2)}) collective-permute-start(bf16[16,2432]{1,0:T(8,128)(2,1)S(1)} %get-tuple-element.49), channel_id=1, source_target_pairs={{0,6},{2,4},{4,2},{6,0},{8,14},{10,12},{12,10},{14,8},{1,7},{3,5},... | collective-permute-start | bytes 233480 | tf_op jit(solution)/shard_map/ppermute | solution.py:295
  19.9 1.5 %collective-permute-start.7 = (bf16[8,2432]{1,0:T(8,128)(2,1)S(1)}, bf16[8,2432]{1,0:T(8,128)(2,1)S(1)}, u32[]{:S(2)}, u32[]{:S(2)}) collective-permute-start(bf16[8,2432]{1,0:T(8,128)(2,1)S(1)} %get-tuple-element.43), channel_id=1, source_target_pairs={{0,4},{2,6},{4,0},{6,2},{8,12},{10,14},{12,8},{14,10},{1,5},{3,7},... | collective-permute-start | bytes 116744 | tf_op jit(solution)/shard_map/ppermute | solution.py:295
  21.4 0.9 %collective-permute-start.12 = (bf16[8,2432]{1,0:T(8,128)(2,1)S(1)}, bf16[8,2432]{1,0:T(8,128)(2,1)S(1)}, u32[]{:S(2)}, u32[]{:S(2)}) collective-permute-start(bf16[8,2432]{1,0:T(8,128)(2,1)S(1)} %get-tuple-element.57), channel_id=1, source_target_pairs={{0,2},{2,0},{4,6},{6,4},{8,10},{10,8},{12,14},{14,12},{1,3},{3,1},... | collective-permute-start | bytes 116744 | tf_op jit(solution)/shard_map/ppermute | solution.py:295
  22.3 1.1 %collective-permute-start.9 = (bf16[8,2432]{1,0:T(8,128)(2,1)S(1)}, bf16[8,2432]{1,0:T(8,128)(2,1)S(1)}, u32[]{:S(2)}, u32[]{:S(2)}) collective-permute-start(bf16[8,2432]{1,0:T(8,128)(2,1)S(1)} %get-tuple-element.45), channel_id=1, source_target_pairs={{0,4},{2,6},{4,0},{6,2},{8,12},{10,14},{12,8},{14,10},{1,5},{3,7},... | collective-permute-start | bytes 116744 | tf_op jit(solution)/shard_map/ppermute | solution.py:295
  23.5 0.5 %collective-permute-start.10 = (bf16[8,2432]{1,0:T(8,128)(2,1)S(1)}, bf16[8,2432]{1,0:T(8,128)(2,1)S(1)}, u32[]{:S(2)}, u32[]{:S(2)}) collective-permute-start(bf16[8,2432]{1,0:T(8,128)(2,1)S(1)} %get-tuple-element.46), channel_id=1, source_target_pairs={{0,2},{2,0},{4,6},{6,4},{8,10},{10,8},{12,14},{14,12},{1,3},{3,1},... | collective-permute-start | bytes 116744 | tf_op jit(solution)/shard_map/ppermute | solution.py:295
  24.0 0.7 %collective-permute-done.7 = bf16[8,2432]{1,0:T(8,128)(2,1)S(1)} collective-permute-done((bf16[8,2432]{1,0:T(8,128)(2,1)S(1)}, bf16[8,2432]{1,0:T(8,128)(2,1)S(1)}, u32[]{:S(2)}, u32[]{:S(2)}) %collective-permute-start.7) | collective-permute-done | bytes 38944 | tf_op jit(solution)/shard_map/ppermute | solution.py:295
  24.7 0.0 collective-permute-start.8
  24.7 0.8 %collective-permute-done.12 = bf16[8,2432]{1,0:T(8,128)(2,1)S(1)} collective-permute-done((bf16[8,2432]{1,0:T(8,128)(2,1)S(1)}, bf16[8,2432]{1,0:T(8,128)(2,1)S(1)}, u32[]{:S(2)}, u32[]{:S(2)}) %collective-permute-start.12) | collective-permute-done | bytes 38944 | tf_op jit(solution)/shard_map/ppermute | solution.py:295
  25.4 0.0 collective-permute-done.11.o3
  25.5 2.4 %collective-permute-start.13 = (bf16[8,2432]{1,0:T(8,128)(2,1)S(1)}, bf16[8,2432]{1,0:T(8,128)(2,1)S(1)}, u32[]{:S(2)}, u32[]{:S(2)}) collective-permute-start(bf16[8,2432]{1,0:T(8,128)(2,1)S(1)} %add_convert_fusion), channel_id=1, source_target_pairs={{0,8},{2,10},{4,12},{6,14},{8,0},{10,2},{12,4},{14,6},{1,9},{3,11}... | collective-permute-start | bytes 116744 | tf_op jit(solution)/shard_map/ppermute | solution.py:295
  27.8 0.0 collective-permute-done.9.o2
  27.8 0.0 collective-permute-done.10.o1
  27.8 0.0 collective-permute-done.8.peer_ref
  27.8 1.6 %weights.1 = (bf16[192,1024]{1,0:T(8,128)(2,1)}, bf16[192,1024]{1,0:T(8,128)(2,1)}, bf16[192,1024]{1,0:T(8,128)(2,1)}) custom-call(bf16[144,1024]{1,0:T(8,128)(2,1)S(1)} %get-tuple-element.50.keep_ref, bf16[144,576]{1,0:T(8,128)(2,1)S(1)} %get-tuple-element.51.hid_ref, bf16[144,1600]{1,0:T(8,128)(2,1)S(1)} %collective-permute-done.8.peer_ref), custom_call_target="tpu_custom_call" | custom-call | flops 339738624 | bytes 1179648 | tf_op jit(solution)/shard_map/weights/pallas_call | solution.py:281
  29.4 1.0 %collective-permute-done.13.rest_0_ = bf16[8,2432]{1,0:T(8,128)(2,1)S(1)} collective-permute-done((bf16[8,2432]{1,0:T(8,128)(2,1)S(1)}, bf16[8,2432]{1,0:T(8,128)(2,1)S(1)}, u32[]{:S(2)}, u32[]{:S(2)}) %collective-permute-start.13) | collective-permute-done | bytes 38944 | tf_op jit(solution)/shard_map/ppermute | solution.py:295
  30.4 0.0 copy-done
  30.4 1.1 %finish.1 = (bf16[128,2048]{1,0:T(8,128)(2,1)}, f32[8,128]{1,0:T(8,128)}) custom-call(s32[8,128]{1,0:T(8,128)S(1)} %bitcast.18, f32[8,128]{1,0:T(8,128)S(1)} %get-tuple-element.35.rank_ref, bf16[8,2432]{1,0:T(8,128)(2,1)S(1)} %get-tuple-element.41.o0, bf16[8,2432]{1,0:T(8,128)(2,1)S(1)} %collective-permute-done.10.o1, ...), custom_call_target="tpu_custom_call" | custom-call | flops 50331648 | bytes 524288 | tf_op jit(solution)/shard_map/finish/pallas_call | solution.py:281
  (1 shorter events, 0.0 us)
Async XLA Ops:
  2.2 7.6 %collective-permute-start = (bf16[16,2432]{1,0:T(8,128)(2,1)S(1)}, bf16[16,2432]{1,0:T(8,128)(2,1)S(1)}, u32[]{:S(2)}, u32[]{:S(2)}) collective-permute-start(bf16[16,2432]{1,0:T(8,128)(2,1)S(1)} %get-tuple-element.37), channel_id=1, source_target_pairs={{0,8},{2,10},{4,12},{6,14},{8,0},{10,2},{12,4},{14,6},{1,9},{3,11}... | collective-permute-start | bytes 233480 | tf_op jit(solution)/shard_map/ppermute | solution.py:295
  6.3 6.9 %collective-permute-start.3 = (bf16[16,2432]{1,0:T(8,128)(2,1)S(1)}, bf16[16,2432]{1,0:T(8,128)(2,1)S(1)}, u32[]{:S(2)}, u32[]{:S(2)}) collective-permute-start(bf16[16,2432]{1,0:T(8,128)(2,1)S(1)} %get-tuple-element.36.refs_0_), channel_id=1, source_target_pairs={{0,4},{2,6},{4,0},{6,2},{8,12},{10,14},{12,8},{14,10},{1,5},{3,7},... | collective-permute-start | bytes 233480 | tf_op jit(solution)/shard_map/ppermute | solution.py:295
  7.9 6.3 %collective-permute-start.1 = (bf16[16,2432]{1,0:T(8,128)(2,1)S(1)}, bf16[16,2432]{1,0:T(8,128)(2,1)S(1)}, u32[]{:S(2)}, u32[]{:S(2)}) collective-permute-start(bf16[16,2432]{1,0:T(8,128)(2,1)S(1)} %get-tuple-element.36.refs_0_), channel_id=1, source_target_pairs={{0,2},{2,0},{4,6},{6,4},{8,10},{10,8},{12,14},{14,12},{1,3},{3,1},... | collective-permute-start | bytes 233480 | tf_op jit(solution)/shard_map/ppermute | solution.py:295
  9.3 7.3 %collective-permute-start.5 = (bf16[16,2432]{1,0:T(8,128)(2,1)S(1)}, bf16[16,2432]{1,0:T(8,128)(2,1)S(1)}, u32[]{:S(2)}, u32[]{:S(2)}) collective-permute-start(bf16[16,2432]{1,0:T(8,128)(2,1)S(1)} %get-tuple-element.36.refs_0_), channel_id=1, source_target_pairs={{0,6},{2,4},{4,2},{6,0},{8,14},{10,12},{12,10},{14,8},{1,7},{3,5},... | collective-permute-start | bytes 233480 | tf_op jit(solution)/shard_map/ppermute | solution.py:295
  9.8 6.9 %collective-permute-start.6 = (bf16[16,2432]{1,0:T(8,128)(2,1)S(1)}, bf16[16,2432]{1,0:T(8,128)(2,1)S(1)}, u32[]{:S(2)}, u32[]{:S(2)}) collective-permute-start(bf16[16,2432]{1,0:T(8,128)(2,1)S(1)} %collective-permute-done.refs_1_), channel_id=1, source_target_pairs={{0,6},{2,4},{4,2},{6,0},{8,14},{10,12},{12,10},{14,8},{1,7},{3,5},... | collective-permute-start | bytes 233480 | tf_op jit(solution)/shard_map/ppermute | solution.py:295
  12.3 4.4 %collective-permute-start.4 = (bf16[16,2432]{1,0:T(8,128)(2,1)S(1)}, bf16[16,2432]{1,0:T(8,128)(2,1)S(1)}, u32[]{:S(2)}, u32[]{:S(2)}) collective-permute-start(bf16[16,2432]{1,0:T(8,128)(2,1)S(1)} %collective-permute-done.refs_1_), channel_id=1, source_target_pairs={{0,4},{2,6},{4,0},{6,2},{8,12},{10,14},{12,8},{14,10},{1,5},{3,7},... | collective-permute-start | bytes 233480 | tf_op jit(solution)/shard_map/ppermute | solution.py:295
  13.2 4.4 %collective-permute-start.2 = (bf16[16,2432]{1,0:T(8,128)(2,1)S(1)}, bf16[16,2432]{1,0:T(8,128)(2,1)S(1)}, u32[]{:S(2)}, u32[]{:S(2)}) collective-permute-start(bf16[16,2432]{1,0:T(8,128)(2,1)S(1)} %collective-permute-done.refs_1_), channel_id=1, source_target_pairs={{0,2},{2,0},{4,6},{6,4},{8,10},{10,8},{12,14},{14,12},{1,3},{3,1},... | collective-permute-start | bytes 233480 | tf_op jit(solution)/shard_map/ppermute | solution.py:295
  17.6 12.8 %copy-start = (s32[128,8]{0,1:T(8,128)S(1)}, s32[128,8]{0,1:T(8,128)}, u32[]{:S(2)}) copy-start(s32[128,8]{0,1:T(8,128)} %param.9) | copy-start | bytes 12292
  18.8 6.7 %collective-permute-start.11 = (bf16[16,2432]{1,0:T(8,128)(2,1)S(1)}, bf16[16,2432]{1,0:T(8,128)(2,1)S(1)}, u32[]{:S(2)}, u32[]{:S(2)}) collective-permute-start(bf16[16,2432]{1,0:T(8,128)(2,1)S(1)} %get-tuple-element.49), channel_id=1, source_target_pairs={{0,6},{2,4},{4,2},{6,0},{8,14},{10,12},{12,10},{14,8},{1,7},{3,5},... | collective-permute-start | bytes 233480 | tf_op jit(solution)/shard_map/ppermute | solution.py:295
  19.9 4.7 %collective-permute-start.7 = (bf16[8,2432]{1,0:T(8,128)(2,1)S(1)}, bf16[8,2432]{1,0:T(8,128)(2,1)S(1)}, u32[]{:S(2)}, u32[]{:S(2)}) collective-permute-start(bf16[8,2432]{1,0:T(8,128)(2,1)S(1)} %get-tuple-element.43), channel_id=1, source_target_pairs={{0,4},{2,6},{4,0},{6,2},{8,12},{10,14},{12,8},{14,10},{1,5},{3,7},... | collective-permute-start | bytes 116744 | tf_op jit(solution)/shard_map/ppermute | solution.py:295
  21.4 4.0 %collective-permute-start.12 = (bf16[8,2432]{1,0:T(8,128)(2,1)S(1)}, bf16[8,2432]{1,0:T(8,128)(2,1)S(1)}, u32[]{:S(2)}, u32[]{:S(2)}) collective-permute-start(bf16[8,2432]{1,0:T(8,128)(2,1)S(1)} %get-tuple-element.57), channel_id=1, source_target_pairs={{0,2},{2,0},{4,6},{6,4},{8,10},{10,8},{12,14},{14,12},{1,3},{3,1},... | collective-permute-start | bytes 116744 | tf_op jit(solution)/shard_map/ppermute | solution.py:295
  22.3 5.5 %collective-permute-start.9 = (bf16[8,2432]{1,0:T(8,128)(2,1)S(1)}, bf16[8,2432]{1,0:T(8,128)(2,1)S(1)}, u32[]{:S(2)}, u32[]{:S(2)}) collective-permute-start(bf16[8,2432]{1,0:T(8,128)(2,1)S(1)} %get-tuple-element.45), channel_id=1, source_target_pairs={{0,4},{2,6},{4,0},{6,2},{8,12},{10,14},{12,8},{14,10},{1,5},{3,7},... | collective-permute-start | bytes 116744 | tf_op jit(solution)/shard_map/ppermute | solution.py:295
  23.5 4.4 %collective-permute-start.10 = (bf16[8,2432]{1,0:T(8,128)(2,1)S(1)}, bf16[8,2432]{1,0:T(8,128)(2,1)S(1)}, u32[]{:S(2)}, u32[]{:S(2)}) collective-permute-start(bf16[8,2432]{1,0:T(8,128)(2,1)S(1)} %get-tuple-element.46), channel_id=1, source_target_pairs={{0,2},{2,0},{4,6},{6,4},{8,10},{10,8},{12,14},{14,12},{1,3},{3,1},... | collective-permute-start | bytes 116744 | tf_op jit(solution)/shard_map/ppermute | solution.py:295
  24.7 3.2 %collective-permute-start.8 = (bf16[144,1600]{1,0:T(8,128)(2,1)S(1)}, bf16[144,1600]{1,0:T(8,128)(2,1)S(1)}, u32[]{:S(2)}, u32[]{:S(2)}) collective-permute-start(bf16[144,1600]{1,0:T(8,128)(2,1)S(1)} %get-tuple-element.44), channel_id=1, source_target_pairs={{0,1},{1,0},{2,3},{3,2},{4,5},{5,4},{6,7},{7,6},{8,9},{9,8},{10,11... | collective-permute-start | bytes 1382408 | tf_op jit(solution)/shard_map/ppermute | solution.py:367
  25.5 5.0 %collective-permute-start.13 = (bf16[8,2432]{1,0:T(8,128)(2,1)S(1)}, bf16[8,2432]{1,0:T(8,128)(2,1)S(1)}, u32[]{:S(2)}, u32[]{:S(2)}) collective-permute-start(bf16[8,2432]{1,0:T(8,128)(2,1)S(1)} %add_convert_fusion), channel_id=1, source_target_pairs={{0,8},{2,10},{4,12},{6,14},{8,0},{10,2},{12,4},{14,6},{1,9},{3,11}... | collective-permute-start | bytes 116744 | tf_op jit(solution)/shard_map/ppermute | solution.py:295
